TPU v7x, 32 devices: a whole 2x2x4 slice. The times are simulated.
32 devices in a mesh: dp: 16 (over z, y, core), shard: 2 (over x).
Axes of the slice: x: 2, y: 2, z: 4, core: 2. Of those that a mesh axis runs over, the one named last changes fastest.
Arguments:
- tokens: bfloat16 [64, 2, 502, 768], P(('dp', 'shard')), may hold values from -6 to 6
- segment_count: int32 [64], P(('dp', 'shard')), may hold values from 1 to 2, as said below
- memory_init: bfloat16 [768, 10], P(('dp', 'shard')), may hold values from -6 to 6
- query_weight: bfloat16 [768, 768], P(('dp', 'shard')), may hold values from -0.21875 to 0.21875
- key_weight: bfloat16 [768, 768], P(('dp', 'shard')), may hold values from -0.21875 to 0.21875
- value_weight: bfloat16 [768, 768], P(('dp', 'shard')), may hold values from -0.21875 to 0.21875
- output_weight: bfloat16 [768, 768], P(('dp', 'shard')), may hold values from -1.75 to 1.75
- up_weight: bfloat16 [768, 3072], P(('dp', 'shard')), may hold values from -0.21875 to 0.21875
- down_weight: bfloat16 [3072, 768], P(('dp', 'shard')), may hold values from -0.109375 to 0.109375
- query_bias: bfloat16 [768], P(('dp', 'shard')), may hold values from -2 to 2
- value_bias: bfloat16 [768], P(('dp', 'shard')), may hold values from -2 to 2
- output_bias: bfloat16 [768], P(('dp', 'shard')), may hold values from -2 to 2
- up_bias: bfloat16 [3072], P(('dp', 'shard')), may hold values from -2 to 2
- down_bias: bfloat16 [768], P(('dp', 'shard')), may hold values from -2 to 2
- first_gain: bfloat16 [768], P(('dp', 'shard')), may hold values from 0.5 to 1.5
- first_shift: bfloat16 [768], P(('dp', 'shard')), may hold values from -2 to 2
- second_gain: bfloat16 [768], P(('dp', 'shard')), may hold values from 0.5 to 1.5
- second_shift: bfloat16 [768], P(('dp', 'shard')), may hold values from -2 to 2
- output_cotangent: bfloat16 [64, 2, 502, 768], P(('dp', 'shard')), may hold values from -6 to 6
- memory_cotangent: bfloat16 [64, 10, 768], P(('dp', 'shard')), may hold values from -6 to 6
Outputs:
- layer_output: bfloat16 [64, 2, 502, 768], P(('dp', 'shard'))
- memory_final: bfloat16 [64, 10, 768], P(('dp', 'shard'))
- token_gradient: bfloat16 [64, 2, 502, 768], P(('dp', 'shard'))
- memory_init_gradient: float32 [768, 10], P(('dp', 'shard'))
- query_weight_gradient: float32 [768, 768], P(('dp', 'shard'))
- key_weight_gradient: float32 [768, 768], P(('dp', 'shard'))
- value_weight_gradient: float32 [768, 768], P(('dp', 'shard'))
- output_weight_gradient: float32 [768, 768], P(('dp', 'shard'))
- up_weight_gradient: float32 [768, 3072], P(('dp', 'shard'))
- down_weight_gradient: float32 [3072, 768], P(('dp', 'shard'))
- query_bias_gradient: float32 [768], P(('dp', 'shard'))
- value_bias_gradient: float32 [768], P(('dp', 'shard'))
- output_bias_gradient: float32 [768], P(('dp', 'shard'))
- up_bias_gradient: float32 [3072], P(('dp', 'shard'))
- down_bias_gradient: float32 [768], P(('dp', 'shard'))
- first_gain_gradient: float32 [768], P(('dp', 'shard'))
- first_shift_gradient: float32 [768], P(('dp', 'shard'))
- second_gain_gradient: float32 [768], P(('dp', 'shard'))
- second_shift_gradient: float32 [768], P(('dp', 'shard'))
Inputs may be any that keep to these rules, and one draw needn't show every extreme that they name: `segment_count`: segments of each item; item 0 has 2 and item 1 has one.
All inputs are finite; a program needn't handle non-finite values.
Results may differ from a plain program's by a relative error of at most 0.019.
Values may be sent and summed in bfloat16 or wider, within the bound.
No kernel may reach another device: no remote copies, remote signals or barrier semaphores. Data moves between devices by JAX's collectives and lax.ppermute only.
A program may use at most 320 MiB of HBM per device.

v0:
```python
import jax
import jax.numpy as jnp
from jax import lax
from jax.sharding import PartitionSpec as P

HEADS = 12
HEAD_DIM = 64


norm_eps = 1e-06
root_half = 0.7071067811865476


def layer_norm(resid, gain, shift):
    center = resid - jnp.mean(resid, axis=-1, keepdims=True)
    spread = jnp.mean(center * center, axis=-1, keepdims=True)
    return center * lax.rsqrt(spread + norm_eps) * gain + shift


def gelu_exact(values):
    return 0.5 * values * (1.0 + jax.scipy.special.erf(values * root_half))


def dense(left, right):
    return jnp.dot(left, right, preferred_element_type=jnp.float32)


def widen(vector):
    return vector.astype(jnp.float32)


def column_sum(matrix):
    return jnp.sum(matrix, axis=0, dtype=jnp.float32)


def forward_segment(inputs, params):
    (
        query_weight,
        key_weight,
        value_weight,
        output_weight,
        up_weight,
        down_weight,
        query_bias,
        value_bias,
        output_bias,
        up_bias,
        down_bias,
        first_gain,
        first_shift,
        second_gain,
        second_shift,
    ) = params
    length = inputs.shape[0]
    inputs_low = inputs.astype(jnp.bfloat16)
    queries = (dense(inputs_low, query_weight) + widen(query_bias)).astype(jnp.bfloat16)
    key_rows = dense(inputs_low, key_weight).astype(jnp.bfloat16)
    value_rows = (dense(inputs_low, value_weight) + widen(value_bias)).astype(jnp.bfloat16)
    head_query = queries.reshape(length, HEADS, HEAD_DIM)
    head_key = key_rows.reshape(length, HEADS, HEAD_DIM)
    head_value = value_rows.reshape(length, HEADS, HEAD_DIM)
    scores = (
        jnp.einsum("qhd,khd->hqk", head_query, head_key, preferred_element_type=jnp.float32) * 0.125
    )
    highest = jnp.max(scores, axis=-1, keepdims=True)
    exponent = jnp.exp(scores - highest)
    denominator = jnp.sum(exponent, axis=-1, keepdims=True)
    attention = (exponent / denominator).astype(jnp.bfloat16)
    log_total = highest + jnp.log(denominator)
    mixed_rows = jnp.einsum(
        "hqk,khd->qhd", attention, head_value, preferred_element_type=jnp.float32
    )
    mixed_rows = mixed_rows.reshape(length, HEADS * HEAD_DIM).astype(jnp.bfloat16)
    first_in = inputs + dense(mixed_rows, output_weight) + widen(output_bias)
    hidden = layer_norm(first_in, widen(first_gain), widen(first_shift))
    hidden_low = hidden.astype(jnp.bfloat16)
    up_value = dense(hidden_low, up_weight) + widen(up_bias)
    activated = gelu_exact(up_value).astype(jnp.bfloat16)
    second_in = hidden + dense(activated, down_weight) + widen(down_bias)
    result = layer_norm(second_in, widen(second_gain), widen(second_shift))
    stored = (
        inputs_low,
        queries,
        key_rows,
        value_rows,
        log_total,
        mixed_rows,
        first_in,
        hidden_low,
        up_value,
        activated,
        second_in,
    )
    return (result, stored)


def backward_segment(result_grad, stored, params):
    (
        query_weight,
        key_weight,
        value_weight,
        output_weight,
        up_weight,
        down_weight,
        query_bias,
        value_bias,
        output_bias,
        up_bias,
        down_bias,
        first_gain,
        first_shift,
        second_gain,
        second_shift,
    ) = params
    (
        inputs_low,
        queries,
        key_rows,
        value_rows,
        log_total,
        mixed_rows,
        first_in,
        hidden_low,
        up_value,
        activated,
        second_in,
    ) = stored
    length = inputs_low.shape[0]
    unused_second, second_back = jax.vjp(
        layer_norm, second_in, widen(second_gain), widen(second_shift)
    )
    delta_second, grad_second_gain, grad_second_shift = second_back(result_grad)
    delta_feed = delta_second.astype(jnp.bfloat16)
    delta_active = jnp.einsum(
        "rd,fd->rf", delta_feed, down_weight, preferred_element_type=jnp.float32
    )
    unused_gelu, gelu_back = jax.vjp(gelu_exact, up_value)
    delta_up = gelu_back(delta_active)[0].astype(jnp.bfloat16)
    delta_hidden = delta_second + jnp.einsum(
        "rf,df->rd", delta_up, up_weight, preferred_element_type=jnp.float32
    )
    unused_first, first_back = jax.vjp(layer_norm, first_in, widen(first_gain), widen(first_shift))
    delta_first, grad_first_gain, grad_first_shift = first_back(delta_hidden)
    delta_branch = delta_first.astype(jnp.bfloat16)
    delta_mixed = jnp.einsum(
        "rd,ad->ra", delta_branch, output_weight, preferred_element_type=jnp.float32
    ).astype(jnp.bfloat16)
    delta_mixed = delta_mixed.reshape(length, HEADS, HEAD_DIM)
    head_query = queries.reshape(length, HEADS, HEAD_DIM)
    head_key = key_rows.reshape(length, HEADS, HEAD_DIM)
    head_value = value_rows.reshape(length, HEADS, HEAD_DIM)
    scores = (
        jnp.einsum("qhd,khd->hqk", head_query, head_key, preferred_element_type=jnp.float32) * 0.125
    )
    attention = jnp.exp(scores - log_total)
    delta_attention = jnp.einsum(
        "qhd,khd->hqk", delta_mixed, head_value, preferred_element_type=jnp.float32
    )
    delta_values = jnp.einsum(
        "hqk,qhd->khd",
        attention.astype(jnp.bfloat16),
        delta_mixed,
        preferred_element_type=jnp.float32,
    )
    delta_values = delta_values.reshape(length, HEADS * HEAD_DIM).astype(jnp.bfloat16)
    row_total = jnp.sum(delta_attention * attention, axis=-1, keepdims=True)
    delta_scores = (attention * (delta_attention - row_total)).astype(jnp.bfloat16)
    delta_queries = (
        jnp.einsum("hqk,khd->qhd", delta_scores, head_key, preferred_element_type=jnp.float32)
        * 0.125
    )
    delta_queries = delta_queries.reshape(length, HEADS * HEAD_DIM).astype(jnp.bfloat16)
    delta_keys = (
        jnp.einsum("hqk,qhd->khd", delta_scores, head_query, preferred_element_type=jnp.float32)
        * 0.125
    )
    delta_keys = delta_keys.reshape(length, HEADS * HEAD_DIM).astype(jnp.bfloat16)
    delta_inputs = delta_first + jnp.einsum(
        "re,de->rd", delta_queries, query_weight, preferred_element_type=jnp.float32
    )
    delta_inputs = delta_inputs + jnp.einsum(
        "re,de->rd", delta_keys, key_weight, preferred_element_type=jnp.float32
    )
    delta_inputs = delta_inputs + jnp.einsum(
        "re,de->rd", delta_values, value_weight, preferred_element_type=jnp.float32
    )
    norm_grads = (grad_first_gain, grad_first_shift, grad_second_gain, grad_second_shift)
    pieces = (
        inputs_low,
        delta_queries,
        delta_keys,
        delta_values,
        mixed_rows,
        delta_branch,
        hidden_low,
        delta_up,
        activated,
        delta_feed,
    )
    return (delta_inputs, norm_grads, pieces)


def weight_terms(piece_list, norm_grads):
    joined = tuple(
        (jnp.concatenate([member[index] for member in piece_list], axis=0) for index in range(10))
    )
    (
        inputs_low,
        delta_queries,
        delta_keys,
        delta_values,
        mixed_rows,
        delta_branch,
        hidden_low,
        delta_up,
        activated,
        delta_feed,
    ) = joined
    grad_query = jnp.einsum(
        "rd,re->de", inputs_low, delta_queries, preferred_element_type=jnp.float32
    )
    grad_key = jnp.einsum("rd,re->de", inputs_low, delta_keys, preferred_element_type=jnp.float32)
    grad_value = jnp.einsum(
        "rd,re->de", inputs_low, delta_values, preferred_element_type=jnp.float32
    )
    grad_output = jnp.einsum(
        "ra,rd->ad", mixed_rows, delta_branch, preferred_element_type=jnp.float32
    )
    grad_up = jnp.einsum("rd,rf->df", hidden_low, delta_up, preferred_element_type=jnp.float32)
    grad_down = jnp.einsum("rf,rd->fd", activated, delta_feed, preferred_element_type=jnp.float32)
    return (
        grad_query,
        grad_key,
        grad_value,
        grad_output,
        grad_up,
        grad_down,
        column_sum(delta_queries),
        column_sum(delta_values),
        column_sum(delta_branch),
        column_sum(delta_up),
        column_sum(delta_feed),
    ) + tuple(norm_grads)


def local(
    tokens,
    segment_count,
    memory_init,
    query_weight,
    key_weight,
    value_weight,
    output_weight,
    up_weight,
    down_weight,
    query_bias,
    value_bias,
    output_bias,
    up_bias,
    down_bias,
    first_gain,
    first_shift,
    second_gain,
    second_shift,
    output_cotangent,
    memory_cotangent,
):
    shards = (
        memory_init,
        query_weight,
        key_weight,
        value_weight,
        output_weight,
        up_weight,
        down_weight,
        query_bias,
        value_bias,
        output_bias,
        up_bias,
        down_bias,
        first_gain,
        first_shift,
        second_gain,
        second_shift,
    )
    groups = lax.axis_size(("dp", "shard"))
    micro_count = tokens.shape[0]
    segment_total = tokens.shape[1]
    seg_tokens = tokens.shape[2]
    mem_rows = memory_init.shape[1]
    resident = shards
    memory_total = jnp.zeros((memory_init.shape[0] * groups, mem_rows), jnp.float32)
    width = memory_init.shape[0] * groups
    norm_total = tuple((jnp.zeros((width,), jnp.float32) for count in range(4)))
    owned = tuple((jnp.zeros(piece.shape, jnp.float32) for piece in shards))
    all_pieces = []
    outputs = []
    memories = []
    token_grads = []
    for micro_batch in range(micro_count):
        resident = (
            lax.all_gather(shards[0], ("dp", "shard"), axis=0, tiled=True),
            lax.all_gather(shards[1], ("dp", "shard"), axis=0, tiled=True),
            lax.all_gather(shards[2], ("dp", "shard"), axis=0, tiled=True),
            lax.all_gather(shards[3], ("dp", "shard"), axis=0, tiled=True),
            lax.all_gather(shards[4], ("dp", "shard"), axis=0, tiled=True),
            lax.all_gather(shards[5], ("dp", "shard"), axis=0, tiled=True),
            lax.all_gather(shards[6], ("dp", "shard"), axis=0, tiled=True),
            lax.all_gather(shards[7], ("dp", "shard"), axis=0, tiled=True),
            lax.all_gather(shards[8], ("dp", "shard"), axis=0, tiled=True),
            lax.all_gather(shards[9], ("dp", "shard"), axis=0, tiled=True),
            lax.all_gather(shards[10], ("dp", "shard"), axis=0, tiled=True),
            lax.all_gather(shards[11], ("dp", "shard"), axis=0, tiled=True),
            lax.all_gather(shards[12], ("dp", "shard"), axis=0, tiled=True),
            lax.all_gather(shards[13], ("dp", "shard"), axis=0, tiled=True),
            lax.all_gather(shards[14], ("dp", "shard"), axis=0, tiled=True),
            lax.all_gather(shards[15], ("dp", "shard"), axis=0, tiled=True),
        )
        segment_limit = segment_count[micro_batch]
        stored_all = []
        produced = []
        memory = None
        for segment in range(segment_total):
            params = resident
            if segment == 0:
                memory = params[0].astype(jnp.float32).T
            segment_rows = jnp.concatenate(
                [memory, tokens[micro_batch, segment].astype(jnp.float32), memory], axis=0
            )
            result, stored = forward_segment(segment_rows, params[1:])
            active = segment_limit > segment
            produced.append(
                jnp.where(active, result[mem_rows : mem_rows + seg_tokens], 0.0).astype(
                    jnp.bfloat16
                )
            )
            memory = jnp.where(active, result[mem_rows + seg_tokens :], memory)
            stored_all.append(stored)
        outputs.append(jnp.stack(produced))
        memories.append(memory.astype(jnp.bfloat16))
        delta_memory = memory_cotangent[micro_batch].astype(jnp.float32)
        segment_grads = [None] * segment_total
        micro_pieces = []
        for segment in reversed(range(segment_total)):
            params = resident
            active = segment_limit > segment
            zero_rows = jnp.zeros(delta_memory.shape, jnp.float32)
            token_cot = jnp.where(
                active, output_cotangent[micro_batch, segment].astype(jnp.float32), 0.0
            )
            result_grad = jnp.concatenate(
                [zero_rows, token_cot, jnp.where(active, delta_memory, 0.0)], axis=0
            )
            delta_inputs, norm_grads, pieces = backward_segment(
                result_grad, stored_all[segment], params[1:]
            )
            norm_total = tuple((running + fresh for running, fresh in zip(norm_total, norm_grads)))
            micro_pieces.append(pieces)
            segment_grads[segment] = delta_inputs[mem_rows : mem_rows + seg_tokens].astype(
                jnp.bfloat16
            )
            delta_memory = (
                jnp.where(active, 0.0, delta_memory)
                + delta_inputs[:mem_rows]
                + delta_inputs[mem_rows + seg_tokens :]
            )
        memory_total = memory_total + delta_memory.T
        token_grads.append(jnp.stack(segment_grads))
        all_pieces = all_pieces + micro_pieces
    terms = (memory_total,) + weight_terms(all_pieces, norm_total)
    owned = lax.psum_scatter(terms, ("dp", "shard"), scatter_dimension=0, tiled=True)
    return (jnp.stack(outputs), jnp.stack(memories), jnp.stack(token_grads)) + tuple(owned)


def solution(mesh):
    in_specs = (
        P(("dp", "shard"), None, None, None),
        P(("dp", "shard")),
        P(("dp", "shard"), None),
        P(("dp", "shard"), None),
        P(("dp", "shard"), None),
        P(("dp", "shard"), None),
        P(("dp", "shard"), None),
        P(("dp", "shard"), None),
        P(("dp", "shard"), None),
        P(("dp", "shard")),
        P(("dp", "shard")),
        P(("dp", "shard")),
        P(("dp", "shard")),
        P(("dp", "shard")),
        P(("dp", "shard")),
        P(("dp", "shard")),
        P(("dp", "shard")),
        P(("dp", "shard")),
        P(("dp", "shard"), None, None, None),
        P(("dp", "shard"), None, None),
    )
    out_specs = (
        P(("dp", "shard"), None, None, None),
        P(("dp", "shard"), None, None),
        P(("dp", "shard"), None, None, None),
        P(("dp", "shard"), None),
        P(("dp", "shard"), None),
        P(("dp", "shard"), None),
        P(("dp", "shard"), None),
        P(("dp", "shard"), None),
        P(("dp", "shard"), None),
        P(("dp", "shard"), None),
        P(("dp", "shard")),
        P(("dp", "shard")),
        P(("dp", "shard")),
        P(("dp", "shard")),
        P(("dp", "shard")),
        P(("dp", "shard")),
        P(("dp", "shard")),
        P(("dp", "shard")),
        P(("dp", "shard")),
    )
    return jax.shard_map(local, mesh=mesh, in_specs=in_specs, out_specs=out_specs, check_vma=False)
```

profile of v0, /device:TPU:0, one launch (start us, length us, event | category | flops | bytes accessed | tf_op | source)
XLA Modules:
  0.0 1726.3 jit_solution(5055407763454142152)
XLA Ops:
  22.7 42.4 %all-reduce.20 = (bf16[768]{0:T(1024)(128)(2,1)S(1)}, bf16[768]{0:T(1024)(128)(2,1)S(1)}, bf16[768]{0:T(1024)(128)(2,1)S(1)}, bf16[768]{0:T(1024)(128)(2,1)S(1)}...) all-reduce(bf16[768]{0:T(1024)(128)(2,1)S(1)} %dynamic-update-slice, ...), channel_id=1, replica_groups=mesh['dp'=16,'shard'=2] {'dp','shard'}, use_global_device_ids=true, to_apply=%add | all-reduce | flops 9216 | bytes 36864
  65.1 67.2 %all-gather = bf16[32,24,10]{1,2,0:T(8,128)(2,1)S(1)} all-gather(bf16[1,24,10]{1,2,0:T(8,128)(2,1)} %bitcast.383), channel_id=1, replica_groups=mesh['dp'=16,'shard'=2] {'dp','shard'}, dimensions={0}, use_global_device_ids=true | all-gather | bytes 15840 | tf_op jit(solution)/shard_map/all_gather | solution.py:302
  166.8 13.5 all-gather.12.cloned.1.call-done
  184.8 7.5 multiply_reduce_fusion.7
  192.2 8.4 fusion
  200.7 10.1 fusion.47
  219.8 16.4 all-gather.14.cloned.1.call-done
  248.2 8.5 fusion.2
  256.8 9.2 fusion.45
  270.6 30.9 %all-gather.16.cloned.1.call-done = bf16[768,3072]{1,0:T(8,128)(2,1)} async-done(((bf16[24,3072]{1,0:T(8,128)(2,1)}), bf16[768,3072]{1,0:T(8,128)(2,1)}) %all-gather.16.cloned.1.call-update) | async-done | bytes 4718608 | tf_op jit(solution)/shard_map/all_gather | solution.py:307
  309.1 7.2 multiply_convert_fusion.7
  316.3 50.4 %all-gather.18.cloned.1.call-done = bf16[3072,768]{1,0:T(8,128)(2,1)} async-done(((bf16[96,768]{1,0:T(8,128)(2,1)}), bf16[3072,768]{1,0:T(8,128)(2,1)}) %all-gather.18.cloned.1.call-update) | async-done | bytes 4718608 | tf_op jit(solution)/shard_map/all_gather | solution.py:308
  393.1 7.2 multiply_reduce_fusion.6
  400.4 8.5 fusion.1
  409.0 9.2 fusion.46
  435.5 9.5 multiply_reduce_fusion.4
  445.0 8.5 fusion.3
  454.1 9.2 fusion.44
  470.9 8.4 multiply_convert_fusion.6
  497.7 12.0 add_convert_fusion.3
  523.1 16.6 multiply_reduce_fusion.1
  539.8 7.9 multiply_convert_fusion.1
  565.7 16.5 multiply_reduce_fusion.3
  582.2 8.0 multiply_convert_fusion.3
  625.8 11.7 add_convert_fusion.2
  652.0 16.4 multiply_reduce_fusion
  668.5 7.8 multiply_convert_fusion
  694.0 16.5 multiply_reduce_fusion.2
  710.4 7.8 multiply_convert_fusion.2
  730.9 20.8 %concatenate.67 = bf16[2088,768]{1,0:T(8,128)(2,1)} concatenate(bf16[522,768]{1,0:T(8,128)(2,1)} %copy-done.88, bf16[522,768]{1,0:T(8,128)(2,1)} %copy-done.92, bf16[522,768]{1,0:T(8,128)(2,1)} %copy-done.87, bf16[522,768]{1,0:T(8,128)(2,1)} %copy-done.91), dimensions={0} | concatenate | bytes 6414336 | tf_op jit(solution)/shard_map/concatenate | solution.py:205
  751.8 62.5 %concatenate.69 = bf16[2088,3072]{1,0:T(8,128)(2,1)} concatenate(bf16[522,3072]{1,0:T(8,128)(2,1)S(1)} %copy-done.97, bf16[522,3072]{1,0:T(8,128)(2,1)} %copy-done.99, bf16[522,3072]{1,0:T(8,128)(2,1)} %copy-done.98, bf16[522,3072]{1,0:T(8,128)(2,1)} %copy-done.100), dimensions={0} | concatenate | bytes 25657344 | tf_op jit(solution)/shard_map/concatenate | solution.py:205
  814.3 20.8 %concatenate.71 = bf16[2088,768]{1,0:T(8,128)(2,1)} concatenate(bf16[522,768]{1,0:T(8,128)(2,1)} %copy-done.86, bf16[522,768]{1,0:T(8,128)(2,1)} %copy-done.90, bf16[522,768]{1,0:T(8,128)(2,1)} %copy-done.85, bf16[522,768]{1,0:T(8,128)(2,1)} %copy-done.89), dimensions={0} | concatenate | bytes 6414336 | tf_op jit(solution)/shard_map/concatenate | solution.py:205
  835.1 16.0 concatenate.62
  867.7 7.2 convert_reduce_fusion
  892.5 7.3 fusion.146
  899.9 7.3 concatenate.64
  907.2 7.3 fusion.147
  920.9 7.4 concatenate.66
  936.1 18.9 %concatenate.68 = bf16[2088,768]{1,0:T(8,128)(2,1)} concatenate(bf16[522,768]{1,0:T(8,128)(2,1)} %copy-done.78, bf16[522,768]{1,0:T(8,128)(2,1)S(1)} %copy-done.71, bf16[522,768]{1,0:T(8,128)(2,1)} %copy-done.79, bf16[522,768]{1,0:T(8,128)(2,1)S(1)} %copy-done.72), dimensions={0} | concatenate | bytes 6414336 | tf_op jit(solution)/shard_map/concatenate | solution.py:205
  955.0 17.5 %fusion.150 = f32[768,3072]{1,0:T(8,128)} fusion(bf16[2088,768]{1,0:T(8,128)(2,1)} %concatenate.68, bf16[2088,3072]{1,0:T(8,128)(2,1)} %concatenate.69), kind=kOutput, calls=%fused_computation.355 | convolution fusion | flops 9852420096 | bytes 25473024 | tf_op jit(solution)/shard_map/rd,rf->df/dot_general | solution.py:229
  972.5 68.6 %concatenate.70 = bf16[2088,3072]{1,0:T(8,128)(2,1)} concatenate(bf16[522,3072]{1,0:T(8,128)(2,1)} %copy-done.94, bf16[522,3072]{1,0:T(8,128)(2,1)} %get-tuple-element.194, bf16[522,3072]{1,0:T(8,128)(2,1)} %copy-done.95, bf16[522,3072]{1,0:T(8,128)(2,1)} %get-tuple-element.195), dimensions={0} | concatenate | bytes 25657344 | tf_op jit(solution)/shard_map/concatenate | solution.py:205
  1041.2 16.1 fusion.151
  1092.4 31.5 %reduce-scatter.8.cloned.1.call-done = f32[24,768]{1,0:T(8,128)} async-done(((f32[768,768]{1,0:T(8,128)}), f32[24,768]{1,0:T(8,128)}) %reduce-scatter.8.cloned.1.call-update) | async-done | bytes 73744 | tf_op jit(solution)/shard_map/reduce_scatter | solution.py:371
  1123.9 104.0 %reduce-scatter.10.cloned.1.call-done = f32[24,768]{1,0:T(8,128)} async-done(((f32[768,768]{1,0:T(8,128)}), f32[24,768]{1,0:T(8,128)}) %reduce-scatter.10.cloned.1.call-update) | async-done | bytes 73744 | tf_op jit(solution)/shard_map/reduce_scatter | solution.py:371
  1227.9 104.6 %reduce-scatter.12.cloned.1.call-done = f32[24,768]{1,0:T(8,128)} async-done(((f32[768,768]{1,0:T(8,128)}), f32[24,768]{1,0:T(8,128)}) %reduce-scatter.12.cloned.1.call-update) | async-done | bytes 73744 | tf_op jit(solution)/shard_map/reduce_scatter | solution.py:371
  1332.5 103.9 %reduce-scatter.14.cloned.1.call-done = f32[24,768]{1,0:T(8,128)} async-done(((f32[768,768]{1,0:T(8,128)}), f32[24,768]{1,0:T(8,128)}) %reduce-scatter.14.cloned.1.call-update) | async-done | bytes 73744 | tf_op jit(solution)/shard_map/reduce_scatter | solution.py:371
  1436.4 141.9 %reduce-scatter.16.cloned.1.call-done = f32[24,3072]{1,0:T(8,128)} async-done(((f32[768,3072]{1,0:T(8,128)}), f32[24,3072]{1,0:T(8,128)}) %reduce-scatter.16.cloned.1.call-update) | async-done | bytes 294928 | tf_op jit(solution)/shard_map/reduce_scatter | solution.py:371
  1578.3 141.3 %reduce-scatter.18.cloned.1.call-done = f32[96,768]{1,0:T(8,128)} async-done(((f32[3072,768]{1,0:T(8,128)}), f32[96,768]{1,0:T(8,128)}) %reduce-scatter.18.cloned.1.call-update) | async-done | bytes 294928 | tf_op jit(solution)/shard_map/reduce_scatter | solution.py:371
  (694 shorter events, 348.3 us)
Async XLA Ops:
  7.2 152.0 %all-gather.8.cloned.1.call-start = ((), (), s32[]{:S(2)}) async-start(), calls=%async_computation.6 | async-start | bytes 1216512 | tf_op jit(solution)/shard_map/all_gather | solution.py:305
  7.9 154.0 %all-gather.10.cloned.1.call-start = ((), (), s32[]{:S(2)}) async-start(), calls=%async_computation.7 | async-start | bytes 1216512 | tf_op jit(solution)/shard_map/all_gather | solution.py:303
  8.7 171.6 %all-gather.12.cloned.1.call-start = ((), (), s32[]{:S(2)}) async-start(), calls=%async_computation.8 | async-start | bytes 1216512 | tf_op jit(solution)/shard_map/all_gather | solution.py:304
  9.4 226.7 %all-gather.14.cloned.1.call-start = ((), (), s32[]{:S(2)}) async-start(), calls=%async_computation.9 | async-start | bytes 1216512 | tf_op jit(solution)/shard_map/all_gather | solution.py:306
  10.0 291.5 %all-gather.16.cloned.1.call-start = ((), (), s32[]{:S(2)}) async-start(), calls=%async_computation.10 | async-start | bytes 4866048 | tf_op jit(solution)/shard_map/all_gather | solution.py:307
  10.6 356.2 %all-gather.18.cloned.1.call-start = ((), (), s32[]{:S(2)}) async-start(), calls=%async_computation.11 | async-start | bytes 4866048 | tf_op jit(solution)/shard_map/all_gather | solution.py:308
  11.1 1068.5 %all-reduce.23.cloned.1.call-start = ((), (), s32[]{:S(2)}) async-start(), calls=%async_computation.18 | async-start | bytes 188416
  140.2 238.3 %copy-start.147 = (f32[768]{0:T(1024)}, f32[768]{0:T(1024)S(1)}, u32[]{:S(2)}) copy-start(f32[768]{0:T(1024)S(1)} %convert_element_type.469) | copy-start | bytes 9220
  156.6 23.7 %copy-start.73 = (bf16[522,768]{1,0:T(8,128)(2,1)}, bf16[522,768]{1,0:T(8,128)(2,1)S(1)}, u32[]{:S(2)}) copy-start(bf16[522,768]{1,0:T(8,128)(2,1)S(1)} %get-tuple-element.180) | copy-start | bytes 2405380
  161.9 38.7 %copy-start.62 = (bf16[522,768]{0,1:T(8,128)(2,1)}, bf16[522,768]{0,1:T(8,128)(2,1)S(1)}, u32[]{:S(2)}) copy-start(bf16[522,768]{0,1:T(8,128)(2,1)S(1)} %copy.196) | copy-start | bytes 2405380
  166.8 18.0 %copy-start.39 = (bf16[522,768]{0,1:T(8,128)(2,1)}, bf16[522,768]{0,1:T(8,128)(2,1)S(1)}, u32[]{:S(2)}) copy-start(bf16[522,768]{0,1:T(8,128)(2,1)S(1)} %copy.197) | copy-start | bytes 2405380
  239.3 127.5 %copy-start.11 = (f32[522,768]{1,0:T(8,128)}, f32[522,768]{1,0:T(8,128)S(1)}, u32[]{:S(2)}) copy-start(f32[522,768]{1,0:T(8,128)S(1)} %get-tuple-element.219) | copy-start | bytes 4810756
  239.3 127.5 %copy-start.135 = (f32[522]{0:T(1024)}, f32[522]{0:T(1024)S(1)}, u32[]{:S(2)}) copy-start(f32[522]{0:T(1024)S(1)} %broadcast_multiply_fusion.7) | copy-start | bytes 6268
  239.6 27.8 %copy-start.153 = (f32[522]{0:T(1024)}, f32[522]{0:T(1024)S(1)}, u32[]{:S(2)}) copy-start(f32[522]{0:T(1024)S(1)} %multiply_reduce_fusion.31) | copy-start | bytes 6268
  267.1 106.5 %copy-start.137 = (f32[522]{0:T(1024)}, f32[522]{0:T(1024)S(1)}, u32[]{:S(2)}) copy-start(f32[522]{0:T(1024)S(1)} %broadcast_multiply_fusion.3) | copy-start | bytes 6268
  267.5 99.3 %copy-start.149 = (f32[522]{0:T(1024)}, f32[522]{0:T(1024)S(1)}, u32[]{:S(2)}) copy-start(f32[522]{0:T(1024)S(1)} %fusion.96) | copy-start | bytes 6268
  267.5 106.1 %copy-start.151 = (f32[522]{0:T(1024)}, f32[522]{0:T(1024)S(1)}, u32[]{:S(2)}) copy-start(f32[522]{0:T(1024)S(1)} %fusion.100) | copy-start | bytes 6268
  380.0 38.2 %copy-start.118 = (f32[10,768]{1,0:T(8,128)}, f32[10,768]{1,0:T(8,128)S(1)}, u32[]{:S(2)}) copy-start(f32[10,768]{1,0:T(8,128)S(1)} %get-tuple-element.178) | copy-start | bytes 92164
  380.0 83.3 %copy-start.120 = (f32[10,768]{1,0:T(8,128)}, f32[10,768]{1,0:T(8,128)S(1)}, u32[]{:S(2)}) copy-start(f32[10,768]{1,0:T(8,128)S(1)} %get-tuple-element.179) | copy-start | bytes 92164
  523.1 16.7 slice-start.12
  523.1 16.7 slice-start.13
  523.1 16.7 slice-start.14
  523.1 16.7 slice-start.15
  565.7 16.5 slice-start.8
  565.7 16.5 slice-start.9
  565.7 16.5 slice-start.10
  565.7 16.5 slice-start.11
  621.1 16.3 slice-start.18
  652.0 16.5 slice-start.4
  652.0 16.5 slice-start.5
  652.0 16.5 slice-start.6
  652.0 16.5 slice-start.7
  693.9 16.5 slice-start
  693.9 16.5 slice-start.1
  693.9 16.5 slice-start.2
  693.9 16.5 slice-start.3
  730.9 20.8 %copy-start.97 = (bf16[522,3072]{1,0:T(8,128)(2,1)S(1)}, bf16[522,3072]{1,0:T(8,128)(2,1)}, u32[]{:S(2)}) copy-start(bf16[522,3072]{1,0:T(8,128)(2,1)} %copy-done.96) | copy-start | bytes 9621508
  814.3 20.9 %copy-start.74 = (bf16[522,768]{1,0:T(8,128)(2,1)S(1)}, bf16[522,768]{1,0:T(8,128)(2,1)}, u32[]{:S(2)}) copy-start(bf16[522,768]{1,0:T(8,128)(2,1)} %copy-done.73) | copy-start | bytes 2405380
  814.3 20.9 %copy-start.77 = (bf16[522,768]{1,0:T(8,128)(2,1)S(1)}, bf16[522,768]{1,0:T(8,128)(2,1)}, u32[]{:S(2)}) copy-start(bf16[522,768]{1,0:T(8,128)(2,1)} %get-tuple-element.181) | copy-start | bytes 2405380
  814.3 20.9 %copy-start.81 = (bf16[522,768]{1,0:T(8,128)(2,1)S(1)}, bf16[522,768]{1,0:T(8,128)(2,1)}, u32[]{:S(2)}) copy-start(bf16[522,768]{1,0:T(8,128)(2,1)} %copy-done.80) | copy-start | bytes 2405380
  814.3 20.9 %copy-start.84 = (bf16[522,768]{1,0:T(8,128)(2,1)S(1)}, bf16[522,768]{1,0:T(8,128)(2,1)}, u32[]{:S(2)}) copy-start(bf16[522,768]{1,0:T(8,128)(2,1)} %copy-done.82) | copy-start | bytes 2405380
  892.3 231.5 %reduce-scatter.8.cloned.1.call-start = ((), (), s32[]{:S(2)}) async-start(), calls=%async_computation.12 | async-start | bytes 2433024 | tf_op jit(solution)/shard_map/reduce_scatter | solution.py:371
  899.9 328.0 %reduce-scatter.10.cloned.1.call-start = ((), (), s32[]{:S(2)}) async-start(), calls=%async_computation.13 | async-start | bytes 2433024 | tf_op jit(solution)/shard_map/reduce_scatter | solution.py:371
  914.5 417.9 %reduce-scatter.12.cloned.1.call-start = ((), (), s32[]{:S(2)}) async-start(), calls=%async_computation.14 | async-start | bytes 2433024 | tf_op jit(solution)/shard_map/reduce_scatter | solution.py:371
  920.9 515.5 %reduce-scatter.14.cloned.1.call-start = ((), (), s32[]{:S(2)}) async-start(), calls=%async_computation.15 | async-start | bytes 2433024 | tf_op jit(solution)/shard_map/reduce_scatter | solution.py:371
  934.7 643.6 %reduce-scatter.16.cloned.1.call-start = ((), (), s32[]{:S(2)}) async-start(), calls=%async_computation.16 | async-start | bytes 9732096 | tf_op jit(solution)/shard_map/reduce_scatter | solution.py:371
  972.5 68.7 %copy-start.35 = (bf16[2088,768]{1,0:T(8,128)(2,1)S(1)}, bf16[2088,768]{1,0:T(8,128)(2,1)}, u32[]{:S(2)}) copy-start(bf16[2088,768]{1,0:T(8,128)(2,1)} %concatenate.71) | copy-start | bytes 9621508
  972.5 747.0 %reduce-scatter.18.cloned.1.call-start = ((), (), s32[]{:S(2)}) async-start(), calls=%async_computation.17 | async-start | bytes 9732096 | tf_op jit(solution)/shard_map/reduce_scatter | solution.py:371
  (181 other events, 761.8 us)
Sparse Core Ops, SparseCore 0:
  10.9 56.8 all-gather.7
  70.8 53.2 all-gather.9
  127.0 53.2 all-gather.11
  183.0 53.0 all-gather.13
  238.9 62.5 all-gather.15
  304.3 62.4 all-gather.17
  892.4 124.6 all-reduce.22
  1023.8 99.9 reduce-scatter.7
  1129.7 98.0 reduce-scatter.9
  1234.4 97.9 reduce-scatter.11
  1338.3 98.0 reduce-scatter.13
  1443.7 134.4 reduce-scatter.15
  1584.7 134.7 reduce-scatter.17
where the time goes:
time: 1740 us; the launch traced here: 1730 us
  waiting for transfers between devices  742 us (43%)
  matrix products  385 us (22%)
  local copies, waits for them, and re-layouts  337 us (19%)
  other arithmetic  131 us (8%)
  blocking collectives  110 us (6%)
  between operations  19.7 us (1%)
    reduce_scatter x6, waiting for transfers between devices, local(): lax.psum_scatter(terms, ('dp', 'shard'), scatter_dimension=0, tiled=True)  627 us
    concatenate x10, local copies, waits for them, and re-layouts, weight_terms(): jnp.concatenate([member[index] for member in piece_list], axis=0)  234 us
    dot_general x24, matrix products, dense(): return jnp.dot(left, right, preferred_element_type=jnp.float32)  75.1 us
    all_gather x1, blocking collectives, local(): lax.all_gather(shards[0], ('dp', 'shard'), axis=0, tiled=True)  67.2 us
    dot_general x4, matrix products, backward_segment(): jnp.einsum('qhd,khd->hqk', delta_mixed, head_value, preferred_element_typ...  66 us
    unnamed x463, local copies, waits for them, and re-layouts  59.6 us
    all_gather x1, waiting for transfers between devices, local(): lax.all_gather(shards[6], ('dp', 'shard'), axis=0, tiled=True)  50.4 us
    unnamed x1, blocking collectives  42.4 us
  transfers between devices with their start and end apart: 13, of which 10 were waited for; matrix products, arithmetic and copies ran while one was open for 19% of the time, Pallas kernels for 0%

commit v1 on v0

v1 whole, which is shorter than its diff:
```python
import functools

import jax
import jax.numpy as jnp
from jax import lax
from jax.experimental import pallas as pl
from jax.experimental.pallas import tpu as pltpu
from jax.sharding import PartitionSpec as P

F32 = jnp.float32
BF16 = jnp.bfloat16
HEADS = 12
HEAD_DIM = 64
NORM_EPS = 1e-06
ROOT_HALF = 0.7071067811865476
ROOT_TWO_PI = 0.3989422804014327
VMEM_BYTES = 60 << 20


def dot_nn(left, right):
    return jnp.dot(left, right, preferred_element_type=F32)


def dot_nt(left, right):
    return lax.dot_general(left, right, (((1,), (1,)), ((), ())), preferred_element_type=F32)


def dot_tn(left, right):
    return lax.dot_general(left, right, (((0,), (0,)), ((), ())), preferred_element_type=F32)


def lane_masks(rows):
    lane = lax.broadcasted_iota(jnp.int32, (rows, 128), 1)
    first = jnp.where(lane < HEAD_DIM, 1.0, 0.0)
    return first, 1.0 - first


def key_counts(rows, tokens):
    row = lax.broadcasted_iota(jnp.int32, (rows, 128), 0)
    return jnp.where(row < tokens, 1.0, 2.0)


def gelu_parts(u):
    bell = jnp.exp(u * u * -0.5)
    t = pl.reciprocal(1.0 + (0.3275911 * ROOT_HALF) * jnp.abs(u))
    poly = t * (
        0.5 * 0.254829592
        + t * (0.5 * -0.284496736 + t * (0.5 * 1.421413741 + t * (0.5 * -1.453152027 + t * (0.5 * 1.061405429))))
    )
    tail = poly * bell
    cdf = jnp.where(u < 0.0, tail, 1.0 - tail)
    return u * cdf, cdf + u * bell * ROOT_TWO_PI


def attend_forward(tok, mem, wq, wk, wv, bq, bv, x_o, q_o, k_o, v_o, e_o, o_o, li_o):
    seg = tok.shape[2]
    rows = x_o.shape[1]
    x_o[0, rows - 16 :, :] = mem[0].astype(BF16)
    x_o[0, :seg, :] = tok[0, 0]
    x = x_o[0]
    q_o[0] = ((dot_nn(x, wq[...]) + bq[...]).astype(BF16).astype(F32) * 0.125).astype(BF16)
    k_o[0] = dot_nn(x, wk[...]).astype(BF16)
    v_o[0] = (dot_nn(x, wv[...]) + bv[...]).astype(BF16)
    masks = lane_masks(rows)
    count = key_counts(rows, seg)
    low_masks = tuple(m.astype(BF16) for m in masks)

    def pair(p, carry):
        at = pl.ds(pl.multiple_of(p * 128, 128), 128)
        q2 = q_o[0, :, at]
        k2 = k_o[0, :, at]
        v2 = v_o[0, :, at].astype(F32) * count
        total = None
        for h in range(2):
            s = dot_nt(q2 * low_masks[h], k2)
            e = jnp.exp(s - jnp.max(s, axis=-1, keepdims=True)).astype(BF16)
            e_o[0, 2 * p + h] = e
            right = jnp.concatenate(
                [(v2 * masks[h]).astype(BF16), (count * masks[h]).astype(BF16)], axis=1
            )
            part = dot_nn(e, right)
            total = part if total is None else total + part
        inv = 1.0 / total[:, 128:]
        li_o[0, :, at] = inv
        o_o[0, :, at] = (total[:, :128] * inv).astype(BF16)
        return carry

    lax.fori_loop(0, HEADS // 2, pair, 0)


def norm_rows(r):
    mean = jnp.mean(r, axis=-1, keepdims=True)
    center = r - mean
    var = jnp.mean(center * center, axis=-1, keepdims=True)
    scale = lax.rsqrt(var + NORM_EPS)
    return center * scale, scale


def feed_forward(
    segment, step,
    count, tok, mem, o, wo, wup, wdown, bo, g1, s1, bup, bdown, g2, s2,
    y_o, mem_o, xh1_o, sc1_o, h_o, a_o, gp_o, xh2_o, sc2_o, x_s,
):
    seg = tok.shape[2]
    rows = o.shape[1]
    ff = wup.shape[1]
    x_s[rows - 16 :, :] = mem[0]
    x_s[:seg, :] = tok[0, 0].astype(F32)
    xh, sc = norm_rows(x_s[...] + dot_nn(o[0], wo[...]) + bo[...])
    xh1_o[0] = xh.astype(BF16)
    sc1_o[0] = jnp.broadcast_to(sc, (rows, 128))
    h1 = xh * g1[...] + s1[...]
    h_o[0] = h1.astype(BF16)
    x_s[...] = h1 + bdown[...]

    def chunk(j, carry):
        at = pl.ds(pl.multiple_of(j * step, step), step)
        act, slope = gelu_parts(dot_nn(h_o[0], wup[:, at]) + bup[:, at])
        a_o[0, :, at] = act.astype(BF16)
        gp_o[0, :, at] = slope.astype(BF16)
        x_s[...] += dot_nn(a_o[0, :, at], wdown[at, :])
        return carry

    lax.fori_loop(0, ff // step, chunk, 0)
    xh, sc = norm_rows(x_s[...])
    xh2_o[0] = xh.astype(BF16)
    sc2_o[0] = jnp.broadcast_to(sc, (rows, 128))
    x_s[...] = xh * g2[...] + s2[...]
    active = count[pl.program_id(0)] > segment
    y_o[0] = jnp.where(active, x_s[:seg, :], 0.0).astype(BF16)
    mem_o[0] = jnp.where(active, x_s[rows - 16 :, :], mem[0])


def norm_back(dy, xh, sc, gain):
    dxh = dy * gain
    m1 = jnp.mean(dxh, axis=-1, keepdims=True)
    m2 = jnp.mean(dxh * xh, axis=-1, keepdims=True)
    return sc * (dxh - m1 - xh * m2)


def col_sum(x):
    return jnp.sum(x, axis=0, keepdims=True)


def feed_backward(
    segment, step,
    count, cot, dmem, xh2, sc2, gp, xh1, sc1, wup, wdown, g1, g2,
    df_o, du_o, dr_o, db_o, vec_o, vup_o, x_s,
):
    seg = cot.shape[2]
    rows = xh2.shape[1]
    ff = wup.shape[1]
    active = jnp.where(count[pl.program_id(0)] > segment, 1.0, 0.0)
    x_s[rows - 16 :, :] = dmem[0] * active
    x_s[:seg, :] = cot[0, 0].astype(F32) * active
    dy = x_s[...]
    xh = xh2[0].astype(F32)
    vec_o[0, 2:3, :] = col_sum(dy * xh)
    vec_o[0, 3:4, :] = col_sum(dy)
    dr = norm_back(dy, xh, sc2[0, :, :1], g2[...])
    df = dr.astype(BF16)
    df_o[0] = df
    vec_o[0, 4:5, :] = col_sum(df.astype(F32))
    x_s[...] = dr

    def chunk(j, carry):
        at = pl.ds(pl.multiple_of(j * step, step), step)
        du = dot_nt(df_o[0], wdown[at, :]) * gp[0, :, at].astype(F32)
        vup_o[0, :, at] = col_sum(du)
        du_o[0, :, at] = du.astype(BF16)
        x_s[...] += dot_nt(du_o[0, :, at], wup[:, at])
        return carry

    lax.fori_loop(0, ff // step, chunk, 0)
    dh = x_s[...]
    xh = xh1[0].astype(F32)
    vec_o[0, 0:1, :] = col_sum(dh * xh)
    vec_o[0, 1:2, :] = col_sum(dh)
    dr = norm_back(dh, xh, sc1[0, :, :1], g1[...])
    dr_o[0] = dr
    db_o[0] = dr.astype(BF16)
    vec_o[0, 5:6, :] = col_sum(dr)


def attend_backward(
    segment,
    count, dmem, dr, db, q, k, v, e, o, li, wo, wq, wk, wv,
    tg_o, dmem_o, dq_o, dk_o, dv_o, vec_o, do_s, x_s,
):
    seg = tg_o.shape[1]
    rows = q.shape[1]
    do_s[...] = dot_nt(db[0], wo[...]).astype(BF16)
    masks = lane_masks(rows)
    count2 = key_counts(rows, seg)
    low_masks = tuple(m.astype(BF16) for m in masks)
    ones = jnp.ones((rows, 128), BF16)

    def pair(p, carry):
        at = pl.ds(pl.multiple_of(p * 128, 128), 128)
        dop = do_s[:, at].astype(F32) * li[0, :, at]
        pr = (dop * o[0, :, at].astype(F32) * -1.0).astype(BF16)
        dop = dop.astype(BF16)
        q2 = q[0, :, at]
        k2 = (k[0, :, at].astype(F32) * (count2 * 0.125)).astype(BF16)
        right = jnp.concatenate([v[0, :, at], ones], axis=1)
        dq = dk = dv = None
        for h in range(2):
            e_h = e[0, 2 * p + h]
            d_h = dop * low_masks[h]
            left = jnp.concatenate([d_h, pr * low_masks[h]], axis=1)
            ds = (e_h.astype(F32) * dot_nt(left, right)).astype(BF16)
            q_t = dot_nn(ds, k2 * low_masks[h])
            k_t = dot_tn(ds, q2 * low_masks[h])
            v_t = dot_tn(e_h, d_h)
            dq = q_t if dq is None else dq + q_t
            dk = k_t if dk is None else dk + k_t
            dv = v_t if dv is None else dv + v_t
        dq_o[0, :, at] = dq.astype(BF16)
        dk_o[0, :, at] = (dk * count2).astype(BF16)
        dv_o[0, :, at] = (dv * count2).astype(BF16)
        return carry

    lax.fori_loop(0, HEADS // 2, pair, 0)
    vec_o[0, 0:1, :] = col_sum(dq_o[0].astype(F32))
    vec_o[0, 1:2, :] = col_sum(dv_o[0].astype(F32))
    x_s[...] = (
        dr[0]
        + dot_nt(dq_o[0], wq[...])
        + dot_nt(dk_o[0], wk[...])
        + dot_nt(dv_o[0], wv[...])
    )
    tg_o[0] = x_s[:seg, :].astype(BF16)
    kept = jnp.where(count[pl.program_id(0)] > segment, 0.0, 1.0)
    dmem_o[0] = dmem[0] * kept + x_s[rows - 16 :, :]


def weight_product(parts, *refs):
    lefts = refs[:parts]
    rights = refs[parts : 2 * parts]
    out = refs[2 * parts]
    total = None
    for left, right in zip(lefts, rights):
        for i in range(left.shape[0]):
            term = dot_tn(left[i], right[i])
            total = term if total is None else total + term
    out[...] = total.astype(out.dtype)


def whole(array):
    dims = array.shape
    return pl.BlockSpec(dims, lambda *g: (0,) * len(dims), pipeline_mode=pl.Buffered(1))


def per_item(dims):
    return pl.BlockSpec((1,) + dims, lambda i: (i,) + (0,) * len(dims))


def out_of(items, dims, dtype):
    return jax.ShapeDtypeStruct((items,) + dims, dtype)


SCALARS = pl.BlockSpec(memory_space=pltpu.SMEM)


def params(**more):
    return pltpu.CompilerParams(vmem_limit_bytes=VMEM_BYTES, **more)


def call_attend_forward(segment, tokens, mem, wq, wk, wv, bq, bv):
    items, _, seg, width = tokens.shape
    rows = seg + 10
    tok = pl.BlockSpec((1, 1, seg, width), lambda i: (i, segment, 0, 0))
    outs = [((rows, width), BF16)] * 4 + [((HEADS, rows, rows), BF16), ((rows, width), BF16), ((rows, width), F32)]
    return pl.pallas_call(
        attend_forward,
        grid=(items,),
        in_specs=[tok, per_item((16, width)), whole(wq), whole(wk), whole(wv), whole(bq), whole(bv)],
        out_specs=[per_item(d) for d, t in outs],
        out_shape=[out_of(items, d, t) for d, t in outs],
        compiler_params=params(),
        cost_estimate=pl.CostEstimate(flops=items * 2 * rows * (3 * width * width + 8 * rows * width), bytes_accessed=items * rows * (width * 14 + HEADS * rows * 2), transcendentals=0),
        name="attend_forward",
    )(tokens, mem, wq, wk, wv, bq, bv)


def call_feed_forward(segment, count, tokens, mem, o, wo, wup, wdown, bo, g1, s1, bup, bdown, g2, s2):
    items, _, seg, width = tokens.shape
    rows = o.shape[1]
    ff = wup.shape[1]
    tok = pl.BlockSpec((1, 1, seg, width), lambda i: (i, segment, 0, 0))
    outs = [
        ((seg, width), BF16), ((16, width), F32), ((rows, width), BF16), ((rows, 128), F32), ((rows, width), BF16),
        ((rows, ff), BF16), ((rows, ff), BF16), ((rows, width), BF16), ((rows, 128), F32),
    ]
    fixed = (wo, wup, wdown, bo, g1, s1, bup, bdown, g2, s2)
    return pl.pallas_call(
        functools.partial(feed_forward, segment, 768),
        grid=(items,),
        in_specs=[SCALARS, tok, per_item((16, width)), per_item((rows, width))] + [whole(w) for w in fixed],
        out_specs=[per_item(d) for d, t in outs],
        out_shape=[out_of(items, d, t) for d, t in outs],
        scratch_shapes=[pltpu.VMEM((rows, width), F32)],
        compiler_params=params(),
        cost_estimate=pl.CostEstimate(flops=items * 2 * rows * width * (width + 2 * ff), bytes_accessed=items * rows * (width * 14 + ff * 4), transcendentals=0),
        name="feed_forward",
    )(count, tokens, mem, o, *fixed)


def call_feed_backward(segment, count, cot, dmem, xh2, sc2, gp, xh1, sc1, wup, wdown, g1, g2):
    items, _, seg, width = cot.shape
    rows = xh2.shape[1]
    ff = wup.shape[1]
    tok = pl.BlockSpec((1, 1, seg, width), lambda i: (i, segment, 0, 0))
    outs = [((rows, width), BF16), ((rows, ff), BF16), ((rows, width), F32), ((rows, width), BF16), ((8, width), F32), ((1, ff), F32)]
    fixed = (wup, wdown, g1, g2)
    return pl.pallas_call(
        functools.partial(feed_backward, segment, 768),
        grid=(items,),
        in_specs=[SCALARS, tok] + [per_item(a.shape[1:]) for a in (dmem, xh2, sc2, gp, xh1, sc1)] + [whole(w) for w in fixed],
        out_specs=[per_item(d) for d, t in outs],
        out_shape=[out_of(items, d, t) for d, t in outs],
        scratch_shapes=[pltpu.VMEM((rows, width), F32)],
        compiler_params=params(),
        cost_estimate=pl.CostEstimate(flops=items * 4 * rows * width * ff, bytes_accessed=items * rows * (width * 14 + ff * 4), transcendentals=0),
        name="feed_backward",
    )(count, cot, dmem, xh2, sc2, gp, xh1, sc1, *fixed)


def call_attend_backward(segment, seg, count, dmem, dr, db, q, k, v, e, o, li, wo, wq, wk, wv):
    items, rows, width = q.shape
    outs = [((seg, width), BF16), ((16, width), F32)] + [((rows, width), BF16)] * 3 + [((8, width), F32)]
    fixed = (wo, wq, wk, wv)
    return pl.pallas_call(
        functools.partial(attend_backward, segment),
        grid=(items,),
        in_specs=[SCALARS] + [per_item(a.shape[1:]) for a in (dmem, dr, db, q, k, v, e, o, li)] + [whole(w) for w in fixed],
        out_specs=[per_item(d) for d, t in outs],
        out_shape=[out_of(items, d, t) for d, t in outs],
        scratch_shapes=[pltpu.VMEM((rows, width), BF16), pltpu.VMEM((rows, width), F32)],
        compiler_params=params(),
        cost_estimate=pl.CostEstimate(flops=items * 2 * rows * width * (4 * width + 16 * rows), bytes_accessed=items * rows * (width * 24 + HEADS * rows * 2), transcendentals=0),
        name="attend_backward",
    )(count, dmem, dr, db, q, k, v, e, o, li, *fixed)


def call_weight_product(lefts, rights, step_left, step_right, dtype):
    parts = len(lefts)
    items, rows, n_left = lefts[0].shape
    n_right = rights[0].shape[2]
    left_spec = pl.BlockSpec((items, rows, step_left), lambda i, j: (0, 0, i))
    right_spec = pl.BlockSpec((items, rows, step_right), lambda i, j: (0, 0, j))
    return pl.pallas_call(
        functools.partial(weight_product, parts),
        grid=(n_left // step_left, n_right // step_right),
        in_specs=[left_spec] * parts + [right_spec] * parts,
        out_specs=pl.BlockSpec((step_left, step_right), lambda i, j: (i, j)),
        out_shape=jax.ShapeDtypeStruct((n_left, n_right), dtype),
        compiler_params=params(),
        cost_estimate=pl.CostEstimate(flops=2 * parts * items * rows * n_left * n_right, bytes_accessed=2 * parts * items * rows * (n_left + n_right), transcendentals=0),
        name="weight_product",
    )(*lefts, *rights)


def local(*args):
    tokens, segment_count = args[:2]
    shards = args[2:18]
    cotangent, memory_cotangent = args[18:]
    axes = ("dp", "shard")
    items, segments, seg, width = tokens.shape

    def gather(a):
        return lax.all_gather(a, axes, axis=0, tiled=True)

    full = [gather(a) for a in shards]
    mem0 = full[0].astype(F32).T
    wq, wk, wv, wo, wup, wdown = full[1:7]
    bq, bv, bo, bup, bdown, g1, s1, g2, s2 = [a.astype(F32)[None, :] for a in full[7:]]
    mem_rows = mem0.shape[0]
    pad = 16 - mem_rows
    mem = jnp.broadcast_to(jnp.pad(mem0, ((pad, 0), (0, 0)))[None], (items, 16, width))
    saved = []
    outputs = []
    for s in range(segments):
        x, q, k, v, e, o, li = call_attend_forward(s, tokens, mem, wq, wk, wv, bq, bv)
        y, mem, xh1, sc1, h, a, gp, xh2, sc2 = call_feed_forward(
            s, segment_count, tokens, mem, o, wo, wup, wdown, bo, g1, s1, bup, bdown, g2, s2
        )
        outputs.append(y)
        saved.append((x, q, k, v, e, o, li, xh1, sc1, h, a, gp, xh2, sc2))
    memory_final = mem[:, pad:].astype(BF16)
    dmem = jnp.pad(memory_cotangent.astype(F32), ((0, 0), (pad, 0), (0, 0)))
    grads = [None] * segments
    pieces = [None] * segments
    vec = 0.0
    vup = 0.0
    vat = 0.0
    for s in reversed(range(segments)):
        x, q, k, v, e, o, li, xh1, sc1, h, a, gp, xh2, sc2 = saved[s]
        df, du, dr, db, vec_s, vup_s = call_feed_backward(
            s, segment_count, cotangent, dmem, xh2, sc2, gp, xh1, sc1, wup, wdown, g1, g2
        )
        tg, dmem, dq, dk, dv, vat_s = call_attend_backward(
            s, seg, segment_count, dmem, dr, db, q, k, v, e, o, li, wo, wq, wk, wv
        )
        grads[s] = tg
        pieces[s] = (x, dq, dk, dv, o, db, h, du, a, df)
        vec = vec + vec_s.sum(axis=0)
        vup = vup + vup_s.sum(axis=(0, 1))
        vat = vat + vat_s.sum(axis=0)
    x, dq, dk, dv, o, db, h, du, a, df = zip(*pieces)
    gq = call_weight_product(x, dq, 768, 256, F32)
    gk = call_weight_product(x, dk, 768, 256, F32)
    gv = call_weight_product(x, dv, 768, 256, F32)
    go = call_weight_product(o, db, 768, 256, F32)
    gup = call_weight_product(h, du, 768, 256, F32)
    gdown = call_weight_product(a, df, 256, 768, F32)
    gmem = dmem[:, pad:].sum(axis=0).T
    terms = (gmem, gq, gk, gv, go, gup, gdown, vat[0], vat[1], vec[5], vup, vec[4], vec[0], vec[1], vec[2], vec[3])
    owned = lax.psum_scatter(terms, axes, scatter_dimension=0, tiled=True)
    return (jnp.stack(outputs, 1), memory_final, jnp.stack(grads, 1)) + tuple(owned)


def solution(mesh):
    rows = P(("dp", "shard"))
    return jax.shard_map(local, mesh=mesh, in_specs=(rows,) * 20, out_specs=(rows,) * 19, check_vma=False)
```

time: 1740 us -> 1420 us (0.82)
  matrix products: 385 us -> 0 us
  Pallas kernels: 0 us -> 306 us
  local copies, waits for them, and re-layouts: 337 us -> 37.7 us
  waiting for transfers between devices: 742 us -> 947 us
  other arithmetic: 131 us -> 4.84 us
    dot_general x78 -> x0, matrix products: 385 us -> none  [the longest x24 75.1 us: dense(): return jnp.dot(left, right, preferred_element_type=jnp.float32)]
    pallas_call x0 -> x14, Pallas kernels: none -> 306 us  [the longest x2 70.4 us: call_attend_backward(): pl.pallas_call(functools.partial(attend_backward, segment), grid=(items,)...]
    concatenate x10 -> x0, local copies, waits for them, and re-layouts: 234 us -> none  [weight_terms(): jnp.concatenate([member[index] for member in piece_list], axis=0)]
    all_gather x6, waiting for transfers between devices: 111 us -> 204 us  [gather(): return lax.all_gather(a, axes, axis=0, tiled=True)]
    reduce_sum x29 -> x7, other arithmetic: 75 us -> 2.42 us  [the longest x1 1.52 us: local(): gmem = dmem[:, pad:].sum(axis=0).T]
    reduce_scatter x6, waiting for transfers between devices: 627 us -> 689 us  [local(): owned = lax.psum_scatter(terms, axes, scatter_dimension=0, tiled=True)]
    unnamed x14, waiting for transfers between devices: 3.75 us -> 53 us
    convert_element_type x30 -> x0, other arithmetic: 43 us -> none  [the longest x4 31.5 us: backward_segment(): (attention * (delta_attention - row_total)).astype(jnp.bfloat16)]
  transfers between devices with their start and end apart: 13 -> 13, of which waited for: 10 -> 11; matrix products, arithmetic and copies ran while one was open for 19% -> 3% of each run, Pallas kernels for 0% -> 6%
where the time goes in v1:
time: 1420 us
  waiting for transfers between devices  947 us (67%)
  Pallas kernels  306 us (22%)
  blocking collectives  108 us (8%)
  local copies, waits for them, and re-layouts  37.7 us (3%)
  between operations  14.5 us (1%)
    reduce_scatter x6, waiting for transfers between devices, local(): owned = lax.psum_scatter(terms, axes, scatter_dimension=0, tiled=True)  689 us
    all_gather x6, waiting for transfers between devices, gather(): return lax.all_gather(a, axes, axis=0, tiled=True)  204 us
    all_gather x1, blocking collectives, gather(): return lax.all_gather(a, axes, axis=0, tiled=True)  70.7 us
    pallas_call x2, Pallas kernels, call_attend_backward(): pl.pallas_call(functools.partial(attend_backward, segment), grid=(items,)...  70.4 us
    pallas_call x2, Pallas kernels, call_feed_forward(): pl.pallas_call(functools.partial(feed_forward, segment, 768), grid=(items...  66.7 us
    pallas_call x6, Pallas kernels, call_weight_product(): pl.pallas_call(functools.partial(weight_product, parts), grid=(n_left //...  64 us
    pallas_call x2, Pallas kernels, call_attend_forward(): pl.pallas_call(attend_forward, grid=(items,), in_specs=[tok, per_item((16...  54.8 us
    unnamed x14, waiting for transfers between devices  53 us
  transfers between devices with their start and end apart: 13, of which 11 were waited for; matrix products, arithmetic and copies ran while one was open for 3% of the time, Pallas kernels for 6%

profile of v1, /device:TPU:0, one launch (start us, length us, event | category | flops | bytes accessed | tf_op | source)
XLA Modules:
  0.0 1418.3 jit_solution(14090242590352189602)
XLA Ops:
  7.2 0.7 all-gather.8.cloned.1.call-update
  8.0 0.7 all-gather.10.cloned.1.call-update
  8.7 0.7 all-gather.12.cloned.1.call-update
  11.3 4.0 copy.62.tok
  15.4 70.7 %all-gather = bf16[32,24,10]{1,2,0:T(8,128)(2,1)S(1)} all-gather(bf16[1,24,10]{1,2,0:T(8,128)(2,1)S(1)} %bitcast.20), channel_id=1, replica_groups=mesh['dp'=16,'shard'=2] {'dp','shard'}, dimensions={0}, use_global_device_ids=true | all-gather | bytes 15840 | tf_op jit(solution)/shard_map/all_gather | solution.py:372
  88.4 37.6 %all-reduce.22 = (bf16[768]{0:T(1024)(128)(2,1)S(1)}, bf16[768]{0:T(1024)(128)(2,1)S(1)}, bf16[768]{0:T(1024)(128)(2,1)S(1)}, bf16[768]{0:T(1024)(128)(2,1)S(1)}...) all-reduce(bf16[768]{0:T(1024)(128)(2,1)S(1)} %dynamic-update-slice, ...), channel_id=1, replica_groups=mesh['dp'=16,'shard'=2] {'dp','shard'}, use_global_device_ids=true, to_apply=%add.2 | all-reduce | flops 9216 | bytes 36864
  131.3 2.0 copy.66.cot
  134.0 46.0 %all-gather.12.cloned.1.call-done.wv = bf16[768,768]{1,0:T(8,128)(2,1)} async-done(((bf16[24,768]{1,0:T(8,128)(2,1)}), bf16[768,768]{1,0:T(8,128)(2,1)}) %all-gather.12.cloned.1.call-update) | async-done | bytes 1179664 | tf_op jit(solution)/shard_map/all_gather | solution.py:372
  180.6 27.5 %attend_forward.2 = (bf16[2,512,768]{2,1,0:T(8,128)(2,1)}, bf16[2,512,768]{2,1,0:T(8,128)(2,1)}, bf16[2,512,768]{2,1,0:T(8,128)(2,1)}, bf16[2,512,768]{2,1,0:T(8...) custom-call(bf16[2,2,502,768]{3,2,1,0:T(8,128)(2,1)} %copy.62.tok, ...), custom_call_target="tpu_custom_call" | custom-call | flops 10066329600 | bytes 23592960 | tf_op jit(solution)/shard_map/attend_forward/pallas_call | solution.py:274
  208.1 27.7 %all-gather.14.cloned.1.call-done.wo = bf16[768,768]{1,0:T(8,128)(2,1)} async-done(((bf16[24,768]{1,0:T(8,128)(2,1)}), bf16[768,768]{1,0:T(8,128)(2,1)}) %all-gather.14.cloned.1.call-update) | async-done | bytes 1179664 | tf_op jit(solution)/shard_map/all_gather | solution.py:372
  235.8 65.4 %all-gather.16.cloned.1.call-done.wup = bf16[768,3072]{1,0:T(8,128)(2,1)} async-done(((bf16[24,3072]{1,0:T(8,128)(2,1)}), bf16[768,3072]{1,0:T(8,128)(2,1)}) %all-gather.16.cloned.1.call-update) | async-done | bytes 4718608 | tf_op jit(solution)/shard_map/all_gather | solution.py:372
  301.2 65.3 %all-gather.18.cloned.1.call-done.wdown = bf16[3072,768]{1,0:T(8,128)(2,1)} async-done(((bf16[96,768]{1,0:T(8,128)(2,1)}), bf16[3072,768]{1,0:T(8,128)(2,1)}) %all-gather.18.cloned.1.call-update) | async-done | bytes 4718608 | tf_op jit(solution)/shard_map/all_gather | solution.py:372
  366.5 33.2 %feed_forward.2 = (bf16[2,502,768]{2,1,0:T(8,128)(2,1)}, f32[2,16,768]{2,1,0:T(8,128)}, bf16[2,512,768]{2,1,0:T(8,128)(2,1)}, f32[2,512,128]{2,1,0:T(8,128)}, bf...) custom-call(s32[2]{0:T(128)} %count.11, ...), custom_call_target="tpu_custom_call" | custom-call | flops 10871635968 | bytes 23592960 | tf_op jit(solution)/shard_map/feed_forward/pallas_call | solution.py:296
  399.7 27.3 %attend_forward.3 = (bf16[2,512,768]{2,1,0:T(8,128)(2,1)}, bf16[2,512,768]{2,1,0:T(8,128)(2,1)}, bf16[2,512,768]{2,1,0:T(8,128)(2,1)}, bf16[2,512,768]{2,1,0:T(8...) custom-call(bf16[2,2,502,768]{3,2,1,0:T(8,128)(2,1)} %copy.62.tok, ...), custom_call_target="tpu_custom_call" | custom-call | flops 10066329600 | bytes 23592960 | tf_op jit(solution)/shard_map/attend_forward/pallas_call | solution.py:274
  427.0 33.5 %feed_forward.3 = (bf16[2,502,768]{2,1,0:T(8,128)(2,1)}, f32[2,16,768]{2,1,0:T(8,128)}, bf16[2,512,768]{2,1,0:T(8,128)(2,1)}, f32[2,512,128]{2,1,0:T(8,128)}, bf...) custom-call(s32[2]{0:T(128)} %count.11, ...), custom_call_target="tpu_custom_call" | custom-call | flops 10871635968 | bytes 23592960 | tf_op jit(solution)/shard_map/feed_forward/pallas_call | solution.py:296
  460.5 24.8 %feed_backward.2 = (bf16[2,512,768]{2,1,0:T(8,128)(2,1)}, bf16[2,512,3072]{2,1,0:T(8,128)(2,1)}, f32[2,512,768]{2,1,0:T(8,128)}, bf16[2,512,768]{2,1,0:T(8,128)(...) custom-call(s32[2]{0:T(128)} %count.11, bf16[2,2,502,768]{3,2,1,0:T(8,128)(2,1)} %copy.66.cot, ...), custom_call_target="tpu_custom_call" | custom-call | flops 9663676416 | bytes 23592960 | tf_op jit(solution)/shard_map/feed_backward/pallas_call | solution.py:316
  485.3 35.1 %attend_backward.2 = (bf16[2,502,768]{2,1,0:T(8,128)(2,1)}, f32[2,16,768]{2,1,0:T(8,128)}, bf16[2,512,768]{2,1,0:T(8,128)(2,1)}, bf16[2,512,768]{2,1,0:T(8,128)(...) custom-call(s32[2]{0:T(128)} %count.11, f32[2,16,768]{2,1,0:T(8,128)} %pad_convert_fusion.dmem, ...), custom_call_target="tpu_custom_call" | custom-call | flops 17716740096 | bytes 31457280 | tf_op jit(solution)/shard_map/attend_backward/pallas_call | solution.py:333
  520.3 25.2 %feed_backward.3 = (bf16[2,512,768]{2,1,0:T(8,128)(2,1)}, bf16[2,512,3072]{2,1,0:T(8,128)(2,1)}, f32[2,512,768]{2,1,0:T(8,128)}, bf16[2,512,768]{2,1,0:T(8,128)(...) custom-call(s32[2]{0:T(128)} %count.11, bf16[2,2,502,768]{3,2,1,0:T(8,128)(2,1)} %copy.66.cot, ...), custom_call_target="tpu_custom_call" | custom-call | flops 9663676416 | bytes 23592960 | tf_op jit(solution)/shard_map/feed_backward/pallas_call | solution.py:316
  545.6 35.3 %attend_backward.3 = (bf16[2,502,768]{2,1,0:T(8,128)(2,1)}, f32[2,16,768]{2,1,0:T(8,128)}, bf16[2,512,768]{2,1,0:T(8,128)(2,1)}, bf16[2,512,768]{2,1,0:T(8,128)(...) custom-call(s32[2]{0:T(128)} %count.11, f32[2,16,768]{2,1,0:T(8,128)} %get-tuple-element.93.dmem, ...), custom_call_target="tpu_custom_call" | custom-call | flops 17716740096 | bytes 31457280 | tf_op jit(solution)/shard_map/attend_backward/pallas_call | solution.py:333
  580.9 1.5 slice_reduce_fusion
  582.5 0.8 reduce_sum.65
  583.4 0.7 slice_reduce_fusion.1
  584.7 6.8 weight_product.6
  591.6 6.8 weight_product.7
  598.5 6.8 weight_product.8
  605.4 6.8 weight_product.9
  612.3 18.5 %weight_product.10 = f32[768,3072]{1,0:T(8,128)} custom-call(bf16[2,512,768]{2,1,0:T(8,128)(2,1)} %get-tuple-element.117.refs_0_, bf16[2,512,768]{2,1,0:T(8,128)(2,1)} %get-tuple-element.118.refs_1_, bf16[2,512,3072]{2,1,0:T(8,128)(2,1)} %get-tuple-element.119.refs_2_, bf16[2,512,3072]{2,1,0:T(8,128)(2,1)} %get-tuple-element.120.refs_3_), custom_call_target="tpu_custom_call" | custom-call | flops 9663676416 | bytes 15728640 | tf_op jit(solution)/shard_map/weight_product/pallas_call | solution.py:352
  630.9 18.2 %weight_product.11 = f32[3072,768]{1,0:T(8,128)} custom-call(bf16[2,512,3072]{2,1,0:T(8,128)(2,1)} %get-tuple-element.121.refs_0_, bf16[2,512,3072]{2,1,0:T(8,128)(2,1)} %get-tuple-element.122.refs_1_, bf16[2,512,768]{2,1,0:T(8,128)(2,1)} %get-tuple-element.123.refs_2_, bf16[2,512,768]{2,1,0:T(8,128)(2,1)} %get-tuple-element.124.refs_3_), custom_call_target="tpu_custom_call" | custom-call | flops 9663676416 | bytes 15728640 | tf_op jit(solution)/shard_map/weight_product/pallas_call | solution.py:352
  649.1 1.4 copy-done.1
  651.3 4.0 copy.68
  656.2 4.0 copy.70
  660.2 49.2 %all-reduce.25.cloned.1.call-done = (f32[768,10]{0,1:T(8,128)}, f32[768]{0:T(1024)}, f32[768]{0:T(1024)}, f32[768]{0:T(1024)}, f32[3072]{0:T(1024)}, /*index=5*/...) async-done(((f32[768,10]{0,1:T(8,128)}, f32[768]{0:T(1024)}, f32[768]{0:T(1024)}, f32[768]{0:T(1024)}, f32[3072]{0:T(1024)}, ...) | async-done | bytes 67600
  709.5 1.3 dynamic-slice.1
  710.7 1.3 dynamic-slice.2
  712.0 1.3 dynamic-slice.3
  713.2 1.3 dynamic-slice.5
  714.5 1.3 dynamic-slice.6
  715.8 1.3 dynamic-slice.7
  717.0 1.3 dynamic-slice.8
  718.3 1.3 dynamic-slice.9
  719.5 1.3 dynamic-slice.4
  720.8 1.4 constant_dynamic-slice_fusion
  722.2 93.9 %reduce-scatter.8.cloned.1.call-done = f32[24,768]{1,0:T(8,128)} async-done(((f32[768,768]{1,0:T(8,128)}), f32[24,768]{1,0:T(8,128)}) %reduce-scatter.8.cloned.1.call-update) | async-done | bytes 73744 | tf_op jit(solution)/shard_map/reduce_scatter | solution.py:419
  816.1 103.9 %reduce-scatter.10.cloned.1.call-done = f32[24,768]{1,0:T(8,128)} async-done(((f32[768,768]{1,0:T(8,128)}), f32[24,768]{1,0:T(8,128)}) %reduce-scatter.10.cloned.1.call-update) | async-done | bytes 73744 | tf_op jit(solution)/shard_map/reduce_scatter | solution.py:419
  920.0 104.7 %reduce-scatter.12.cloned.1.call-done = f32[24,768]{1,0:T(8,128)} async-done(((f32[768,768]{1,0:T(8,128)}), f32[24,768]{1,0:T(8,128)}) %reduce-scatter.12.cloned.1.call-update) | async-done | bytes 73744 | tf_op jit(solution)/shard_map/reduce_scatter | solution.py:419
  1024.7 103.9 %reduce-scatter.14.cloned.1.call-done = f32[24,768]{1,0:T(8,128)} async-done(((f32[768,768]{1,0:T(8,128)}), f32[24,768]{1,0:T(8,128)}) %reduce-scatter.14.cloned.1.call-update) | async-done | bytes 73744 | tf_op jit(solution)/shard_map/reduce_scatter | solution.py:419
  1128.6 142.1 %reduce-scatter.16.cloned.1.call-done = f32[24,3072]{1,0:T(8,128)} async-done(((f32[768,3072]{1,0:T(8,128)}), f32[24,3072]{1,0:T(8,128)}) %reduce-scatter.16.cloned.1.call-update) | async-done | bytes 294928 | tf_op jit(solution)/shard_map/reduce_scatter | solution.py:419
  1270.7 140.9 %reduce-scatter.18.cloned.1.call-done = f32[96,768]{1,0:T(8,128)} async-done(((f32[3072,768]{1,0:T(8,128)}), f32[96,768]{1,0:T(8,128)}) %reduce-scatter.18.cloned.1.call-update) | async-done | bytes 294928 | tf_op jit(solution)/shard_map/reduce_scatter | solution.py:419
  (113 shorter events, 13.6 us)
Async XLA Ops:
  7.2 126.8 %all-gather.8.cloned.1.call-start = ((), (), s32[]{:S(2)}) async-start(), calls=%async_computation.6 | async-start | bytes 1216512 | tf_op jit(solution)/shard_map/all_gather | solution.py:372
  7.9 126.1 %all-gather.10.cloned.1.call-start = ((), (), s32[]{:S(2)}) async-start(), calls=%async_computation.7 | async-start | bytes 1216512 | tf_op jit(solution)/shard_map/all_gather | solution.py:372
  8.7 171.3 %all-gather.12.cloned.1.call-start = ((), (), s32[]{:S(2)}) async-start(), calls=%async_computation.8 | async-start | bytes 1216512 | tf_op jit(solution)/shard_map/all_gather | solution.py:372
  9.4 226.4 %all-gather.14.cloned.1.call-start = ((), (), s32[]{:S(2)}) async-start(), calls=%async_computation.9 | async-start | bytes 1216512 | tf_op jit(solution)/shard_map/all_gather | solution.py:372
  10.0 291.2 %all-gather.16.cloned.1.call-start = ((), (), s32[]{:S(2)}) async-start(), calls=%async_computation.10 | async-start | bytes 4866048 | tf_op jit(solution)/shard_map/all_gather | solution.py:372
  10.6 355.9 %all-gather.18.cloned.1.call-start = ((), (), s32[]{:S(2)}) async-start(), calls=%async_computation.11 | async-start | bytes 4866048 | tf_op jit(solution)/shard_map/all_gather | solution.py:372
  11.2 698.3 %all-reduce.25.cloned.1.call-start = ((), (), s32[]{:S(2)}) async-start(), calls=%async_computation.18 | async-start | bytes 188416
  11.2 4.1 copy-start.12
  11.2 75.0 %copy-start.13 = (bf16[24]{0:T(256)(128)(2,1)S(1)}, bf16[24]{0:T(256)(128)(2,1)}, u32[]{:S(2)}) copy-start(bf16[24]{0:T(256)(128)(2,1)} %param.29) | copy-start | bytes 148
  11.2 75.2 %copy-start.14 = (bf16[24]{0:T(256)(128)(2,1)S(1)}, bf16[24]{0:T(256)(128)(2,1)}, u32[]{:S(2)}) copy-start(bf16[24]{0:T(256)(128)(2,1)} %param.30) | copy-start | bytes 148
  11.2 75.5 %copy-start.15 = (bf16[24]{0:T(256)(128)(2,1)S(1)}, bf16[24]{0:T(256)(128)(2,1)}, u32[]{:S(2)}) copy-start(bf16[24]{0:T(256)(128)(2,1)} %param.31) | copy-start | bytes 148
  11.2 75.7 %copy-start.16 = (bf16[24]{0:T(256)(128)(2,1)S(1)}, bf16[24]{0:T(256)(128)(2,1)}, u32[]{:S(2)}) copy-start(bf16[24]{0:T(256)(128)(2,1)} %param.34) | copy-start | bytes 148
  11.3 75.9 %copy-start.17 = (bf16[24]{0:T(256)(128)(2,1)S(1)}, bf16[24]{0:T(256)(128)(2,1)}, u32[]{:S(2)}) copy-start(bf16[24]{0:T(256)(128)(2,1)} %param.35) | copy-start | bytes 148
  11.3 76.1 %copy-start.18 = (bf16[24]{0:T(256)(128)(2,1)S(1)}, bf16[24]{0:T(256)(128)(2,1)}, u32[]{:S(2)}) copy-start(bf16[24]{0:T(256)(128)(2,1)} %param.33) | copy-start | bytes 148
  11.3 76.4 %copy-start.19 = (bf16[24]{0:T(256)(128)(2,1)S(1)}, bf16[24]{0:T(256)(128)(2,1)}, u32[]{:S(2)}) copy-start(bf16[24]{0:T(256)(128)(2,1)} %param.36) | copy-start | bytes 148
  11.3 76.6 %copy-start.20 = (bf16[24]{0:T(256)(128)(2,1)S(1)}, bf16[24]{0:T(256)(128)(2,1)}, u32[]{:S(2)}) copy-start(bf16[24]{0:T(256)(128)(2,1)} %param.37) | copy-start | bytes 148
  11.3 76.8 %copy-start.21 = (bf16[96]{0:T(256)(128)(2,1)S(1)}, bf16[96]{0:T(256)(128)(2,1)}, u32[]{:S(2)}) copy-start(bf16[96]{0:T(256)(128)(2,1)} %param.32) | copy-start | bytes 580
  11.3 120.0 %copy-start.8 = (bf16[2,10,768]{2,0,1:T(2,128)(2,1)S(1)}, bf16[2,10,768]{2,0,1:T(2,128)(2,1)}, u32[]{:S(2)}) copy-start(bf16[2,10,768]{2,0,1:T(2,128)(2,1)} %param.39) | copy-start | bytes 92164
  11.3 120.0 %copy-start = (bf16[2,2,502,768]{3,1,2,0:T(2,128)(2,1)S(1)}, bf16[2,2,502,768]{3,1,2,0:T(2,128)(2,1)}, u32[]{:S(2)}) copy-start(bf16[2,2,502,768]{3,1,2,0:T(2,128)(2,1)} %param.38) | copy-start | bytes 9252868
  545.5 36.9 %copy-start.5 = (f32[2,8,768]{2,1,0:T(8,128)S(1)}, f32[2,8,768]{2,1,0:T(8,128)}, u32[]{:S(2)}) copy-start(f32[2,8,768]{2,1,0:T(8,128)} %get-tuple-element.127) | copy-start | bytes 147460
  545.5 36.9 %copy-start.7 = (f32[2,8,768]{2,1,0:T(8,128)S(1)}, f32[2,8,768]{2,1,0:T(8,128)}, u32[]{:S(2)}) copy-start(f32[2,8,768]{2,1,0:T(8,128)} %get-tuple-element.128) | copy-start | bytes 147460
  545.5 36.9 %copy-start.6 = (f32[2,8,768]{2,1,0:T(8,128)S(1)}, f32[2,8,768]{2,1,0:T(8,128)}, u32[]{:S(2)}) copy-start(f32[2,8,768]{2,1,0:T(8,128)} %get-tuple-element.125) | copy-start | bytes 147460
  545.5 37.7 %copy-start.10 = (f32[2,1,3072]{2,1,0:T(1,128)S(1)}, f32[2,1,3072]{2,1,0:T(1,128)}, u32[]{:S(2)}) copy-start(f32[2,1,3072]{2,1,0:T(1,128)} %get-tuple-element.129) | copy-start | bytes 73732
  545.6 37.8 %copy-start.11 = (f32[2,1,3072]{2,1,0:T(1,128)S(1)}, f32[2,1,3072]{2,1,0:T(1,128)}, u32[]{:S(2)}) copy-start(f32[2,1,3072]{2,1,0:T(1,128)} %get-tuple-element.130) | copy-start | bytes 73732
  584.7 231.4 %reduce-scatter.8.cloned.1.call-start = ((), (), s32[]{:S(2)}) async-start(), calls=%async_computation.12 | async-start | bytes 2433024 | tf_op jit(solution)/shard_map/reduce_scatter | solution.py:419
  591.6 328.4 %reduce-scatter.10.cloned.1.call-start = ((), (), s32[]{:S(2)}) async-start(), calls=%async_computation.13 | async-start | bytes 2433024 | tf_op jit(solution)/shard_map/reduce_scatter | solution.py:419
  598.4 426.3 %reduce-scatter.12.cloned.1.call-start = ((), (), s32[]{:S(2)}) async-start(), calls=%async_computation.14 | async-start | bytes 2433024 | tf_op jit(solution)/shard_map/reduce_scatter | solution.py:419
  605.3 523.3 %reduce-scatter.14.cloned.1.call-start = ((), (), s32[]{:S(2)}) async-start(), calls=%async_computation.15 | async-start | bytes 2433024 | tf_op jit(solution)/shard_map/reduce_scatter | solution.py:419
  612.2 658.4 %reduce-scatter.16.cloned.1.call-start = ((), (), s32[]{:S(2)}) async-start(), calls=%async_computation.16 | async-start | bytes 9732096 | tf_op jit(solution)/shard_map/reduce_scatter | solution.py:419
  630.8 780.8 %reduce-scatter.18.cloned.1.call-start = ((), (), s32[]{:S(2)}) async-start(), calls=%async_computation.17 | async-start | bytes 9732096 | tf_op jit(solution)/shard_map/reduce_scatter | solution.py:419
  649.1 1.4 copy-start.1
  649.1 1.9 copy-start.2
  651.2 4.1 copy-start.9
  651.2 4.7 copy-start.3
  651.2 4.7 copy-start.4
Sparse Core Ops, SparseCore 0:
  10.9 56.8 all-gather.7
  70.8 53.1 all-gather.9
  126.9 52.9 all-gather.11
  182.7 53.0 all-gather.13
  238.6 62.5 all-gather.15
  304.0 62.4 all-gather.17
  584.8 124.5 all-reduce.24
  716.2 99.9 reduce-scatter.7
  822.0 97.9 reduce-scatter.9
  926.6 98.1 reduce-scatter.11
  1030.6 98.0 reduce-scatter.13
  1136.0 134.6 reduce-scatter.15
  1277.2 134.3 reduce-scatter.17

commit v2 on v1

--- a/solution.py
+++ b/solution.py
@@ -361,23 +361,374 @@
     )(*lefts, *rights)
 
 
+AXES = ("dp", "shard")
+UNIT = 24
+
+
+def spot(z, y, c, x):
+    return ((z * 2 + y) * 2 + c) * 2 + x
+
+
+def swap(array, dz, dy, dc, dx):
+    pairs = [
+        (spot(z, y, c, x), spot(z ^ dz, y ^ dy, c ^ dc, x ^ dx))
+        for z in range(4)
+        for y in range(2)
+        for c in range(2)
+        for x in range(2)
+    ]
+    return lax.ppermute(array, AXES, pairs)
+
+
+def coordinates():
+    dp = lax.axis_index("dp")
+    return jnp.stack([dp // 4, dp // 2 % 2, dp % 2, lax.axis_index("shard")]).astype(jnp.int32)
+
+
+def join(*parts):
+    return jnp.concatenate(parts, axis=0)
+
+
+def gather_units(unit):
+    own = unit[None]
+    a = join(own, swap(own, 1, 0, 0, 0))
+    b = join(swap(own, 2, 0, 0, 0), swap(own, 3, 0, 0, 0))
+    a = join(a, swap(a, 0, 1, 0, 0))
+    b = join(b, swap(b, 0, 0, 0, 1))
+    mine = (a, swap(a, 0, 0, 0, 1), b, swap(b, 0, 1, 0, 0))
+    return mine + tuple(swap(m, 0, 0, 1, 0) for m in mine)
+
+
+def add_low(left, right):
+    return (left.astype(F32) + right.astype(F32)).astype(BF16)
+
+
+def reduce_units(keep, send):
+    got = swap(send, 0, 0, 1, 0)
+    send_a = add_low(keep[:2, :, 1], got[:2, :, 1])
+    send_b = add_low(keep[2:, 1], got[2:, 1])
+    got_a = swap(send_a, 0, 0, 0, 1)
+    got_b = swap(send_b, 0, 1, 0, 0)
+    a = keep[:2, :, 0].astype(F32) + got[:2, :, 0].astype(F32) + got_a.astype(F32)
+    b = keep[2:, 0].astype(F32) + got[2:, 0].astype(F32) + got_b.astype(F32)
+    got_a = swap(a[:, 1].astype(BF16), 0, 1, 0, 0)
+    got_b = swap(b[:, 1].astype(BF16), 0, 0, 0, 1)
+    a = a[:, 0] + got_a.astype(F32)
+    b = b[:, 0] + got_b.astype(F32)
+    one = swap(a[1].astype(BF16), 1, 0, 0, 0)
+    two = swap(b[0].astype(BF16), 2, 0, 0, 0)
+    three = swap(b[1].astype(BF16), 3, 0, 0, 0)
+    return a[0] + one.astype(F32) + two.astype(F32) + three.astype(F32)
+
+
+def unit_pairs(me, bufs, emit):
+    mz, my, mc, mx = me[0], me[1], me[2], me[3]
+    flip = jnp.broadcast_to(mx, (8, 128)) == 1
+
+    def send(dz, dy, dc, near, far):
+        dp = ((mz ^ dz) * 2 + (my ^ dy)) * 2 + (mc ^ dc)
+        emit(dp, near, far)
+
+    for dc in range(2):
+        a, a_far, b, b_far = bufs[4 * dc : 4 * dc + 4]
+        for i in range(2):
+            for j in range(2):
+                send(j, i, dc, (a, 2 * i + j), (a_far, 2 * i + j))
+        for i, buf in enumerate((b, b_far)):
+            for j in range(2):
+                send(2 + j, i, dc, (buf, j), (buf, 2 + j))
+
+
+def assemble_first(me, *refs):
+    bufs, (wq, wk, wv, small) = refs[:8], refs[8:]
+    mx = me[3]
+
+    def emit(dp, near, far):
+        n = near[0][near[1]].astype(F32)
+        f = far[0][far[1]].astype(F32)
+        low = jnp.where(mx == 0, n, f)
+        high = jnp.where(mx == 0, f, n)
+        at = pl.ds(pl.multiple_of(dp * 48, 16), 48)
+        for w, ref in enumerate((wq, wk, wv)):
+            ref[at, :] = jnp.concatenate(
+                [low[UNIT * w : UNIT * (w + 1)], high[UNIT * w : UNIT * (w + 1)]], axis=0
+            ).astype(BF16)
+        small[dp * 2] = low[3 * UNIT : 3 * UNIT + 1]
+        small[dp * 2 + 1] = high[3 * UNIT : 3 * UNIT + 1]
+
+    unit_pairs(me, bufs, emit)
+
+
+def assemble_second(me, *refs):
+    bufs, (wo, wup) = refs[:8], refs[8:]
+    mx = me[3]
+    width = wo.shape[1]
+
+    def emit(dp, near, far):
+        at = pl.ds(pl.multiple_of(dp * 48, 16), 48)
+        for w in range(5):
+            n = near[0][near[1], w].astype(F32)
+            f = far[0][far[1], w].astype(F32)
+            low = jnp.where(mx == 0, n, f)
+            high = jnp.where(mx == 0, f, n)
+            rows = jnp.concatenate([low, high], axis=0).astype(BF16)
+            if w == 0:
+                wo[at, :] = rows
+            else:
+                wup[at, (w - 1) * width : w * width] = rows
+
+    unit_pairs(me, bufs, emit)
+
+
+def assemble_third(me, *refs):
+    bufs, (wdown,) = refs[:8], refs[8:]
+    mx = me[3]
+    tall = 4 * UNIT
+
+    def emit(dp, near, far):
+        for (buf, i), x in ((near, mx), (far, 1 - mx)):
+            at = pl.ds(pl.multiple_of((dp * 2 + x) * tall, 16), tall)
+            wdown[at, :] = buf[i]
+
+    unit_pairs(me, bufs, emit)
+
+
+def call_assemble(body, me, bufs, outs, name):
+    vm = pl.BlockSpec(memory_space=pltpu.VMEM)
+    return pl.pallas_call(
+        body,
+        in_specs=[SCALARS] + [vm] * 8,
+        out_specs=[vm] * len(outs),
+        out_shape=[jax.ShapeDtypeStruct(d, t) for d, t in outs],
+        compiler_params=params(),
+        name=name,
+    )(me, *bufs)
+
+
+def emit_units(me, keep, send, value_of):
+    mz, my, mc, mx = me[0], me[1], me[2], me[3]
+    for core in range(2):
+
+        @pl.when(mc == core)
+        def _():
+            for z in range(4):
+                for y in range(2):
+                    for x in range(2):
+                        to = (z ^ mz, y ^ my, x ^ mx)
+                        keep[to] = value_of(z, y, core, x)
+                        send[to] = value_of(z, y, 1 - core, x)
+
+
+def product_sum(lefts, rights):
+    total = None
+    for left, right in zip(lefts, rights):
+        for i in range(left.shape[0]):
+            term = dot_tn(left[i], right[i])
+            total = term if total is None else total + term
+    return total
+
+
+def product_up(segments, me, *refs):
+    o, db, h, du = (refs[segments * i : segments * (i + 1)] for i in range(4))
+    keep, send, acc = refs[4 * segments :]
+
+    @pl.when(pl.program_id(0) == 0)
+    def _():
+        acc[...] = product_sum(o, db)
+
+    @pl.when(pl.program_id(0) > 0)
+    def _():
+        acc[...] = product_sum(h, du)
+
+    def value_of(*at):
+        idx = spot(*at)
+        return acc[UNIT * idx : UNIT * (idx + 1), :].astype(BF16)
+
+    emit_units(me, keep.at[:, :, :, 0], send.at[:, :, :, 0], value_of)
+
+
+def product_down(segments, me, *refs):
+    a, df = refs[:segments], refs[segments : 2 * segments]
+    keep, send, acc = refs[2 * segments :]
+    tall = 4 * UNIT
+    acc[...] = product_sum(a, df)
+    my, mc, mx = me[1], me[2], me[3]
+    for core in range(2):
+
+        @pl.when(mc == core)
+        def _():
+            for y in range(2):
+                for x in range(2):
+                    for ref, c in ((keep, core), (send, 1 - core)):
+                        row = ((y * 2 + c) * 2 + x) * tall
+                        ref[0, y ^ my, x ^ mx] = acc[row : row + tall, :].astype(BF16)
+
+
+def product_first(segments, me, small, *refs):
+    x, dq, dk, dv = (refs[segments * i : segments * (i + 1)] for i in range(4))
+    keep, send, acc = refs[4 * segments :]
+    step = pl.program_id(0)
+
+    for w, right in enumerate((dq, dk, dv)):
+        term = product_sum(x, right)
+
+        @pl.when(step == 0)
+        def _():
+            acc[w] = term
+
+        @pl.when(step > 0)
+        def _():
+            acc[w] += term
+
+    @pl.when(step == pl.num_programs(0) - 1)
+    def _():
+        def value_of(*at):
+            idx = spot(*at)
+            rows = [acc[w, UNIT * idx : UNIT * (idx + 1), :] for w in range(3)]
+            return jnp.concatenate(rows + [small[idx]], axis=0).astype(BF16)
+
+        emit_units(me, keep, send, value_of)
+
+
+def call_product_up(me, o, db, h, du):
+    segments = len(o)
+    items, rows, width = o[0].shape
+    ff = du[0].shape[2]
+    steps = ff // width
+    fixed = [pl.BlockSpec((items, rows, width), lambda j, m: (0, 0, 0), pipeline_mode=pl.Buffered(1))] * (3 * segments)
+    moving = [pl.BlockSpec((items, rows, width), lambda j, m: (0, 0, jnp.maximum(j - 1, 0)))] * segments
+    dims = (4, 2, 2, steps + 1, UNIT, width)
+    out = pl.BlockSpec((4, 2, 2, 1, UNIT, width), lambda j, m: (0, 0, 0, j, 0, 0))
+    return pl.pallas_call(
+        functools.partial(product_up, segments),
+        grid_spec=pltpu.PrefetchScalarGridSpec(
+            num_scalar_prefetch=1,
+            grid=(steps + 1,),
+            in_specs=fixed + moving,
+            out_specs=[out, out],
+            scratch_shapes=[pltpu.VMEM((width, width), F32)],
+        ),
+        out_shape=[jax.ShapeDtypeStruct(dims, BF16)] * 2,
+        compiler_params=params(),
+        cost_estimate=pl.CostEstimate(flops=2 * segments * items * rows * width * (ff + width), bytes_accessed=2 * segments * items * rows * (ff + 3 * width) + 2 * width * (ff + width), transcendentals=0),
+        name="product_up",
+    )(me, *o, *db, *h, *du)
+
+
+def call_product_down(me, a, df):
+    segments = len(a)
+    items, rows, width = df[0].shape
+    ff = a[0].shape[2]
+    moving = [pl.BlockSpec((items, rows, ff // 4), lambda j, m: (0, 0, j ^ m[0]))] * segments
+    fixed = [pl.BlockSpec((items, rows, width), lambda j, m: (0, 0, 0), pipeline_mode=pl.Buffered(1))] * segments
+    dims = (4, 2, 2, 4 * UNIT, width)
+    out = pl.BlockSpec((1, 2, 2, 4 * UNIT, width), lambda j, m: (j, 0, 0, 0, 0))
+    return pl.pallas_call(
+        functools.partial(product_down, segments),
+        grid_spec=pltpu.PrefetchScalarGridSpec(
+            num_scalar_prefetch=1,
+            grid=(4,),
+            in_specs=moving + fixed,
+            out_specs=[out, out],
+            scratch_shapes=[pltpu.VMEM((ff // 4, width), F32)],
+        ),
+        out_shape=[jax.ShapeDtypeStruct(dims, BF16)] * 2,
+        compiler_params=params(),
+        cost_estimate=pl.CostEstimate(flops=2 * segments * items * rows * width * ff, bytes_accessed=2 * segments * items * rows * (ff + width) + 2 * width * ff, transcendentals=0),
+        name="product_down",
+    )(me, *a, *df)
+
+
+def call_product_first(me, small, x, dq, dk, dv):
+    segments = len(x)
+    items, rows, width = x[0].shape
+    moving = [pl.BlockSpec((1, rows, width), lambda j, m: (j, 0, 0))] * (4 * segments)
+    tall = 3 * UNIT + 8
+    dims = (4, 2, 2, tall, width)
+    out = pl.BlockSpec(dims, lambda j, m: (0,) * 5, pipeline_mode=pl.Buffered(1))
+    return pl.pallas_call(
+        functools.partial(product_first, segments),
+        grid_spec=pltpu.PrefetchScalarGridSpec(
+            num_scalar_prefetch=1,
+            grid=(items,),
+            in_specs=[pl.BlockSpec(small.shape, lambda j, m: (0, 0, 0), pipeline_mode=pl.Buffered(1))] + moving,
+            out_specs=[out, out],
+            scratch_shapes=[pltpu.VMEM((3, width, width), F32)],
+        ),
+        out_shape=[jax.ShapeDtypeStruct(dims, BF16)] * 2,
+        compiler_params=params(),
+        cost_estimate=pl.CostEstimate(flops=6 * segments * items * rows * width * width, bytes_accessed=8 * segments * items * rows * width + 6 * width * width, transcendentals=0),
+        name="product_first",
+    )(me, small, *x, *dq, *dk, *dv)
+
+
+def unpack_small(small):
+    devices = small.shape[0]
+    per = small[:, : 18 * UNIT].reshape(devices, 18, UNIT)
+    vectors = per.transpose(1, 0, 2).reshape(18, devices * UNIT)
+    hidden = small[:, 18 * UNIT : 22 * UNIT].reshape(1, devices * 4 * UNIT)
+    return vectors, hidden
+
+
+def gather_weights(me, shards):
+    mem, wq, wk, wv, wo, wup, wdown, bq, bv, bo, bup, bdown, g1, s1, g2, s2 = shards
+    width = wq.shape[1]
+    ff = wup.shape[1]
+    vectors = jnp.concatenate([bq, bv, bo, bdown, g1, s1, mem.T.reshape(-1), g2, s2, bup])
+    vectors = jnp.pad(vectors[None, :], ((0, 7), (0, width - vectors.shape[0])))
+    first = gather_units(jnp.concatenate([wq, wk, wv, vectors], axis=0))
+    up_blocks = wup.reshape(UNIT, ff // width, width).transpose(1, 0, 2)
+    second = gather_units(jnp.concatenate([wo[None], up_blocks], axis=0))
+    third = gather_units(wdown)
+    square = ((width, width), BF16)
+    wq, wk, wv, small = call_assemble(
+        assemble_first, me, first, [square] * 3 + [((width // UNIT, 1, width), F32)], "assemble_first"
+    )
+    wo, wup = call_assemble(assemble_second, me, second, [square, ((width, ff), BF16)], "assemble_second")
+    (wdown,) = call_assemble(assemble_third, me, third, [((ff, width), BF16)], "assemble_third")
+    vectors, hidden = unpack_small(small[:, 0])
+    return wq, wk, wv, wo, wup, wdown, vectors, hidden
+
+
+def gather_plain(shards):
+    mem, wq, wk, wv, wo, wup, wdown, bq, bv, bo, bup, bdown, g1, s1, g2, s2 = [
+        lax.all_gather(a, AXES, axis=0, tiled=True) for a in shards
+    ]
+    rows = [bq, bv, bo, bdown, g1, s1, mem.T, g2, s2]
+    vectors = jnp.concatenate([r.reshape(-1, wq.shape[1]) for r in rows], axis=0).astype(F32)
+    return wq, wk, wv, wo, wup, wdown, vectors, bup.astype(F32)[None, :]
+
+
+def reduce_plain(pieces, vectors, hidden):
+    x, dq, dk, dv, o, db, h, du, a, df = pieces
+    gq = call_weight_product(x, dq, 768, 256, F32)
+    gk = call_weight_product(x, dk, 768, 256, F32)
+    gv = call_weight_product(x, dv, 768, 256, F32)
+    go = call_weight_product(o, db, 768, 256, F32)
+    gup = call_weight_product(h, du, 768, 256, F32)
+    gdown = call_weight_product(a, df, 256, 768, F32)
+    terms = (vectors[6:16].T, gq, gk, gv, go, gup, gdown, hidden) + tuple(
+        vectors[i] for i in (0, 1, 2, 3, 4, 5, 16, 17)
+    )
+    owned = lax.psum_scatter(terms, AXES, scatter_dimension=0, tiled=True)
+    mem, gq, gk, gv, go, gup, gdown, bup, bq, bv, bo, bdown, g1, s1, g2, s2 = owned
+    return mem, gq, gk, gv, go, gup, gdown, bq, bv, bo, bup, bdown, g1, s1, g2, s2
+
+
 def local(*args):
     tokens, segment_count = args[:2]
     shards = args[2:18]
     cotangent, memory_cotangent = args[18:]
-    axes = ("dp", "shard")
     items, segments, seg, width = tokens.shape
-
-    def gather(a):
-        return lax.all_gather(a, axes, axis=0, tiled=True)
-
-    full = [gather(a) for a in shards]
-    mem0 = full[0].astype(F32).T
-    wq, wk, wv, wo, wup, wdown = full[1:7]
-    bq, bv, bo, bup, bdown, g1, s1, g2, s2 = [a.astype(F32)[None, :] for a in full[7:]]
-    mem_rows = mem0.shape[0]
+    mem_rows = shards[0].shape[1]
     pad = 16 - mem_rows
-    mem = jnp.broadcast_to(jnp.pad(mem0, ((pad, 0), (0, 0)))[None], (items, 16, width))
+    planned = lax.axis_size("dp") == 16 and lax.axis_size("shard") == 2
+    me = coordinates()
+    weights = gather_weights(me, shards) if planned else gather_plain(shards)
+    wq, wk, wv, wo, wup, wdown, vectors, bup = weights
+    bq, bv, bo, bdown, g1, s1 = [vectors[i : i + 1] for i in range(6)]
+    g2, s2 = vectors[16:17], vectors[17:18]
+    mem = jnp.broadcast_to(vectors[None, :16], (items, 16, width))
     saved = []
     outputs = []
     for s in range(segments):
@@ -399,24 +750,41 @@
         df, du, dr, db, vec_s, vup_s = call_feed_backward(
             s, segment_count, cotangent, dmem, xh2, sc2, gp, xh1, sc1, wup, wdown, g1, g2
         )
+        pieces[s] = (x, o, db, h, du, a, df)
+        vec = vec + vec_s.sum(axis=0)
+        vup = vup + vup_s.sum(axis=0)
+        if s == 0 and planned:
+            o_all, db_all, h_all, du_all, a_all, df_all = list(zip(*pieces))[1:]
+            down = reduce_units(*call_product_down(me, a_all, df_all))
+            up = reduce_units(*call_product_up(me, o_all, db_all, h_all, du_all))
         tg, dmem, dq, dk, dv, vat_s = call_attend_backward(
             s, seg, segment_count, dmem, dr, db, q, k, v, e, o, li, wo, wq, wk, wv
         )
         grads[s] = tg
-        pieces[s] = (x, dq, dk, dv, o, db, h, du, a, df)
-        vec = vec + vec_s.sum(axis=0)
-        vup = vup + vup_s.sum(axis=(0, 1))
+        pieces[s] += (dq, dk, dv)
         vat = vat + vat_s.sum(axis=0)
-    x, dq, dk, dv, o, db, h, du, a, df = zip(*pieces)
-    gq = call_weight_product(x, dq, 768, 256, F32)
-    gk = call_weight_product(x, dk, 768, 256, F32)
-    gv = call_weight_product(x, dv, 768, 256, F32)
-    go = call_weight_product(o, db, 768, 256, F32)
-    gup = call_weight_product(h, du, 768, 256, F32)
-    gdown = call_weight_product(a, df, 256, 768, F32)
-    gmem = dmem[:, pad:].sum(axis=0).T
-    terms = (gmem, gq, gk, gv, go, gup, gdown, vat[0], vat[1], vec[5], vup, vec[4], vec[0], vec[1], vec[2], vec[3])
-    owned = lax.psum_scatter(terms, axes, scatter_dimension=0, tiled=True)
+    x, o, db, h, du, a, df, dq, dk, dv = zip(*pieces)
+    vectors = jnp.concatenate(
+        [vat[:2], vec[5:6], vec[4:5], vec[0:2], dmem[:, pad:].sum(axis=0), vec[2:4]], axis=0
+    )
+    if planned:
+        devices = lax.axis_size(AXES)
+        per = vectors.reshape(18, devices, UNIT).transpose(1, 0, 2).reshape(devices, 18 * UNIT)
+        small = jnp.concatenate([per, vup.reshape(devices, 4 * UNIT)], axis=1)
+        small = jnp.pad(small[:, None, :], ((0, 0), (0, 7), (0, width - small.shape[1])))
+        first = reduce_units(*call_product_first(me, small, x, dq, dk, dv))
+        gq, gk, gv = [first[UNIT * w : UNIT * (w + 1)] for w in range(3)]
+        line = first[3 * UNIT]
+        per = line[: 18 * UNIT].reshape(18, UNIT)
+        bq, bv, bo, bdown, g1, s1 = [per[i] for i in range(6)]
+        go = up[0]
+        gup = up[1:].transpose(1, 0, 2).reshape(UNIT, -1)
+        owned = (
+            per[6:16].T, gq, gk, gv, go, gup, down, bq, bv, bo,
+            line[18 * UNIT : 22 * UNIT], bdown, g1, s1, per[16], per[17],
+        )
+    else:
+        owned = reduce_plain((x, dq, dk, dv, o, db, h, du, a, df), vectors, vup[0])
     return (jnp.stack(outputs, 1), memory_final, jnp.stack(grads, 1)) + tuple(owned)
 
 

time: 1420 us -> 549 us (0.39)
  waiting for transfers between devices: 947 us -> 98.1 us
  blocking collectives: 108 us -> 0 us
  starting transfers between devices: 0.52 us -> 65.7 us
  other arithmetic: 4.84 us -> 19.1 us
    reduce_scatter x6 -> x0, waiting for transfers between devices: 689 us -> none  [local(): owned = lax.psum_scatter(terms, axes, scatter_dimension=0, tiled=True)]
    all_gather x6 -> x0, waiting for transfers between devices: 204 us -> none  [gather(): return lax.all_gather(a, axes, axis=0, tiled=True)]
    ppermute x0 -> x57, waiting for transfers between devices: none -> 98.1 us  [swap(): return lax.ppermute(array, AXES, pairs)]
    all_gather x1 -> x0, blocking collectives: 70.7 us -> none  [gather(): return lax.all_gather(a, axes, axis=0, tiled=True)]
    ppermute x0 -> x57, starting transfers between devices: none -> 65.7 us  [swap(): return lax.ppermute(array, AXES, pairs)]
    unnamed x14 -> x0, waiting for transfers between devices: 53 us -> none
    unnamed x1 -> x0, blocking collectives: 37.6 us -> none
    unnamed x79 -> x76, local copies, waits for them, and re-layouts: 31.7 us -> 19.7 us
  transfers between devices with their start and end apart: 13 -> 57, of which waited for: 11 -> 21; matrix products, arithmetic and copies ran while one was open for 3% -> 8% of each run, Pallas kernels for 6% -> 14%
where the time goes in v2:
time: 549 us; the launch traced here: 543 us
  Pallas kernels  313 us (57%)
  waiting for transfers between devices  98.1 us (18%)
  starting transfers between devices  65.7 us (12%)
  local copies, waits for them, and re-layouts  45 us (8%)
  other arithmetic  19.1 us (3%)
    ppermute x57, waiting for transfers between devices, swap(): return lax.ppermute(array, AXES, pairs)  98.1 us
    pallas_call x2, Pallas kernels, call_attend_backward(): pl.pallas_call(functools.partial(attend_backward, segment), grid=(items,)...  70.6 us
    pallas_call x2, Pallas kernels, call_feed_forward(): pl.pallas_call(functools.partial(feed_forward, segment, 768), grid=(items...  66.8 us
    ppermute x57, starting transfers between devices, swap(): return lax.ppermute(array, AXES, pairs)  65.7 us
    pallas_call x2, Pallas kernels, call_attend_forward(): pl.pallas_call(attend_forward, grid=(items,), in_specs=[tok, per_item((16...  55 us
    pallas_call x2, Pallas kernels, call_feed_backward(): pl.pallas_call(functools.partial(feed_backward, segment, 768), grid=(item...  49.8 us
    pallas_call x1, Pallas kernels, call_product_up(): pl.pallas_call(functools.partial(product_up, segments), grid_spec=pltpu.P...  20.8 us
    unnamed x76, local copies, waits for them, and re-layouts  19.7 us
  transfers between devices with their start and end apart: 57, of which 21 were waited for; matrix products, arithmetic and copies ran while one was open for 8% of the time, Pallas kernels for 14%

profile of v2, /device:TPU:0, one launch (start us, length us, event | category | flops | bytes accessed | tf_op | source)
XLA Modules:
  0.0 543.1 jit_solution(10302080472315640944)
XLA Ops:
  1.5 6.1 %concatenate.57 = bf16[528]{0:T(1024)(128)(2,1)S(1)} concatenate(bf16[24]{0:T(256)(128)(2,1)} %param.29, bf16[24]{0:T(256)(128)(2,1)} %param.30, bf16[24]{0:T(256)(128)(2,1)} %param.31, bf16[24]{0:T(256)(128)(2,1)} %param.33, bf16[24]{0:T(256)(128)(2,1)} %param.34, bf16[24]{0:T(256)(128)(2,1)} %param.35, bf16[240]{0:T(256)(128)(2,1)S(1)} %reshape.160, bf16[24]{0:T(256)(128)(2,1)} %param.36, ...), dimensions={0} | concatenate | bytes 2112 | tf_op jit(solution)/shard_map/concatenate | solution.py:677
  8.4 3.1 collective-permute-start
  11.5 2.5 collective-permute-start.4
  14.1 2.9 collective-permute-start.26
  20.9 2.4 collective-permute-start.15
  23.3 14.8 %collective-permute-done.3 = bf16[1,80,768]{2,1,0:T(8,128)(2,1)S(1)} collective-permute-done((bf16[1,80,768]{2,1,0:T(8,128)(2,1)S(1)}, bf16[1,80,768]{2,1,0:T(8,128)(2,1)S(1)}, u32[]{:S(2)}, u32[]{:S(2)}) %collective-permute-start.3) | collective-permute-done | bytes 122912 | tf_op jit(solution)/shard_map/ppermute | solution.py:380
  38.2 3.6 collective-permute-start.11
  43.4 3.0 collective-permute-done.25
  49.5 4.0 collective-permute-done.14
  57.4 1.6 collective-permute-start.6
  59.0 4.4 collective-permute-done.23
  66.5 4.8 collective-permute-done.12
  73.6 8.2 %collective-permute-done.6.refs_3_ = bf16[4,80,768]{2,1,0:T(8,128)(2,1)S(1)} collective-permute-done((bf16[4,80,768]{2,1,0:T(8,128)(2,1)S(1)}, bf16[4,80,768]{2,1,0:T(8,128)(2,1)S(1)}, u32[]{:S(2)}, u32[]{:S(2)}) %collective-permute-start.6) | collective-permute-done | bytes 491552 | tf_op jit(solution)/shard_map/ppermute | solution.py:380
  88.8 5.8 %collective-permute-done.28.refs_3_ = bf16[4,96,768]{2,1,0:T(8,128)(2,1)} collective-permute-done((bf16[4,96,768]{2,1,0:T(8,128)(2,1)S(1)}, bf16[4,96,768]{2,1,0:T(8,128)(2,1)}, u32[]{:S(2)}, u32[]{:S(2)}) %collective-permute-start.28) | collective-permute-done | bytes 589856 | tf_op jit(solution)/shard_map/ppermute | solution.py:380
  97.0 2.1 copy.83.tok
  100.0 2.0 copy.87.cot
  103.3 4.5 assemble_first.1
  119.2 27.7 %attend_forward.2 = (bf16[2,512,768]{2,1,0:T(8,128)(2,1)}, bf16[2,512,768]{2,1,0:T(8,128)(2,1)}, bf16[2,512,768]{2,1,0:T(8,128)(2,1)}, bf16[2,512,768]{2,1,0:T(8...) custom-call(bf16[2,2,502,768]{3,2,1,0:T(8,128)(2,1)} %copy.83.tok, ...), custom_call_target="tpu_custom_call" | custom-call | flops 10066329600 | bytes 23592960 | tf_op jit(solution)/shard_map/attend_forward/pallas_call | solution.py:274
  147.8 4.8 assemble_third.1.wdown
  154.8 6.1 %assemble_second.1 = (bf16[768,768]{1,0:T(8,128)(2,1)}, bf16[768,3072]{1,0:T(8,128)(2,1)}) custom-call(s32[4]{0:T(128)} %pad_add_fusion.me, bf16[4,5,24,768]{3,2,1,0:T(8,128)(2,1)} %pad_maximum_fusion.2.refs_0_, bf16[4,5,24,768]{3,2,1,0:T(8,128)(2,1)} %collective-permute-done.13.refs_1_, bf16[4,5,24,768]{3,2,1,0:T(8,128)(2,1)} %constant_dynamic-update-slice_fusion.3.refs_2_, ...), custom_call_target="tpu_custom_call" | custom-call | tf_op jit(solution)/shard_map/assemble_second/pallas_call | solution.py:498
  160.9 33.2 %feed_forward.2 = (bf16[2,502,768]{2,1,0:T(8,128)(2,1)}, f32[2,16,768]{2,1,0:T(8,128)}, bf16[2,512,768]{2,1,0:T(8,128)(2,1)}, f32[2,512,128]{2,1,0:T(8,128)}, bf...) custom-call(s32[2]{0:T(128)} %count.11, ...), custom_call_target="tpu_custom_call" | custom-call | flops 10871635968 | bytes 23592960 | tf_op jit(solution)/shard_map/feed_forward/pallas_call | solution.py:296
  194.2 27.3 %attend_forward.3 = (bf16[2,512,768]{2,1,0:T(8,128)(2,1)}, bf16[2,512,768]{2,1,0:T(8,128)(2,1)}, bf16[2,512,768]{2,1,0:T(8,128)(2,1)}, bf16[2,512,768]{2,1,0:T(8...) custom-call(bf16[2,2,502,768]{3,2,1,0:T(8,128)(2,1)} %copy.83.tok, ...), custom_call_target="tpu_custom_call" | custom-call | flops 10066329600 | bytes 23592960 | tf_op jit(solution)/shard_map/attend_forward/pallas_call | solution.py:274
  221.5 33.6 %feed_forward.3 = (bf16[2,502,768]{2,1,0:T(8,128)(2,1)}, f32[2,16,768]{2,1,0:T(8,128)}, bf16[2,512,768]{2,1,0:T(8,128)(2,1)}, f32[2,512,128]{2,1,0:T(8,128)}, bf...) custom-call(s32[2]{0:T(128)} %count.11, ...), custom_call_target="tpu_custom_call" | custom-call | flops 10871635968 | bytes 23592960 | tf_op jit(solution)/shard_map/feed_forward/pallas_call | solution.py:296
  255.1 24.8 %feed_backward.2 = (bf16[2,512,768]{2,1,0:T(8,128)(2,1)}, bf16[2,512,3072]{2,1,0:T(8,128)(2,1)}, f32[2,512,768]{2,1,0:T(8,128)}, bf16[2,512,768]{2,1,0:T(8,128)(...) custom-call(s32[2]{0:T(128)} %count.11, bf16[2,2,502,768]{3,2,1,0:T(8,128)(2,1)} %copy.87.cot, ...), custom_call_target="tpu_custom_call" | custom-call | flops 9663676416 | bytes 23592960 | tf_op jit(solution)/shard_map/feed_backward/pallas_call | solution.py:316
  279.9 35.1 %attend_backward.2 = (bf16[2,502,768]{2,1,0:T(8,128)(2,1)}, f32[2,16,768]{2,1,0:T(8,128)}, bf16[2,512,768]{2,1,0:T(8,128)(2,1)}, bf16[2,512,768]{2,1,0:T(8,128)(...) custom-call(s32[2]{0:T(128)} %count.11, f32[2,16,768]{2,1,0:T(8,128)} %pad_convert_fusion.dmem, ...), custom_call_target="tpu_custom_call" | custom-call | flops 17716740096 | bytes 31457280 | tf_op jit(solution)/shard_map/attend_backward/pallas_call | solution.py:333
  315.0 25.0 %feed_backward.3 = (bf16[2,512,768]{2,1,0:T(8,128)(2,1)}, bf16[2,512,3072]{2,1,0:T(8,128)(2,1)}, f32[2,512,768]{2,1,0:T(8,128)}, bf16[2,512,768]{2,1,0:T(8,128)(...) custom-call(s32[2]{0:T(128)} %count.11, bf16[2,2,502,768]{3,2,1,0:T(8,128)(2,1)} %copy.87.cot, ...), custom_call_target="tpu_custom_call" | custom-call | flops 9663676416 | bytes 23592960 | tf_op jit(solution)/shard_map/feed_backward/pallas_call | solution.py:316
  340.9 35.5 %attend_backward.3 = (bf16[2,502,768]{2,1,0:T(8,128)(2,1)}, f32[2,16,768]{2,1,0:T(8,128)}, bf16[2,512,768]{2,1,0:T(8,128)(2,1)}, bf16[2,512,768]{2,1,0:T(8,128)(...) custom-call(s32[2]{0:T(128)} %count.11, f32[2,16,768]{2,1,0:T(8,128)} %get-tuple-element.111.dmem, ...), custom_call_target="tpu_custom_call" | custom-call | flops 17716740096 | bytes 31457280 | tf_op jit(solution)/shard_map/attend_backward/pallas_call | solution.py:333
  380.0 18.4 %product_first.1 = (bf16[4,2,2,80,768]{4,3,2,1,0:T(8,128)(2,1)}, bf16[4,2,2,80,768]{4,3,2,1,0:T(8,128)(2,1)}) custom-call(s32[4]{0:T(128)} %pad_add_fusion.me, f32[32,8,768]{2,1,0:T(8,128)} %pad.17.small, bf16[2,512,768]{2,1,0:T(8,128)(2,1)} %get-tuple-element.133.refs_0_, bf16[2,512,768]{2,1,0:T(8,128)(2,1)} %get-tuple-element.134.refs_1_, ...), custom_call_target="tpu_custom_call" | custom-call | flops 7247757312 | bytes 16121856 | tf_op jit(solution)/shard_map/product_first/pallas_call | solution.py:649
  398.5 16.3 %product_down.1 = (bf16[4,2,2,96,768]{4,3,2,1,0:T(8,128)(2,1)}, bf16[4,2,2,96,768]{4,3,2,1,0:T(8,128)(2,1)}) custom-call(s32[4]{0:T(128)} %pad_add_fusion.me, bf16[2,512,3072]{2,1,0:T(8,128)(2,1)} %get-tuple-element.149.refs_0_, bf16[2,512,3072]{2,1,0:T(8,128)(2,1)} %get-tuple-element.150.refs_1_, bf16[2,512,768]{2,1,0:T(8,128)(2,1)} %get-tuple-element.151.refs_2_, ...), custom_call_target="tpu_custom_call" | custom-call | flops 9663676416 | bytes 20447232 | tf_op jit(solution)/shard_map/product_down/pallas_call | solution.py:626
  415.6 4.0 copy.113
  420.6 4.0 copy.115
  424.6 20.8 %product_up.1 = (bf16[4,2,2,5,24,768]{5,4,3,2,1,0:T(8,128)(2,1)}, bf16[4,2,2,5,24,768]{5,4,3,2,1,0:T(8,128)(2,1)}) custom-call(s32[4]{0:T(128)} %pad_add_fusion.me, bf16[2,512,768]{2,1,0:T(8,128)(2,1)} %get-tuple-element.91.o.refs_0_, bf16[2,512,768]{2,1,0:T(8,128)(2,1)} %get-tuple-element.96.o.refs_1_, bf16[2,512,768]{2,1,0:T(8,128)(2,1)} %get-tuple-element.118.db.refs_2_, ...), custom_call_target="tpu_custom_call" | custom-call | flops 12079595520 | bytes 27918336 | tf_op jit(solution)/shard_map/product_up/pallas_call | solution.py:602
  450.6 2.0 fusion.6
  455.4 5.7 %collective-permute-done.37 = bf16[2,2,80,768]{3,2,1,0:T(8,128)(2,1)S(1)} collective-permute-done((bf16[2,2,80,768]{3,2,1,0:T(8,128)(2,1)S(1)}, bf16[2,2,80,768]{3,2,1,0:T(8,128)(2,1)S(1)}, u32[]{:S(2)}, u32[]{:S(2)}) %collective-permute-start.37) | collective-permute-done | bytes 491552 | tf_op jit(solution)/shard_map/ppermute | solution.py:380
  462.3 1.6 collective-permute-start.38
  464.7 4.7 collective-permute-done.38
  469.8 2.3 collective-permute-start.40
  472.0 6.5 %collective-permute-done.35 = bf16[2,80,768]{2,1,0:T(8,128)(2,1)S(1)} collective-permute-done((bf16[2,80,768]{2,1,0:T(8,128)(2,1)S(1)}, bf16[2,80,768]{2,1,0:T(8,128)(2,1)S(1)}, u32[]{:S(2)}, u32[]{:S(2)}) %collective-permute-start.35) | collective-permute-done | bytes 245792 | tf_op jit(solution)/shard_map/ppermute | solution.py:380
  481.1 2.4 collective-permute-done.36
  486.3 1.6 bitcast_add_fusion.2
  489.4 6.8 %collective-permute-done.50 = bf16[2,2,96,768]{3,2,0,1:T(8,128)(2,1)} collective-permute-done((bf16[2,2,96,768]{3,2,0,1:T(8,128)(2,1)}, bf16[2,2,96,768]{3,2,0,1:T(8,128)(2,1)}, u32[]{:S(2)}, u32[]{:S(2)}) %collective-permute-start.50) | collective-permute-done | bytes 589856 | tf_op jit(solution)/shard_map/ppermute | solution.py:380
  502.3 3.1 collective-permute-start.55
  507.8 2.1 collective-permute-start.52
  509.9 10.0 %collective-permute-done.45 = bf16[2,2,5,24,768]{4,3,2,1,0:T(8,128)(2,1)S(1)} collective-permute-done((bf16[2,2,5,24,768]{4,3,2,1,0:T(8,128)(2,1)S(1)}, bf16[2,2,5,24,768]{4,3,2,1,0:T(8,128)(2,1)S(1)}, u32[]{:S(2)}, u32[]{:S(2)}) %collective-permute-start.45) | collective-permute-done | bytes 737312 | tf_op jit(solution)/shard_map/ppermute | solution.py:380
  522.3 5.4 collective-permute-done.46
  527.8 2.8 collective-permute-start.47
  530.6 1.6 collective-permute-start.48
  534.3 6.0 %collective-permute-done.47 = bf16[5,24,768]{2,1,0:T(8,128)(2,1)S(1)} collective-permute-done((bf16[5,24,768]{2,1,0:T(8,128)(2,1)S(1)}, bf16[5,24,768]{2,1,0:T(8,128)(2,1)S(1)}, u32[]{:S(2)}, u32[]{:S(2)}) %collective-permute-start.47) | collective-permute-done | bytes 184352 | tf_op jit(solution)/shard_map/ppermute | solution.py:380
  (266 shorter events, 84.0 us)
Async XLA Ops:
  8.4 10.7 %collective-permute-start = (bf16[1,80,768]{2,1,0:T(8,128)(2,1)S(1)}, bf16[1,80,768]{2,1,0:T(8,128)(2,1)S(1)}, u32[]{:S(2)}, u32[]{:S(2)}) collective-permute-start(bf16[1,80,768]{2,1,0:T(8,128)(2,1)S(1)} %fusion.34), channel_id=1, source_target_pairs={{0,8},{1,9},{2,10},{3,11},{4,12},{5,13},{6,14},{7,15},{8,0},{9,1},... | collective-permute-start | bytes 368648 | tf_op jit(solution)/shard_map/ppermute | solution.py:380
  14.0 24.1 %collective-permute-start.3 = (bf16[1,80,768]{2,1,0:T(8,128)(2,1)S(1)}, bf16[1,80,768]{2,1,0:T(8,128)(2,1)S(1)}, u32[]{:S(2)}, u32[]{:S(2)}) collective-permute-start(bf16[1,80,768]{2,1,0:T(8,128)(2,1)S(1)} %fusion.34), channel_id=1, source_target_pairs={{0,16},{1,17},{2,18},{3,19},{4,20},{5,21},{6,22},{7,23},{8,24},{9,... | collective-permute-start | bytes 368648 | tf_op jit(solution)/shard_map/ppermute | solution.py:380
  14.1 27.7 %collective-permute-start.26 = (bf16[1,96,768]{2,1,0:T(8,128)(2,1)}, bf16[1,96,768]{2,1,0:T(8,128)(2,1)S(1)}, u32[]{:S(2)}, u32[]{:S(2)}) collective-permute-start(bf16[1,96,768]{2,1,0:T(8,128)(2,1)} %bitcast.189), channel_id=1, source_target_pairs={{0,24},{1,25},{2,26},{3,27},{4,28},{5,29},{6,30},{7,31},{8,16},{9,... | collective-permute-start | bytes 442376 | tf_op jit(solution)/shard_map/ppermute | solution.py:380
  17.0 29.4 %collective-permute-start.25 = (bf16[1,96,768]{2,1,0:T(8,128)(2,1)}, bf16[1,96,768]{2,1,0:T(8,128)(2,1)S(1)}, u32[]{:S(2)}, u32[]{:S(2)}) collective-permute-start(bf16[1,96,768]{2,1,0:T(8,128)(2,1)} %bitcast.190), channel_id=1, source_target_pairs={{0,16},{1,17},{2,18},{3,19},{4,20},{5,21},{6,22},{7,23},{8,24},{9,... | collective-permute-start | bytes 442376 | tf_op jit(solution)/shard_map/ppermute | solution.py:380
  19.1 19.1 %collective-permute-start.22 = (bf16[1,96,768]{2,1,0:T(8,128)(2,1)}, bf16[1,96,768]{2,1,0:T(8,128)(2,1)S(1)}, u32[]{:S(2)}, u32[]{:S(2)}) collective-permute-start(bf16[1,96,768]{2,1,0:T(8,128)(2,1)} %bitcast.191), channel_id=1, source_target_pairs={{0,8},{1,9},{2,10},{3,11},{4,12},{5,13},{6,14},{7,15},{8,0},{9,1},... | collective-permute-start | bytes 442376 | tf_op jit(solution)/shard_map/ppermute | solution.py:380
  20.9 27.0 %collective-permute-start.15 = (bf16[1,5,24,768]{3,2,1,0:T(8,128)(2,1)S(1)}, bf16[1,5,24,768]{3,2,1,0:T(8,128)(2,1)S(1)}, u32[]{:S(2)}, u32[]{:S(2)}) collective-permute-start(bf16[1,5,24,768]{3,2,1,0:T(8,128)(2,1)S(1)} %maximum_bitcast_fusion), channel_id=1, source_target_pairs={{0,24},{1,25},{2,26},{3,27},{4,28},{5,29},{6,30},{7,31},{8,16},{9,... | collective-permute-start | bytes 552968 | tf_op jit(solution)/shard_map/ppermute | solution.py:380
  38.1 15.4 %collective-permute-start.14 = (bf16[1,5,24,768]{3,2,1,0:T(8,128)(2,1)S(1)}, bf16[1,5,24,768]{3,2,1,0:T(8,128)(2,1)S(1)}, u32[]{:S(2)}, u32[]{:S(2)}) collective-permute-start(bf16[1,5,24,768]{3,2,1,0:T(8,128)(2,1)S(1)} %maximum_bitcast_fusion), channel_id=1, source_target_pairs={{0,16},{1,17},{2,18},{3,19},{4,20},{5,21},{6,22},{7,23},{8,24},{9,... | collective-permute-start | bytes 552968 | tf_op jit(solution)/shard_map/ppermute | solution.py:380
  38.2 16.9 %collective-permute-start.11 = (bf16[1,5,24,768]{3,2,1,0:T(8,128)(2,1)S(1)}, bf16[1,5,24,768]{3,2,1,0:T(8,128)(2,1)S(1)}, u32[]{:S(2)}, u32[]{:S(2)}) collective-permute-start(bf16[1,5,24,768]{3,2,1,0:T(8,128)(2,1)S(1)} %maximum_bitcast_fusion), channel_id=1, source_target_pairs={{0,8},{1,9},{2,10},{3,11},{4,12},{5,13},{6,14},{7,15},{8,0},{9,1},... | collective-permute-start | bytes 552968 | tf_op jit(solution)/shard_map/ppermute | solution.py:380
  41.8 14.8 %collective-permute-start.5 = (bf16[2,80,768]{2,1,0:T(8,128)(2,1)S(1)}, bf16[2,80,768]{2,1,0:T(8,128)(2,1)S(1)}, u32[]{:S(2)}, u32[]{:S(2)}) collective-permute-start(bf16[2,80,768]{2,1,0:T(8,128)(2,1)S(1)} %pad_maximum_fusion.10), channel_id=1, source_target_pairs={{0,1},{1,0},{2,3},{3,2},{4,5},{5,4},{6,7},{7,6},{8,9},{9,8},{10,11... | collective-permute-start | bytes 737288 | tf_op jit(solution)/shard_map/ppermute | solution.py:380
  46.4 10.9 %collective-permute-start.1 = (bf16[2,80,768]{2,1,0:T(8,128)(2,1)S(1)}, bf16[2,80,768]{2,1,0:T(8,128)(2,1)S(1)}, u32[]{:S(2)}, u32[]{:S(2)}) collective-permute-start(bf16[2,80,768]{2,1,0:T(8,128)(2,1)S(1)} %pad_maximum_fusion.9), channel_id=1, source_target_pairs={{0,4},{1,5},{2,6},{3,7},{4,0},{5,1},{6,2},{7,3},{8,12},{9,13},{10,... | collective-permute-start | bytes 737288 | tf_op jit(solution)/shard_map/ppermute | solution.py:380
  55.0 11.5 %collective-permute-start.16 = (bf16[2,5,24,768]{3,2,1,0:T(8,128)(2,1)S(1)}, bf16[2,5,24,768]{3,2,1,0:T(8,128)(2,1)S(1)}, u32[]{:S(2)}, u32[]{:S(2)}) collective-permute-start(bf16[2,5,24,768]{3,2,1,0:T(8,128)(2,1)S(1)} %pad_maximum_fusion.6), channel_id=1, source_target_pairs={{0,1},{1,0},{2,3},{3,2},{4,5},{5,4},{6,7},{7,6},{8,9},{9,8},{10,11... | collective-permute-start | bytes 1105928 | tf_op jit(solution)/shard_map/ppermute | solution.py:380
  56.6 14.7 %collective-permute-start.12 = (bf16[2,5,24,768]{3,2,1,0:T(8,128)(2,1)S(1)}, bf16[2,5,24,768]{3,2,1,0:T(8,128)(2,1)S(1)}, u32[]{:S(2)}, u32[]{:S(2)}) collective-permute-start(bf16[2,5,24,768]{3,2,1,0:T(8,128)(2,1)S(1)} %pad_maximum_fusion.5), channel_id=1, source_target_pairs={{0,4},{1,5},{2,6},{3,7},{4,0},{5,1},{6,2},{7,3},{8,12},{9,13},{10,... | collective-permute-start | bytes 1105928 | tf_op jit(solution)/shard_map/ppermute | solution.py:380
  57.2 14.1 %collective-permute-start.9 = (bf16[4,80,768]{2,1,0:T(8,128)(2,1)S(1)}, bf16[4,80,768]{2,1,0:T(8,128)(2,1)S(1)}, u32[]{:S(2)}, u32[]{:S(2)}) collective-permute-start(bf16[4,80,768]{2,1,0:T(8,128)(2,1)S(1)} %constant_dynamic-update-slice_fusion.refs_2_), channel_id=1, source_target_pairs={{0,2},{1,3},{2,0},{3,1},{4,6},{5,7},{6,4},{7,5},{8,10},{9,11},{10,... | collective-permute-start | bytes 1474568 | tf_op jit(solution)/shard_map/ppermute | solution.py:380
  57.4 24.4 %collective-permute-start.6 = (bf16[4,80,768]{2,1,0:T(8,128)(2,1)S(1)}, bf16[4,80,768]{2,1,0:T(8,128)(2,1)S(1)}, u32[]{:S(2)}, u32[]{:S(2)}) collective-permute-start(bf16[4,80,768]{2,1,0:T(8,128)(2,1)S(1)} %constant_dynamic-update-slice_fusion.refs_2_), channel_id=1, source_target_pairs={{0,4},{1,5},{2,6},{3,7},{4,0},{5,1},{6,2},{7,3},{8,12},{9,13},{10,... | collective-permute-start | bytes 1474568 | tf_op jit(solution)/shard_map/ppermute | solution.py:380
  63.4 18.4 %collective-permute-start.2 = (bf16[4,80,768]{2,1,0:T(8,128)(2,1)S(1)}, bf16[4,80,768]{2,1,0:T(8,128)(2,1)S(1)}, u32[]{:S(2)}, u32[]{:S(2)}) collective-permute-start(bf16[4,80,768]{2,1,0:T(8,128)(2,1)S(1)} %pad_maximum_fusion.4.refs_0_), channel_id=1, source_target_pairs={{0,1},{1,0},{2,3},{3,2},{4,5},{5,4},{6,7},{7,6},{8,9},{9,8},{10,11... | collective-permute-start | bytes 1474568 | tf_op jit(solution)/shard_map/ppermute | solution.py:380
  66.5 19.9 %collective-permute-start.31 = (bf16[4,96,768]{2,1,0:T(8,128)(2,1)S(1)}, bf16[4,96,768]{2,1,0:T(8,128)(2,1)S(1)}, u32[]{:S(2)}, u32[]{:S(2)}) collective-permute-start(bf16[4,96,768]{2,1,0:T(8,128)(2,1)S(1)} %constant_dynamic-update-slice_fusion.6.refs_2_), channel_id=1, source_target_pairs={{0,2},{1,3},{2,0},{3,1},{4,6},{5,7},{6,4},{7,5},{8,10},{9,11},{10,... | collective-permute-start | bytes 1769480 | tf_op jit(solution)/shard_map/ppermute | solution.py:380
  71.3 13.5 %collective-permute-start.7 = (bf16[4,80,768]{2,1,0:T(8,128)(2,1)S(1)}, bf16[4,80,768]{2,1,0:T(8,128)(2,1)S(1)}, u32[]{:S(2)}, u32[]{:S(2)}) collective-permute-start(bf16[4,80,768]{2,1,0:T(8,128)(2,1)S(1)} %pad_maximum_fusion.4.refs_0_), channel_id=1, source_target_pairs={{0,2},{1,3},{2,0},{3,1},{4,6},{5,7},{6,4},{7,5},{8,10},{9,11},{10,... | collective-permute-start | bytes 1474568 | tf_op jit(solution)/shard_map/ppermute | solution.py:380
  71.3 23.3 %collective-permute-start.28 = (bf16[4,96,768]{2,1,0:T(8,128)(2,1)S(1)}, bf16[4,96,768]{2,1,0:T(8,128)(2,1)}, u32[]{:S(2)}, u32[]{:S(2)}) collective-permute-start(bf16[4,96,768]{2,1,0:T(8,128)(2,1)S(1)} %constant_dynamic-update-slice_fusion.6.refs_2_), channel_id=1, source_target_pairs={{0,4},{1,5},{2,6},{3,7},{4,0},{5,1},{6,2},{7,3},{8,12},{9,13},{10,... | collective-permute-start | bytes 1769480 | tf_op jit(solution)/shard_map/ppermute | solution.py:380
  81.8 12.8 %collective-permute-start.10 = (bf16[4,80,768]{2,1,0:T(8,128)(2,1)S(1)}, bf16[4,80,768]{2,1,0:T(8,128)(2,1)S(1)}, u32[]{:S(2)}, u32[]{:S(2)}) collective-permute-start(bf16[4,80,768]{2,1,0:T(8,128)(2,1)S(1)} %collective-permute-done.6.refs_3_), channel_id=1, source_target_pairs={{0,2},{1,3},{2,0},{3,1},{4,6},{5,7},{6,4},{7,5},{8,10},{9,11},{10,... | collective-permute-start | bytes 1474568 | tf_op jit(solution)/shard_map/ppermute | solution.py:380
  81.9 14.3 %collective-permute-start.8 = (bf16[4,80,768]{2,1,0:T(8,128)(2,1)S(1)}, bf16[4,80,768]{2,1,0:T(8,128)(2,1)S(1)}, u32[]{:S(2)}, u32[]{:S(2)}) collective-permute-start(bf16[4,80,768]{2,1,0:T(8,128)(2,1)S(1)} %collective-permute-done.2.refs_1_), channel_id=1, source_target_pairs={{0,2},{1,3},{2,0},{3,1},{4,6},{5,7},{6,4},{7,5},{8,10},{9,11},{10,... | collective-permute-start | bytes 1474568 | tf_op jit(solution)/shard_map/ppermute | solution.py:380
  84.8 32.7 %collective-permute-start.17 = (bf16[4,5,24,768]{3,2,1,0:T(8,128)(2,1)}, bf16[4,5,24,768]{3,2,1,0:T(8,128)(2,1)}, u32[]{:S(2)}, u32[]{:S(2)}) collective-permute-start(bf16[4,5,24,768]{3,2,1,0:T(8,128)(2,1)} %constant_dynamic-update-slice_fusion.3.refs_2_), channel_id=1, source_target_pairs={{0,4},{1,5},{2,6},{3,7},{4,0},{5,1},{6,2},{7,3},{8,12},{9,13},{10,... | collective-permute-start | bytes 2211848 | tf_op jit(solution)/shard_map/ppermute | solution.py:380
  86.4 31.7 %collective-permute-start.13 = (bf16[4,5,24,768]{3,2,1,0:T(8,128)(2,1)}, bf16[4,5,24,768]{3,2,1,0:T(8,128)(2,1)}, u32[]{:S(2)}, u32[]{:S(2)}) collective-permute-start(bf16[4,5,24,768]{3,2,1,0:T(8,128)(2,1)} %pad_maximum_fusion.2.refs_0_), channel_id=1, source_target_pairs={{0,1},{1,0},{2,3},{3,2},{4,5},{5,4},{6,7},{7,6},{8,9},{9,8},{10,11... | collective-permute-start | bytes 2211848 | tf_op jit(solution)/shard_map/ppermute | solution.py:380
  94.6 21.3 %collective-permute-start.29 = (bf16[4,96,768]{2,1,0:T(8,128)(2,1)}, bf16[4,96,768]{2,1,0:T(8,128)(2,1)}, u32[]{:S(2)}, u32[]{:S(2)}) collective-permute-start(bf16[4,96,768]{2,1,0:T(8,128)(2,1)} %pad_maximum_fusion.3.refs_0_), channel_id=1, source_target_pairs={{0,2},{1,3},{2,0},{3,1},{4,6},{5,7},{6,4},{7,5},{8,10},{9,11},{10,... | collective-permute-start | bytes 1769480 | tf_op jit(solution)/shard_map/ppermute | solution.py:380
  94.6 22.9 %collective-permute-start.24 = (bf16[4,96,768]{2,1,0:T(8,128)(2,1)}, bf16[4,96,768]{2,1,0:T(8,128)(2,1)}, u32[]{:S(2)}, u32[]{:S(2)}) collective-permute-start(bf16[4,96,768]{2,1,0:T(8,128)(2,1)} %pad_maximum_fusion.3.refs_0_), channel_id=1, source_target_pairs={{0,1},{1,0},{2,3},{3,2},{4,5},{5,4},{6,7},{7,6},{8,9},{9,8},{10,11... | collective-permute-start | bytes 1769480 | tf_op jit(solution)/shard_map/ppermute | solution.py:380
  96.2 22.0 %collective-permute-start.32 = (bf16[4,96,768]{2,1,0:T(8,128)(2,1)}, bf16[4,96,768]{2,1,0:T(8,128)(2,1)}, u32[]{:S(2)}, u32[]{:S(2)}) collective-permute-start(bf16[4,96,768]{2,1,0:T(8,128)(2,1)} %collective-permute-done.28.refs_3_), channel_id=1, source_target_pairs={{0,2},{1,3},{2,0},{3,1},{4,6},{5,7},{6,4},{7,5},{8,10},{9,11},{10,... | collective-permute-start | bytes 1769480 | tf_op jit(solution)/shard_map/ppermute | solution.py:380
  115.9 36.6 %collective-permute-start.20 = (bf16[4,5,24,768]{3,2,1,0:T(8,128)(2,1)}, bf16[4,5,24,768]{3,2,1,0:T(8,128)(2,1)S(1)}, u32[]{:S(2)}, u32[]{:S(2)}) collective-permute-start(bf16[4,5,24,768]{3,2,1,0:T(8,128)(2,1)} %constant_dynamic-update-slice_fusion.3.refs_2_), channel_id=1, source_target_pairs={{0,2},{1,3},{2,0},{3,1},{4,6},{5,7},{6,4},{7,5},{8,10},{9,11},{10,... | collective-permute-start | bytes 2211848 | tf_op jit(solution)/shard_map/ppermute | solution.py:380
  117.5 35.0 %collective-permute-start.18 = (bf16[4,5,24,768]{3,2,1,0:T(8,128)(2,1)}, bf16[4,5,24,768]{3,2,1,0:T(8,128)(2,1)S(1)}, u32[]{:S(2)}, u32[]{:S(2)}) collective-permute-start(bf16[4,5,24,768]{3,2,1,0:T(8,128)(2,1)} %pad_maximum_fusion.2.refs_0_), channel_id=1, source_target_pairs={{0,2},{1,3},{2,0},{3,1},{4,6},{5,7},{6,4},{7,5},{8,10},{9,11},{10,... | collective-permute-start | bytes 2211848 | tf_op jit(solution)/shard_map/ppermute | solution.py:380
  117.6 29.4 %collective-permute-start.30 = (bf16[4,96,768]{2,1,0:T(8,128)(2,1)}, bf16[4,96,768]{2,1,0:T(8,128)(2,1)S(1)}, u32[]{:S(2)}, u32[]{:S(2)}) collective-permute-start(bf16[4,96,768]{2,1,0:T(8,128)(2,1)} %collective-permute-done.24.refs_1_), channel_id=1, source_target_pairs={{0,2},{1,3},{2,0},{3,1},{4,6},{5,7},{6,4},{7,5},{8,10},{9,11},{10,... | collective-permute-start | bytes 1769480 | tf_op jit(solution)/shard_map/ppermute | solution.py:380
  118.1 34.5 %collective-permute-start.21 = (bf16[4,5,24,768]{3,2,1,0:T(8,128)(2,1)}, bf16[4,5,24,768]{3,2,1,0:T(8,128)(2,1)S(1)}, u32[]{:S(2)}, u32[]{:S(2)}) collective-permute-start(bf16[4,5,24,768]{3,2,1,0:T(8,128)(2,1)} %collective-permute-done.17.refs_3_), channel_id=1, source_target_pairs={{0,2},{1,3},{2,0},{3,1},{4,6},{5,7},{6,4},{7,5},{8,10},{9,11},{10,... | collective-permute-start | bytes 2211848 | tf_op jit(solution)/shard_map/ppermute | solution.py:380
  118.1 34.5 %collective-permute-start.19 = (bf16[4,5,24,768]{3,2,1,0:T(8,128)(2,1)}, bf16[4,5,24,768]{3,2,1,0:T(8,128)(2,1)S(1)}, u32[]{:S(2)}, u32[]{:S(2)}) collective-permute-start(bf16[4,5,24,768]{3,2,1,0:T(8,128)(2,1)} %collective-permute-done.13.refs_1_), channel_id=1, source_target_pairs={{0,2},{1,3},{2,0},{3,1},{4,6},{5,7},{6,4},{7,5},{8,10},{9,11},{10,... | collective-permute-start | bytes 2211848 | tf_op jit(solution)/shard_map/ppermute | solution.py:380
  398.4 47.2 %collective-permute-start.33 = (bf16[4,2,2,80,768]{4,3,2,1,0:T(8,128)(2,1)}, bf16[4,2,2,80,768]{4,3,2,1,0:T(8,128)(2,1)}, u32[]{:S(2)}, u32[]{:S(2)}) collective-permute-start(bf16[4,2,2,80,768]{4,3,2,1,0:T(8,128)(2,1)} %get-tuple-element.142), channel_id=1, source_target_pairs={{0,2},{1,3},{2,0},{3,1},{4,6},{5,7},{6,4},{7,5},{8,10},{9,11},{10,... | collective-permute-start | bytes 5898248 | tf_op jit(solution)/shard_map/ppermute | solution.py:380
  414.8 35.8 %collective-permute-start.49 = (bf16[4,2,2,96,768]{4,3,2,1,0:T(8,128)(2,1)}, bf16[4,2,2,96,768]{4,3,2,1,0:T(8,128)(2,1)}, u32[]{:S(2)}, u32[]{:S(2)}) collective-permute-start(bf16[4,2,2,96,768]{4,3,2,1,0:T(8,128)(2,1)} %get-tuple-element.154), channel_id=1, source_target_pairs={{0,2},{1,3},{2,0},{3,1},{4,6},{5,7},{6,4},{7,5},{8,10},{9,11},{10,... | collective-permute-start | bytes 7077896 | tf_op jit(solution)/shard_map/ppermute | solution.py:380
  445.4 52.8 %collective-permute-start.41 = (bf16[4,2,2,5,24,768]{5,4,3,2,1,0:T(8,128)(2,1)}, bf16[4,2,2,5,24,768]{5,4,3,2,1,0:T(8,128)(2,1)S(1)}, u32[]{:S(2)}, u32[]{:S(2)}) collective-permute-start(bf16[4,2,2,5,24,768]{5,4,3,2,1,0:T(8,128)(2,1)} %get-tuple-element.148), channel_id=1, source_target_pairs={{0,2},{1,3},{2,0},{3,1},{4,6},{5,7},{6,4},{7,5},{8,10},{9,11},{10,... | collective-permute-start | bytes 8847368 | tf_op jit(solution)/shard_map/ppermute | solution.py:380
  447.0 14.1 %collective-permute-start.37 = (bf16[2,2,80,768]{3,2,1,0:T(8,128)(2,1)S(1)}, bf16[2,2,80,768]{3,2,1,0:T(8,128)(2,1)S(1)}, u32[]{:S(2)}, u32[]{:S(2)}) collective-permute-start(bf16[2,2,80,768]{3,2,1,0:T(8,128)(2,1)S(1)} %fusion.11), channel_id=1, source_target_pairs={{0,4},{1,5},{2,6},{3,7},{4,0},{5,1},{6,2},{7,3},{8,12},{9,13},{10,... | collective-permute-start | bytes 1474568 | tf_op jit(solution)/shard_map/ppermute | solution.py:380
  449.1 14.8 %collective-permute-start.34 = (bf16[2,2,80,768]{3,2,0,1:T(8,128)(2,1)S(1)}, bf16[2,2,80,768]{3,2,0,1:T(8,128)(2,1)S(1)}, u32[]{:S(2)}, u32[]{:S(2)}) collective-permute-start(bf16[2,2,80,768]{3,2,0,1:T(8,128)(2,1)S(1)} %fusion.10), channel_id=1, source_target_pairs={{0,1},{1,0},{2,3},{3,2},{4,5},{5,4},{6,7},{7,6},{8,9},{9,8},{10,11... | collective-permute-start | bytes 1474568 | tf_op jit(solution)/shard_map/ppermute | solution.py:380
  452.6 33.6 %collective-permute-start.53 = (bf16[2,2,96,768]{3,2,1,0:T(8,128)(2,1)}, bf16[2,2,96,768]{3,2,1,0:T(8,128)(2,1)}, u32[]{:S(2)}, u32[]{:S(2)}) collective-permute-start(bf16[2,2,96,768]{3,2,1,0:T(8,128)(2,1)} %fusion.6), channel_id=1, source_target_pairs={{0,4},{1,5},{2,6},{3,7},{4,0},{5,1},{6,2},{7,3},{8,12},{9,13},{10,... | collective-permute-start | bytes 1769480 | tf_op jit(solution)/shard_map/ppermute | solution.py:380
  464.1 14.4 %collective-permute-start.35 = (bf16[2,80,768]{2,1,0:T(8,128)(2,1)S(1)}, bf16[2,80,768]{2,1,0:T(8,128)(2,1)S(1)}, u32[]{:S(2)}, u32[]{:S(2)}) collective-permute-start(bf16[2,80,768]{2,1,0:T(8,128)(2,1)S(1)} %fusion.25), channel_id=1, source_target_pairs={{0,4},{1,5},{2,6},{3,7},{4,0},{5,1},{6,2},{7,3},{8,12},{9,13},{10,... | collective-permute-start | bytes 737288 | tf_op jit(solution)/shard_map/ppermute | solution.py:380
  469.5 10.2 %collective-permute-start.39 = (bf16[80,768]{1,0:T(8,128)(2,1)S(1)}, bf16[80,768]{1,0:T(8,128)(2,1)S(1)}, u32[]{:S(2)}, u32[]{:S(2)}) collective-permute-start(bf16[80,768]{1,0:T(8,128)(2,1)S(1)} %get-tuple-element.214), channel_id=1, source_target_pairs={{0,16},{1,17},{2,18},{3,19},{4,20},{5,21},{6,22},{7,23},{8,24},{9,... | collective-permute-start | bytes 368648 | tf_op jit(solution)/shard_map/ppermute | solution.py:380
  469.8 11.3 %collective-permute-start.40 = (bf16[80,768]{1,0:T(8,128)(2,1)S(1)}, bf16[80,768]{1,0:T(8,128)(2,1)S(1)}, u32[]{:S(2)}, u32[]{:S(2)}) collective-permute-start(bf16[80,768]{1,0:T(8,128)(2,1)S(1)} %get-tuple-element.215), channel_id=1, source_target_pairs={{0,24},{1,25},{2,26},{3,27},{4,28},{5,29},{6,30},{7,31},{8,16},{9,... | collective-permute-start | bytes 368648 | tf_op jit(solution)/shard_map/ppermute | solution.py:380
  479.6 16.6 %collective-permute-start.50 = (bf16[2,2,96,768]{3,2,0,1:T(8,128)(2,1)}, bf16[2,2,96,768]{3,2,0,1:T(8,128)(2,1)}, u32[]{:S(2)}, u32[]{:S(2)}) collective-permute-start(bf16[2,2,96,768]{3,2,0,1:T(8,128)(2,1)} %fusion.5), channel_id=1, source_target_pairs={{0,1},{1,0},{2,3},{3,2},{4,5},{5,4},{6,7},{7,6},{8,9},{9,8},{10,11... | collective-permute-start | bytes 1769480 | tf_op jit(solution)/shard_map/ppermute | solution.py:380
  487.9 14.3 %collective-permute-start.54 = (bf16[2,96,768]{2,1,0:T(8,128)(2,1)S(1)}, bf16[2,96,768]{2,1,0:T(8,128)(2,1)S(1)}, u32[]{:S(2)}, u32[]{:S(2)}) collective-permute-start(bf16[2,96,768]{2,1,0:T(8,128)(2,1)S(1)} %fusion.21), channel_id=1, source_target_pairs={{0,1},{1,0},{2,3},{3,2},{4,5},{5,4},{6,7},{7,6},{8,9},{9,8},{10,11... | collective-permute-start | bytes 884744 | tf_op jit(solution)/shard_map/ppermute | solution.py:380
  497.7 10.0 %collective-permute-start.51 = (bf16[2,96,768]{2,1,0:T(8,128)(2,1)S(1)}, bf16[2,96,768]{2,1,0:T(8,128)(2,1)S(1)}, u32[]{:S(2)}, u32[]{:S(2)}) collective-permute-start(bf16[2,96,768]{2,1,0:T(8,128)(2,1)S(1)} %fusion.20), channel_id=1, source_target_pairs={{0,4},{1,5},{2,6},{3,7},{4,0},{5,1},{6,2},{7,3},{8,12},{9,13},{10,... | collective-permute-start | bytes 884744 | tf_op jit(solution)/shard_map/ppermute | solution.py:380
  498.5 21.4 %collective-permute-start.45 = (bf16[2,2,5,24,768]{4,3,2,1,0:T(8,128)(2,1)S(1)}, bf16[2,2,5,24,768]{4,3,2,1,0:T(8,128)(2,1)S(1)}, u32[]{:S(2)}, u32[]{:S(2)}) collective-permute-start(bf16[2,2,5,24,768]{4,3,2,1,0:T(8,128)(2,1)S(1)} %fusion.1), channel_id=1, source_target_pairs={{0,4},{1,5},{2,6},{3,7},{4,0},{5,1},{6,2},{7,3},{8,12},{9,13},{10,... | collective-permute-start | bytes 2211848 | tf_op jit(solution)/shard_map/ppermute | solution.py:380
  500.3 21.2 %collective-permute-start.42 = (bf16[2,2,5,24,768]{4,3,2,0,1:T(8,128)(2,1)S(1)}, bf16[2,2,5,24,768]{4,3,2,0,1:T(8,128)(2,1)S(1)}, u32[]{:S(2)}, u32[]{:S(2)}) collective-permute-start(bf16[2,2,5,24,768]{4,3,2,0,1:T(8,128)(2,1)S(1)} %fusion), channel_id=1, source_target_pairs={{0,1},{1,0},{2,3},{3,2},{4,5},{5,4},{6,7},{7,6},{8,9},{9,8},{10,11... | collective-permute-start | bytes 2211848 | tf_op jit(solution)/shard_map/ppermute | solution.py:380
  502.3 30.0 %collective-permute-start.55 = (bf16[96,768]{1,0:T(8,128)(2,1)S(1)}, bf16[96,768]{1,0:T(8,128)(2,1)S(1)}, u32[]{:S(2)}, u32[]{:S(2)}) collective-permute-start(bf16[96,768]{1,0:T(8,128)(2,1)S(1)} %get-tuple-element.201), channel_id=1, source_target_pairs={{0,16},{1,17},{2,18},{3,19},{4,20},{5,21},{6,22},{7,23},{8,24},{9,... | collective-permute-start | bytes 442376 | tf_op jit(solution)/shard_map/ppermute | solution.py:380
  505.4 28.1 %collective-permute-start.56 = (bf16[96,768]{1,0:T(8,128)(2,1)S(1)}, bf16[96,768]{1,0:T(8,128)(2,1)S(1)}, u32[]{:S(2)}, u32[]{:S(2)}) collective-permute-start(bf16[96,768]{1,0:T(8,128)(2,1)S(1)} %get-tuple-element.202), channel_id=1, source_target_pairs={{0,24},{1,25},{2,26},{3,27},{4,28},{5,29},{6,30},{7,31},{8,16},{9,... | collective-permute-start | bytes 442376 | tf_op jit(solution)/shard_map/ppermute | solution.py:380
  507.8 25.8 %collective-permute-start.52 = (bf16[96,768]{1,0:T(8,128)(2,1)S(1)}, bf16[96,768]{1,0:T(8,128)(2,1)S(1)}, u32[]{:S(2)}, u32[]{:S(2)}) collective-permute-start(bf16[96,768]{1,0:T(8,128)(2,1)S(1)} %fusion.32), channel_id=1, source_target_pairs={{0,8},{1,9},{2,10},{3,11},{4,12},{5,13},{6,14},{7,15},{8,0},{9,1},... | collective-permute-start | bytes 442376 | tf_op jit(solution)/shard_map/ppermute | solution.py:380
  527.8 12.5 %collective-permute-start.47 = (bf16[5,24,768]{2,1,0:T(8,128)(2,1)S(1)}, bf16[5,24,768]{2,1,0:T(8,128)(2,1)S(1)}, u32[]{:S(2)}, u32[]{:S(2)}) collective-permute-start(bf16[5,24,768]{2,1,0:T(8,128)(2,1)S(1)} %get-tuple-element.199), channel_id=1, source_target_pairs={{0,16},{1,17},{2,18},{3,19},{4,20},{5,21},{6,22},{7,23},{8,24},{9,... | collective-permute-start | bytes 552968 | tf_op jit(solution)/shard_map/ppermute | solution.py:380
  (40 other events, 496.3 us)

commit v3 on v2

v3 whole, which is shorter than its diff:
```python
import functools

import jax
import jax.numpy as jnp
from jax import lax
from jax.experimental import pallas as pl
from jax.experimental.pallas import tpu as pltpu
from jax.sharding import PartitionSpec as P

F32 = jnp.float32
BF16 = jnp.bfloat16
HEADS = 12
HEAD_DIM = 64
NORM_EPS = 1e-06
ROOT_HALF = 0.7071067811865476
ROOT_TWO_PI = 0.3989422804014327
VMEM_BYTES = 60 << 20


def dot_nn(left, right):
    return jnp.dot(left, right, preferred_element_type=F32)


def dot_nt(left, right):
    return lax.dot_general(left, right, (((1,), (1,)), ((), ())), preferred_element_type=F32)


def dot_tn(left, right):
    return lax.dot_general(left, right, (((0,), (0,)), ((), ())), preferred_element_type=F32)


def lane_masks(rows):
    lane = lax.broadcasted_iota(jnp.int32, (rows, 128), 1)
    first = jnp.where(lane < HEAD_DIM, 1.0, 0.0)
    return first, 1.0 - first


def key_counts(rows, tokens):
    row = lax.broadcasted_iota(jnp.int32, (rows, 128), 0)
    return jnp.where(row < tokens, 1.0, 2.0)


def gelu_parts(u):
    bell = jnp.exp(u * u * -0.5)
    t = pl.reciprocal(1.0 + (0.3275911 * ROOT_HALF) * jnp.abs(u))
    poly = t * (
        0.5 * 0.254829592
        + t * (0.5 * -0.284496736 + t * (0.5 * 1.421413741 + t * (0.5 * -1.453152027 + t * (0.5 * 1.061405429))))
    )
    tail = poly * bell
    cdf = jnp.where(u < 0.0, tail, 1.0 - tail)
    return u * cdf, cdf + u * bell * ROOT_TWO_PI


def attend_forward(tok, mem, wq, wk, wv, vec, x_o, q_o, k_o, v_o, e_o, o_o, li_o):
    bq, bv = vec[0, 0:1, :], vec[0, 1:2, :]
    seg = tok.shape[2]
    rows = x_o.shape[1]
    x_o[0, rows - 16 :, :] = mem[0].astype(BF16)
    x_o[0, :seg, :] = tok[0, 0]
    x = x_o[0]
    q_o[0] = ((dot_nn(x, wq[...]) + bq).astype(BF16).astype(F32) * 0.125).astype(BF16)
    k_o[0] = dot_nn(x, wk[...]).astype(BF16)
    v_o[0] = (dot_nn(x, wv[...]) + bv).astype(BF16)
    masks = lane_masks(rows)
    count = key_counts(rows, seg)
    low_masks = tuple(m.astype(BF16) for m in masks)

    def pair(p, carry):
        at = pl.ds(pl.multiple_of(p * 128, 128), 128)
        q2 = q_o[0, :, at]
        k2 = k_o[0, :, at]
        v2 = v_o[0, :, at].astype(F32) * count
        total = None
        for h in range(2):
            s = dot_nt(q2 * low_masks[h], k2)
            e = jnp.exp(s - jnp.max(s, axis=-1, keepdims=True)).astype(BF16)
            e_o[0, 2 * p + h] = e
            right = jnp.concatenate(
                [(v2 * masks[h]).astype(BF16), (count * masks[h]).astype(BF16)], axis=1
            )
            part = dot_nn(e, right)
            total = part if total is None else total + part
        inv = 1.0 / total[:, 128:]
        li_o[0, :, at] = inv
        o_o[0, :, at] = (total[:, :128] * inv).astype(BF16)
        return carry

    lax.fori_loop(0, HEADS // 2, pair, 0, unroll=True)


def norm_rows(r):
    mean = jnp.mean(r, axis=-1, keepdims=True)
    center = r - mean
    var = jnp.mean(center * center, axis=-1, keepdims=True)
    scale = lax.rsqrt(var + NORM_EPS)
    return center * scale, scale


def feed_forward(
    segment, step,
    count, tok, mem, o, wo, wup, wdown, vec, bup,
    y_o, mem_o, xh1_o, sc1_o, h_o, a_o, gp_o, xh2_o, sc2_o, x_s,
):
    seg = tok.shape[2]
    rows = o.shape[1]
    ff = wup.shape[1]
    bo, bdown, g1, s1, g2, s2 = (vec[0, r : r + 1, :] for r in (2, 3, 4, 5, 16, 17))
    x_s[rows - 16 :, :] = mem[0]
    x_s[:seg, :] = tok[0, 0].astype(F32)
    xh, sc = norm_rows(x_s[...] + dot_nn(o[0], wo[...]) + bo)
    xh1_o[0] = xh.astype(BF16)
    sc1_o[0] = jnp.broadcast_to(sc, (rows, 128))
    h1 = xh * g1 + s1
    h_o[0] = h1.astype(BF16)
    x_s[...] = h1 + bdown

    def chunk(j, carry):
        at = pl.ds(pl.multiple_of(j * step, step), step)
        act, slope = gelu_parts(dot_nn(h_o[0], wup[:, at]) + bup[:, at])
        a_o[0, :, at] = act.astype(BF16)
        gp_o[0, :, at] = slope.astype(BF16)
        x_s[...] += dot_nn(a_o[0, :, at], wdown[at, :])
        return carry

    lax.fori_loop(0, ff // step, chunk, 0, unroll=True)
    xh, sc = norm_rows(x_s[...])
    xh2_o[0] = xh.astype(BF16)
    sc2_o[0] = jnp.broadcast_to(sc, (rows, 128))
    x_s[...] = xh * g2 + s2
    active = count[pl.program_id(0)] > segment
    y_o[0, 0] = jnp.where(active, x_s[:seg, :], 0.0).astype(BF16)
    mem_o[0] = jnp.where(active, x_s[rows - 16 :, :], mem[0])


def norm_back(dy, xh, sc, gain):
    dxh = dy * gain
    m1 = jnp.mean(dxh, axis=-1, keepdims=True)
    m2 = jnp.mean(dxh * xh, axis=-1, keepdims=True)
    return sc * (dxh - m1 - xh * m2)


def col_sum(x):
    return jnp.sum(x, axis=0, keepdims=True)


def feed_backward(
    segment, step,
    count, cot, dmem, xh2, sc2, gp, xh1, sc1, wup, wdown, vec,
    df_o, du_o, dr_o, db_o, vec_o, vup_o, x_s,
):
    seg = cot.shape[2]
    rows = xh2.shape[1]
    ff = wup.shape[1]
    g1, g2 = vec[0, 4:5, :], vec[0, 16:17, :]
    active = jnp.where(count[pl.program_id(0)] > segment, 1.0, 0.0)
    x_s[rows - 16 :, :] = dmem[0] * active
    x_s[:seg, :] = cot[0, 0].astype(F32) * active
    dy = x_s[...]
    xh = xh2[0].astype(F32)
    vec_o[0, 4:5, :] = col_sum(dy * xh)
    vec_o[0, 5:6, :] = col_sum(dy)
    dr = norm_back(dy, xh, sc2[0, :, :1], g2)
    df = dr.astype(BF16)
    df_o[0] = df
    vec_o[0, 1:2, :] = col_sum(df.astype(F32))
    x_s[...] = dr

    def chunk(j, carry):
        at = pl.ds(pl.multiple_of(j * step, step), step)
        du = dot_nt(df_o[0], wdown[at, :]) * gp[0, :, at].astype(F32)
        vup_o[0, :, at] = col_sum(du)
        du_o[0, :, at] = du.astype(BF16)
        x_s[...] += dot_nt(du_o[0, :, at], wup[:, at])
        return carry

    lax.fori_loop(0, ff // step, chunk, 0, unroll=True)
    dh = x_s[...]
    xh = xh1[0].astype(F32)
    vec_o[0, 2:3, :] = col_sum(dh * xh)
    vec_o[0, 3:4, :] = col_sum(dh)
    dr = norm_back(dh, xh, sc1[0, :, :1], g1)
    dr_o[0] = dr
    db_o[0] = dr.astype(BF16)
    vec_o[0, 0:1, :] = col_sum(dr)


def attend_backward(
    segment, first,
    count, dmem, dr, db, q, k, v, e, o, li, wo, wq, wk, wv,
    tg_o, dmem_o, dq_o, dk_o, dv_o, vec_o, do_s, x_s,
):
    seg = tg_o.shape[2]
    rows = q.shape[1]
    do_s[...] = dot_nt(db[0], wo[...]).astype(BF16)
    masks = lane_masks(rows)
    count2 = key_counts(rows, seg)
    low_masks = tuple(m.astype(BF16) for m in masks)
    ones = jnp.ones((rows, 128), BF16)

    def pair(p, carry):
        at = pl.ds(pl.multiple_of(p * 128, 128), 128)
        dop = do_s[:, at].astype(F32) * li[0, :, at]
        pr = (dop * o[0, :, at].astype(F32) * -1.0).astype(BF16)
        dop = dop.astype(BF16)
        q2 = q[0, :, at]
        k2 = (k[0, :, at].astype(F32) * (count2 * 0.125)).astype(BF16)
        right = jnp.concatenate([v[0, :, at], ones], axis=1)
        dq = dk = dv = None
        for h in range(2):
            e_h = e[0, 2 * p + h]
            d_h = dop * low_masks[h]
            left = jnp.concatenate([d_h, pr * low_masks[h]], axis=1)
            ds = (e_h.astype(F32) * dot_nt(left, right)).astype(BF16)
            q_t = dot_nn(ds, k2 * low_masks[h])
            k_t = dot_tn(ds, q2 * low_masks[h])
            v_t = dot_tn(e_h, d_h)
            dq = q_t if dq is None else dq + q_t
            dk = k_t if dk is None else dk + k_t
            dv = v_t if dv is None else dv + v_t
        dq_o[0, :, at] = dq.astype(BF16)
        dk_o[0, :, at] = (dk * count2).astype(BF16)
        dv_o[0, :, at] = (dv * count2).astype(BF16)
        return carry

    lax.fori_loop(0, HEADS // 2, pair, 0, unroll=True)
    vec_o[0, 0:1, :] = col_sum(dq_o[0].astype(F32))
    vec_o[0, 1:2, :] = col_sum(dv_o[0].astype(F32))
    x_s[...] = (
        dr[0]
        + dot_nt(dq_o[0], wq[...])
        + dot_nt(dk_o[0], wk[...])
        + dot_nt(dv_o[0], wv[...])
    )
    tg_o[0, 0] = x_s[:seg, :].astype(BF16)
    kept = jnp.where(count[pl.program_id(0) + first] > segment, 0.0, 1.0)
    dmem_o[0] = dmem[0] * kept + x_s[rows - 16 :, :]


def weight_product(parts, *refs):
    lefts = refs[:parts]
    rights = refs[parts : 2 * parts]
    out = refs[2 * parts]
    total = None
    for left, right in zip(lefts, rights):
        for i in range(left.shape[0]):
            term = dot_tn(left[i], right[i])
            total = term if total is None else total + term
    out[...] = total.astype(out.dtype)


def whole(array):
    dims = array.shape
    return pl.BlockSpec(dims, lambda *g: (0,) * len(dims), pipeline_mode=pl.Buffered(1))


def per_item(dims, first=0):
    return pl.BlockSpec((1,) + dims, lambda i: (i + first,) + (0,) * len(dims))


def per_segment(dims, segment, first=0):
    return pl.BlockSpec((1, 1) + dims, lambda i: (i + first, segment) + (0,) * len(dims))


def memory_spec(array, first=0):
    shared = array.shape[0] == 1
    return pl.BlockSpec((1, 16, array.shape[2]), lambda i: (0 if shared else i + first, 0, 0))


def out_of(items, dims, dtype):
    return jax.ShapeDtypeStruct((items,) + dims, dtype)


SCALARS = pl.BlockSpec(memory_space=pltpu.SMEM)


def params(**more):
    return pltpu.CompilerParams(vmem_limit_bytes=VMEM_BYTES, **more)


def launch(body, grid, args, in_specs, out_specs, out_shape, into=None, **more):
    into = into or {}
    n_in = len(args)
    aliases = {n_in + k: o for k, o in enumerate(into)}

    def run(*refs):
        body(*refs[:n_in], *refs[n_in + len(into) :])

    return pl.pallas_call(
        run if into else body,
        grid=grid,
        in_specs=list(in_specs) + [pl.BlockSpec(memory_space=pl.ANY)] * len(into),
        out_specs=out_specs,
        out_shape=out_shape,
        input_output_aliases=aliases,
        compiler_params=params(),
        **more,
    )(*args, *into.values())


def call_attend_forward(segment, tokens, mem, wq, wk, wv, vec, first=0, many=None, into=None):
    items, _, seg, width = tokens.shape
    many = many or items
    rows = seg + 10
    outs = [((rows, width), BF16)] * 4 + [((HEADS, rows, rows), BF16), ((rows, width), BF16), ((rows, width), F32)]
    return launch(
        attend_forward,
        (many,),
        (tokens, mem, wq, wk, wv, vec),
        [per_segment((seg, width), segment, first), memory_spec(mem, first)] + [whole(w) for w in (wq, wk, wv, vec)],
        [per_item(d, first) for d, t in outs],
        [out_of(items, d, t) for d, t in outs],
        into=dict(enumerate(into)) if into else None,
        cost_estimate=pl.CostEstimate(flops=many * 2 * rows * (3 * width * width + 8 * rows * width), bytes_accessed=many * rows * (width * 14 + HEADS * rows * 2), transcendentals=0),
        name="attend_forward",
    )


def call_feed_forward(segment, count, tokens, mem, o, wo, wup, wdown, vec, bup, into=None):
    items, segments, seg, width = tokens.shape
    rows = o.shape[1]
    ff = wup.shape[1]
    outs = [
        ((16, width), F32), ((rows, width), BF16), ((rows, 128), F32), ((rows, width), BF16),
        ((rows, ff), BF16), ((rows, ff), BF16), ((rows, width), BF16), ((rows, 128), F32),
    ]
    fixed = (wo, wup, wdown, vec, bup)

    def body(*refs):
        feed_forward(segment, 768, *refs)

    return pl_scratch(
        body, (items,), (count, tokens, mem, o) + fixed,
        [SCALARS, per_segment((seg, width), segment), memory_spec(mem), per_item((rows, width))] + [whole(w) for w in fixed],
        [per_segment((seg, width), segment)] + [per_item(d) for d, t in outs],
        [out_of(items, (segments, seg, width), BF16)] + [out_of(items, d, t) for d, t in outs],
        [pltpu.VMEM((rows, width), F32)],
        into={0: into} if into is not None else None,
        cost_estimate=pl.CostEstimate(flops=items * 2 * rows * width * (width + 2 * ff), bytes_accessed=items * rows * (width * 14 + ff * 4), transcendentals=0),
        name="feed_forward",
    )


def pl_scratch(body, grid, args, in_specs, out_specs, out_shape, scratch, into=None, **more):
    return launch(body, grid, args, in_specs, out_specs, out_shape, into=into, scratch_shapes=scratch, **more)


def call_feed_backward(segment, count, cot, dmem, xh2, sc2, gp, xh1, sc1, wup, wdown, vec):
    items, _, seg, width = cot.shape
    rows = xh2.shape[1]
    ff = wup.shape[1]
    outs = [((rows, width), BF16), ((rows, ff), BF16), ((rows, width), F32), ((rows, width), BF16), ((8, width), F32), ((1, ff), F32)]
    fixed = (wup, wdown, vec)

    def body(*refs):
        feed_backward(segment, 768, *refs)

    return pl_scratch(
        body, (items,), (count, cot, dmem, xh2, sc2, gp, xh1, sc1) + fixed,
        [SCALARS, per_segment((seg, width), segment)] + [per_item(a.shape[1:]) for a in (dmem, xh2, sc2, gp, xh1, sc1)] + [whole(w) for w in fixed],
        [per_item(d) for d, t in outs],
        [out_of(items, d, t) for d, t in outs],
        [pltpu.VMEM((rows, width), F32)],
        cost_estimate=pl.CostEstimate(flops=items * 4 * rows * width * ff, bytes_accessed=items * rows * (width * 14 + ff * 4), transcendentals=0),
        name="feed_backward",
    )


def call_attend_backward(segment, segments, seg, count, dmem, dr, db, q, k, v, e, o, li, wo, wq, wk, wv, first=0, many=None, into=None):
    items, rows, width = q.shape
    many = many or items
    outs = [((16, width), F32)] + [((rows, width), BF16)] * 3 + [((8, width), F32)]
    fixed = (wo, wq, wk, wv)

    def body(*refs):
        attend_backward(segment, first, *refs)

    return pl_scratch(
        body, (many,), (count, dmem, dr, db, q, k, v, e, o, li) + fixed,
        [SCALARS] + [per_item(a.shape[1:], first) for a in (dmem, dr, db, q, k, v, e, o, li)] + [whole(w) for w in fixed],
        [per_segment((seg, width), segment, first)] + [per_item(d, first) for d, t in outs],
        [out_of(items, (segments, seg, width), BF16)] + [out_of(items, d, t) for d, t in outs],
        [pltpu.VMEM((rows, width), BF16), pltpu.VMEM((rows, width), F32)],
        into=into,
        cost_estimate=pl.CostEstimate(flops=many * 2 * rows * width * (4 * width + 16 * rows), bytes_accessed=many * rows * (width * 24 + HEADS * rows * 2), transcendentals=0),
        name="attend_backward",
    )


def call_weight_product(lefts, rights, step_left, step_right, dtype):
    parts = len(lefts)
    items, rows, n_left = lefts[0].shape
    n_right = rights[0].shape[2]
    left_spec = pl.BlockSpec((items, rows, step_left), lambda i, j: (0, 0, i))
    right_spec = pl.BlockSpec((items, rows, step_right), lambda i, j: (0, 0, j))
    return pl.pallas_call(
        functools.partial(weight_product, parts),
        grid=(n_left // step_left, n_right // step_right),
        in_specs=[left_spec] * parts + [right_spec] * parts,
        out_specs=pl.BlockSpec((step_left, step_right), lambda i, j: (i, j)),
        out_shape=jax.ShapeDtypeStruct((n_left, n_right), dtype),
        compiler_params=params(),
        cost_estimate=pl.CostEstimate(flops=2 * parts * items * rows * n_left * n_right, bytes_accessed=2 * parts * items * rows * (n_left + n_right), transcendentals=0),
        name="weight_product",
    )(*lefts, *rights)


AXES = ("dp", "shard")
UNIT = 24


def spot(z, y, c, x):
    return ((z * 2 + y) * 2 + c) * 2 + x


def swap(array, dz, dy, dc, dx):
    pairs = [
        (spot(z, y, c, x), spot(z ^ dz, y ^ dy, c ^ dc, x ^ dx))
        for z in range(4)
        for y in range(2)
        for c in range(2)
        for x in range(2)
    ]
    return lax.ppermute(array, AXES, pairs)


def coordinates():
    dp = lax.axis_index("dp")
    return jnp.stack([dp // 4, dp // 2 % 2, dp % 2, lax.axis_index("shard")]).astype(jnp.int32)


def join(*parts):
    return jnp.concatenate(parts, axis=0)


def after(array, *others):
    return lax.optimization_barrier((array,) + others)[0]


def gather_z(unit):
    one, two, three = swap(unit, 1, 0, 0, 0), swap(unit, 2, 0, 0, 0), swap(unit, 3, 0, 0, 0)
    return jnp.stack([unit, one]), jnp.stack([two, three])


def gather_near(a, b):
    return join(a, swap(a, 0, 1, 0, 0)), join(b, swap(b, 0, 0, 0, 1))


def gather_far(a, b):
    return (a, swap(a, 0, 0, 0, 1), b, swap(b, 0, 1, 0, 0))


def gather_core(mine):
    return mine + tuple(swap(m, 0, 0, 1, 0) for m in mine)


def add_low(left, right):
    return (left.astype(F32) + right.astype(F32)).astype(BF16)


def reduce_core(keep, send):
    got = swap(send, 0, 0, 1, 0)
    send_a = add_low(keep[:2, :, 1], got[:2, :, 1])
    send_b = add_low(keep[2:, 1], got[2:, 1])
    return (send_a, send_b), (keep, got)


def reduce_far(sends, held):
    keep, got = held
    got_a = swap(sends[0], 0, 0, 0, 1)
    got_b = swap(sends[1], 0, 1, 0, 0)
    a = keep[:2, :, 0].astype(F32) + got[:2, :, 0].astype(F32) + got_a.astype(F32)
    b = keep[2:, 0].astype(F32) + got[2:, 0].astype(F32) + got_b.astype(F32)
    return (a[:, 1].astype(BF16), b[:, 1].astype(BF16)), (a[:, 0], b[:, 0])


def reduce_near(sends, held):
    a = held[0] + swap(sends[0], 0, 1, 0, 0).astype(F32)
    b = held[1] + swap(sends[1], 0, 0, 0, 1).astype(F32)
    return (a[1].astype(BF16), b[0].astype(BF16), b[1].astype(BF16)), a[0]


def reduce_z(sends, held):
    for step, array in enumerate(sends):
        held = held + swap(array, step + 1, 0, 0, 0).astype(F32)
    return held


def unit_pairs(me, bufs, emit):
    mz, my, mc, mx = me[0], me[1], me[2], me[3]
    flip = jnp.broadcast_to(mx, (8, 128)) == 1

    def send(dz, dy, dc, near, far):
        dp = ((mz ^ dz) * 2 + (my ^ dy)) * 2 + (mc ^ dc)
        emit(dp, near, far)

    for dc in range(2):
        a, a_far, b, b_far = bufs[4 * dc : 4 * dc + 4]
        for i in range(2):
            for j in range(2):
                send(j, i, dc, (a, 2 * i + j), (a_far, 2 * i + j))
        for i, buf in enumerate((b, b_far)):
            for j in range(2):
                send(2 + j, i, dc, (buf, j), (buf, 2 + j))


def pack_first(wq, wk, wv, vec, bup, out):
    blocks = [vec[8 * c : 8 * c + 8, :] for c in range(3)] + [jnp.broadcast_to(bup[...], (8, 128))]
    width = out.shape[1]
    tail = jnp.concatenate(blocks + [jnp.zeros((8, width - 512), F32)], axis=1)
    out[...] = jnp.concatenate([w[...].astype(F32) for w in (wq, wk, wv)] + [tail], axis=0).astype(BF16)


def assemble_first(me, *refs):
    bufs, (wq, wk, wv, vec, bup, small) = refs[:8], refs[8:]
    mx = me[3]

    def emit(dp, near, far):
        n = near[0][near[1]].astype(F32)
        f = far[0][far[1]].astype(F32)
        low = jnp.where(mx == 0, n, f)
        high = jnp.where(mx == 0, f, n)
        at = pl.ds(pl.multiple_of(dp * 48, 16), 48)
        for w, ref in enumerate((wq, wk, wv)):
            ref[at, :] = jnp.concatenate(
                [low[UNIT * w : UNIT * (w + 1)], high[UNIT * w : UNIT * (w + 1)]], axis=0
            ).astype(BF16)
        for x, rows in enumerate((low, high)):
            for c in range(4):
                small[dp * 2 + x, 8 * c : 8 * c + 8, :] = rows[3 * UNIT :, 128 * c : 128 * c + 128]

    unit_pairs(me, bufs, emit)
    for idx in range(small.shape[0]):
        vec[0, :, UNIT * idx : UNIT * (idx + 1)] = small[idx, :24, :UNIT]
        bup[:, 4 * UNIT * idx : 4 * UNIT * (idx + 1)] = small[idx, 24:25, : 4 * UNIT]


def assemble_rest(units, wo, wup, wdown):
    count = units.shape[0]
    width = wo.shape[1]
    for w in range(5):
        rows = jnp.concatenate([units[i, w].astype(F32) for i in range(count)], axis=0).astype(BF16)
        if w == 0:
            wo[...] = rows
        else:
            wup[:, (w - 1) * width : w * width] = rows
    for i in range(0, count):
        rows = jnp.concatenate([units[i, w].astype(F32) for w in range(5, 9)], axis=0)
        wdown[4 * UNIT * i : 4 * UNIT * (i + 1), :] = rows.astype(BF16)


def call_assemble_rest(units, ff):
    devices, blocks, rows, width = units.shape
    step = 8
    return pl.pallas_call(
        assemble_rest,
        grid=(devices // step,),
        in_specs=[pl.BlockSpec((step, blocks, rows, width), lambda i: (i, 0, 0, 0))],
        out_specs=[
            pl.BlockSpec((step * rows, width), lambda i: (i, 0)),
            pl.BlockSpec((step * rows, ff), lambda i: (i, 0)),
            pl.BlockSpec((step * rows * 4, width), lambda i: (i, 0)),
        ],
        out_shape=[jax.ShapeDtypeStruct(d, BF16) for d in ((width, width), (width, ff), (ff, width))],
        compiler_params=params(),
        name="assemble_rest",
    )(units)


def call_pack_first(wq, wk, wv, vec, bup):
    return pl.pallas_call(
        pack_first, out_shape=jax.ShapeDtypeStruct((3 * UNIT + 8, wq.shape[1]), BF16), name="pack_first"
    )(wq, wk, wv, vec, bup)


def call_assemble(body, me, bufs, outs, name, scratch=()):
    vm = pl.BlockSpec(memory_space=pltpu.VMEM)
    return pl.pallas_call(
        body,
        in_specs=[SCALARS] + [vm] * 8,
        out_specs=[vm] * len(outs),
        out_shape=[jax.ShapeDtypeStruct(d, t) for d, t in outs],
        scratch_shapes=list(scratch),
        compiler_params=params(),
        name=name,
    )(me, *bufs)


def emit_units(me, keep, send, value_of):
    mz, my, mc, mx = me[0], me[1], me[2], me[3]
    for core in range(2):

        @pl.when(mc == core)
        def _():
            for z in range(4):
                for y in range(2):
                    for x in range(2):
                        to = (z ^ mz, y ^ my, x ^ mx)
                        keep[to] = value_of(z, y, core, x)
                        send[to] = value_of(z, y, 1 - core, x)


def product_sum(lefts, rights):
    total = None
    for left, right in zip(lefts, rights):
        for i in range(left.shape[0]):
            term = dot_tn(left[i], right[i])
            total = term if total is None else total + term
    return total


def product_up(segments, me, *refs):
    o, db, h, du = (refs[segments * i : segments * (i + 1)] for i in range(4))
    keep, send, acc = refs[4 * segments :]

    @pl.when(pl.program_id(0) == 0)
    def _():
        acc[...] = product_sum(o, db)

    @pl.when(pl.program_id(0) > 0)
    def _():
        acc[...] = product_sum(h, du)

    def value_of(*at):
        idx = spot(*at)
        return acc[UNIT * idx : UNIT * (idx + 1), :].astype(BF16)

    emit_units(me, keep.at[:, :, :, 0], send.at[:, :, :, 0], value_of)


def product_down(segments, me, *refs):
    a, df = refs[:segments], refs[segments : 2 * segments]
    keep, send, acc = refs[2 * segments :]
    tall = 4 * UNIT
    acc[...] = product_sum(a, df)
    my, mc, mx = me[1], me[2], me[3]
    for core in range(2):

        @pl.when(mc == core)
        def _():
            for y in range(2):
                for x in range(2):
                    for ref, c in ((keep, core), (send, 1 - core)):
                        row = ((y * 2 + c) * 2 + x) * tall
                        ref[0, y ^ my, x ^ mx] = acc[row : row + tall, :].astype(BF16)


def product_first(segments, me, *refs):
    vat, vec, vup = (refs[segments * i : segments * (i + 1)] for i in range(3))
    dmem = refs[3 * segments]
    refs = refs[3 * segments + 1 :]
    x, dq, dk, dv = (refs[segments * i : segments * (i + 1)] for i in range(4))
    keep, send, acc, vec_s, bup_s = refs[4 * segments :]
    step = pl.program_id(0)

    for w, right in enumerate((dq, dk, dv)):
        term = product_sum(x, right)

        @pl.when(step == 0)
        def _():
            acc[w] = term

        @pl.when(step > 0)
        def _():
            acc[w] += term

    @pl.when(step == pl.num_programs(0) - 1)
    def _():
        vat_sum = sum(v[...].sum(axis=0) for v in vat)
        vec_sum = sum(v[...].sum(axis=0) for v in vec)
        vec_s[...] = jnp.zeros_like(vec_s)
        vec_s[0:16, :] = dmem[...].sum(axis=0)
        vec_s[0:2, :] = vat_sum[0:2]
        vec_s[2:6, :] = vec_sum[0:4]
        vec_s[16:18, :] = vec_sum[4:6]
        bup_s[...] = sum(v[...].sum(axis=0) for v in vup)
        width = acc.shape[2]
        blank = jnp.zeros((8, width - 512), F32)

        def turned(array, shift):
            return array if shift == 0 else pltpu.roll(array, array.shape[1] - shift, 1)

        def value_of(*at):
            idx = spot(*at)
            rows = [acc[w, UNIT * idx : UNIT * (idx + 1), :] for w in range(3)]
            vectors = turned(vec_s[...], UNIT * idx)[:, :128]
            hidden = turned(jnp.broadcast_to(bup_s[...], (8, bup_s.shape[1])), 4 * UNIT * idx)[:, :128]
            tail = jnp.concatenate([vectors[0:8], vectors[8:16], vectors[16:24], hidden, blank], axis=1)
            return jnp.concatenate(rows + [tail], axis=0).astype(BF16)

        emit_units(me, keep, send, value_of)


def call_product_up(me, o, db, h, du):
    segments = len(o)
    items, rows, width = o[0].shape
    ff = du[0].shape[2]
    steps = ff // width
    fixed = [pl.BlockSpec((items, rows, width), lambda j, m: (0, 0, 0), pipeline_mode=pl.Buffered(1))] * (3 * segments)
    moving = [pl.BlockSpec((items, rows, width), lambda j, m: (0, 0, jnp.maximum(j - 1, 0)))] * segments
    dims = (4, 2, 2, steps + 1, UNIT, width)
    out = pl.BlockSpec((4, 2, 2, 1, UNIT, width), lambda j, m: (0, 0, 0, j, 0, 0))
    return pl.pallas_call(
        functools.partial(product_up, segments),
        grid_spec=pltpu.PrefetchScalarGridSpec(
            num_scalar_prefetch=1,
            grid=(steps + 1,),
            in_specs=fixed + moving,
            out_specs=[out, out],
            scratch_shapes=[pltpu.VMEM((width, width), F32)],
        ),
        out_shape=[jax.ShapeDtypeStruct(dims, BF16)] * 2,
        compiler_params=params(),
        cost_estimate=pl.CostEstimate(flops=2 * segments * items * rows * width * (ff + width), bytes_accessed=2 * segments * items * rows * (ff + 3 * width) + 2 * width * (ff + width), transcendentals=0),
        name="product_up",
    )(me, *o, *db, *h, *du)


def call_product_down(me, a, df):
    segments = len(a)
    items, rows, width = df[0].shape
    ff = a[0].shape[2]
    moving = [pl.BlockSpec((items, rows, ff // 4), lambda j, m: (0, 0, j ^ m[0]))] * segments
    fixed = [pl.BlockSpec((items, rows, width), lambda j, m: (0, 0, 0), pipeline_mode=pl.Buffered(1))] * segments
    dims = (4, 2, 2, 4 * UNIT, width)
    out = pl.BlockSpec((1, 2, 2, 4 * UNIT, width), lambda j, m: (j, 0, 0, 0, 0))
    return pl.pallas_call(
        functools.partial(product_down, segments),
        grid_spec=pltpu.PrefetchScalarGridSpec(
            num_scalar_prefetch=1,
            grid=(4,),
            in_specs=moving + fixed,
            out_specs=[out, out],
            scratch_shapes=[pltpu.VMEM((ff // 4, width), F32)],
        ),
        out_shape=[jax.ShapeDtypeStruct(dims, BF16)] * 2,
        compiler_params=params(),
        cost_estimate=pl.CostEstimate(flops=2 * segments * items * rows * width * ff, bytes_accessed=2 * segments * items * rows * (ff + width) + 2 * width * ff, transcendentals=0),
        name="product_down",
    )(me, *a, *df)


def call_product_first(me, vat, vec, vup, dmem, x, dq, dk, dv):
    segments = len(x)
    items, rows, width = x[0].shape
    fixed = (*vat, *vec, *vup, dmem)
    moving = [pl.BlockSpec((1, rows, width), lambda j, m: (j, 0, 0))] * (4 * segments)
    tall = 3 * UNIT + 8
    dims = (4, 2, 2, tall, width)
    out = pl.BlockSpec(dims, lambda j, m: (0,) * 5, pipeline_mode=pl.Buffered(1))
    return pl.pallas_call(
        functools.partial(product_first, segments),
        grid_spec=pltpu.PrefetchScalarGridSpec(
            num_scalar_prefetch=1,
            grid=(items,),
            in_specs=[whole(a) for a in fixed] + moving,
            out_specs=[out, out],
            scratch_shapes=[
                pltpu.VMEM((3, width, width), F32),
                pltpu.VMEM((24, width), F32),
                pltpu.VMEM(vup[0].shape[1:], F32),
            ],
        ),
        out_shape=[jax.ShapeDtypeStruct(dims, BF16)] * 2,
        compiler_params=params(),
        cost_estimate=pl.CostEstimate(flops=6 * segments * items * rows * width * width, bytes_accessed=8 * segments * items * rows * width + 6 * width * width, transcendentals=0),
        name="product_first",
    )(me, *fixed, *x, *dq, *dk, *dv)


def shown(array):
    return lax.optimization_barrier(array.transpose(0, 2, 1, 3))


def gather_weights(me, shards):
    mem, wq, wk, wv, wo, wup, wdown, bq, bv, bo, bup, bdown, g1, s1, g2, s2 = shards
    width = wq.shape[1]
    ff = wup.shape[1]
    vec = jnp.concatenate([jnp.stack([bq, bv, bo, bdown, g1, s1]), mem.T, jnp.stack([g2, s2])], axis=0)
    vec = jnp.pad(vec, ((0, 6), (0, 128 - UNIT))).astype(F32)
    hidden = jnp.pad(bup[None], ((0, 0), (0, 128 - 4 * UNIT))).astype(F32)
    up_blocks = wup.reshape(UNIT, ff // width, width).transpose(1, 0, 2)
    units = jnp.concatenate([wo[None], up_blocks, wdown.reshape(4, UNIT, width)], axis=0)
    units = lax.all_gather(units, AXES, axis=0)
    first = gather_core(gather_far(*gather_near(*gather_z(call_pack_first(wq, wk, wv, vec, hidden)))))
    square = ((width, width), BF16)
    wq, wk, wv, vec, bup = call_assemble(
        assemble_first, me, first, [square] * 3 + [((1, 24, width), F32), ((1, ff), F32)],
        "assemble_first", [pltpu.VMEM((width // UNIT, 32, 128), F32)],
    )
    return (wq, wk, wv, vec, bup), units


def gather_plain(shards):
    mem, wq, wk, wv, wo, wup, wdown, bq, bv, bo, bup, bdown, g1, s1, g2, s2 = [
        lax.all_gather(a, AXES, axis=0, tiled=True) for a in shards
    ]
    rows = [bq, bv, bo, bdown, g1, s1, mem.T, g2, s2]
    vectors = jnp.concatenate([r.reshape(-1, wq.shape[1]) for r in rows], axis=0).astype(F32)
    vectors = jnp.pad(vectors, ((0, 6), (0, 0)))[None]
    return (wq, wk, wv, vectors, bup.astype(F32)[None, :]), (wo, wup, wdown)


def reduce_plain(pieces, vat, vec, vup, dmem):
    x, o, db, h, du, a, df, dq, dk, dv = pieces
    vat = sum(v.sum(axis=0) for v in vat)
    vec = sum(v.sum(axis=0) for v in vec)
    gq = call_weight_product(x, dq, 768, 256, F32)
    gk = call_weight_product(x, dk, 768, 256, F32)
    gv = call_weight_product(x, dv, 768, 256, F32)
    go = call_weight_product(o, db, 768, 256, F32)
    gup = call_weight_product(h, du, 768, 256, F32)
    gdown = call_weight_product(a, df, 256, 768, F32)
    terms = (dmem.sum(axis=0)[6:16].T, gq, gk, gv, go, gup, gdown, sum(v.sum(axis=(0, 1)) for v in vup))
    terms += (vat[0], vat[1]) + tuple(vec[i] for i in range(6))
    owned = lax.psum_scatter(terms, AXES, scatter_dimension=0, tiled=True)
    mem, gq, gk, gv, go, gup, gdown, bup, bq, bv, bo, bdown, g1, s1, g2, s2 = owned
    return mem, gq, gk, gv, go, gup, gdown, bq, bv, bo, bup, bdown, g1, s1, g2, s2


def local(*args):
    tokens, segment_count = args[:2]
    shards = args[2:18]
    cotangent, memory_cotangent = args[18:]
    items, segments, seg, width = tokens.shape
    pad = 16 - shards[0].shape[1]
    planned = lax.axis_size("dp") == 16 and lax.axis_size("shard") == 2
    me = coordinates()
    gathered = gather_weights(me, shards) if planned else gather_plain(shards)
    (wq, wk, wv, vec, bup), rest = gathered
    mem = vec
    saved = []
    y = None
    for s in range(segments):
        part = call_attend_forward(s, tokens, mem, wq, wk, wv, vec)
        if s == 0:
            if planned:
                rest = call_assemble_rest(after(rest, part[0]), 4 * width)
            wo, wup, wdown = rest
        o = part[5]
        y, mem, *more = call_feed_forward(s, segment_count, tokens, mem, o, wo, wup, wdown, vec, bup, y)
        saved.append((*part, *more))
    memory_final = mem[:, pad:].astype(BF16)
    dmem = jnp.pad(memory_cotangent.astype(F32), ((0, 0), (pad, 0), (0, 0)))
    tg = None
    pieces = [None] * segments
    vecs, vups, vats = [], [], []
    for s in reversed(range(segments)):
        x, q, k, v, e, o, li, xh1, sc1, h, a, gp, xh2, sc2 = saved[s]
        df, du, dr, db, vec_s, vup_s = call_feed_backward(
            s, segment_count, cotangent, dmem, xh2, sc2, gp, xh1, sc1, wup, wdown, vec
        )
        pieces[s] = (x, o, db, h, du, a, df)
        vecs.append(vec_s)
        vups.append(vup_s)
        into = {} if tg is None else {0: tg}
        back = functools.partial(call_attend_backward, s, segments, seg)
        tail = (q, k, v, e, o, li, wo, wq, wk, wv)
        if s > 0 or not planned:
            tg, dmem, dq, dk, dv, vat_s = back(segment_count, dmem, dr, db, *tail, into=into)
        else:
            o_all, db_all, h_all, du_all, a_all, df_all = list(zip(*pieces))[1:]
            down = call_weight_product(a_all, df_all, 768, 768, BF16)
            o_all = (after(o_all[0], down),) + tuple(o_all[1:])
            down = lax.psum_scatter(down, AXES, scatter_dimension=0, tiled=True).astype(F32)
            up = reduce_core(*call_product_up(me, o_all, db_all, h_all, du_all))
            gate = up[0]
            up_far = reduce_far(*up)
            part = back(segment_count, dmem, after(dr, *gate), db, *tail, first=0, many=1, into=into)
            for item in range(1, items):
                part = back(
                    segment_count, dmem, after(dr, part[1], *up_far[0]), db, *tail,
                    first=item, many=1, into=dict(enumerate(part)),
                )
            tg, dmem, dq, dk, dv, vat_s = part
            up_near = reduce_near(*up_far)
        pieces[s] += (dq, dk, dv)
        vats.append(vat_s)
    pieces = tuple(zip(*pieces))
    if planned:
        x, dq, dk, dv = pieces[0], *pieces[7:]
        x = (after(x[0], *up_near[0]),) + x[1:]
        first = reduce_core(*call_product_first(me, vats, vecs, vups, dmem, x, dq, dk, dv))
        up = reduce_z(*up_near)
        y = shown(after(y, *first[0]))
        first = reduce_far(*first)
        tg = shown(after(tg, *first[0]))
        sends, held = reduce_near(*first)
        sends, y, tg = lax.optimization_barrier((sends, y, tg))
        first = reduce_z(sends, held)
        y, tg = y.transpose(0, 2, 1, 3), tg.transpose(0, 2, 1, 3)
        gq, gk, gv = [first[UNIT * w : UNIT * (w + 1)] for w in range(3)]
        tail = first[3 * UNIT :]
        per = jnp.concatenate([tail[:, 128 * c : 128 * c + UNIT] for c in range(3)], axis=0)
        bq, bv, bo, bdown, g1, s1 = [per[i] for i in range(6)]
        owned = (
            per[6:16].T, gq, gk, gv, up[0], up[1:].transpose(1, 0, 2).reshape(UNIT, -1), down, bq, bv, bo,
            tail[0, 384 : 384 + 4 * UNIT], bdown, g1, s1, per[16], per[17],
        )
    else:
        owned = reduce_plain(pieces, vats, vecs, vups, dmem)
    return (y, memory_final, tg) + tuple(owned)


def solution(mesh):
    rows = P(("dp", "shard"))
    return jax.shard_map(local, mesh=mesh, in_specs=(rows,) * 20, out_specs=(rows,) * 19, check_vma=False)
```

time: 549 us -> 461 us (0.84)
  Pallas kernels: 313 us -> 274 us
  starting transfers between devices: 65.7 us -> 30.4 us
  local copies, waits for them, and re-layouts: 45 us -> 26.3 us
  between operations: 2.03 us -> 14.8 us
  waiting for transfers between devices: 98.1 us -> 91.8 us
    ppermute x57 -> x27, starting transfers between devices: 65.7 us -> 30.3 us  [swap(): return lax.ppermute(array, AXES, pairs)]
    pallas_call x9 -> x12, Pallas kernels: 259 us -> 230 us  [the longest x9 205 us: launch(): pl.pallas_call(run if into else body, grid=grid, in_specs=list(in_specs)...]
    ppermute x57 -> x27, waiting for transfers between devices: 98.1 us -> 74.5 us  [swap(): return lax.ppermute(array, AXES, pairs)]
    all_gather x0 -> x1, waiting for transfers between devices: none -> 17.2 us  [gather_weights(): units = lax.all_gather(units, AXES, axis=0)]
    pallas_call x3 -> x1, Pallas kernels: 15.4 us -> 5.07 us  [call_assemble(): pl.pallas_call(body, in_specs=[SCALARS] + [vm] * 8, out_specs=[vm] * len(...]
    slice x29 -> x3, local copies, waits for them, and re-layouts: 10.5 us -> 2.4 us  [the longest x2 2.4 us: reduce_far(): got[:2, :, 0].astype(F32)]
    concatenate x5 -> x2, local copies, waits for them, and re-layouts: 7.08 us -> 1.06 us  [the longest x1 0.87 us: gather_weights(): jnp.concatenate([wo[None], up_blocks, wdown.reshape(4, UNIT, width)], axi...]
    unnamed x76 -> x49, local copies, waits for them, and re-layouts: 19.7 us -> 14.6 us
  transfers between devices with their start and end apart: 57 -> 29, of which waited for: 21 -> 12; matrix products, arithmetic and copies ran while one was open for 8% -> 8% of each run, Pallas kernels for 14% -> 18%
where the time goes in v3:
time: 461 us; the launch traced here: 453 us
  Pallas kernels  274 us (59%)
  waiting for transfers between devices  91.8 us (20%)
  starting transfers between devices  30.4 us (7%)
  local copies, waits for them, and re-layouts  26.3 us (6%)
  other arithmetic  16 us (3%)
  between operations  14.8 us (3%)
    pallas_call x9, Pallas kernels, launch(): pl.pallas_call(run if into else body, grid=grid, in_specs=list(in_specs)...  205 us
    ppermute x27, waiting for transfers between devices, swap(): return lax.ppermute(array, AXES, pairs)  74.5 us
    ppermute x27, starting transfers between devices, swap(): return lax.ppermute(array, AXES, pairs)  30.3 us
    pallas_call x1, Pallas kernels, call_product_up(): pl.pallas_call(functools.partial(product_up, segments), grid_spec=pltpu.P...  20.9 us
    pallas_call x1, Pallas kernels, call_product_first(): pl.pallas_call(functools.partial(product_first, segments), grid_spec=pltp...  18.2 us
    all_gather x1, waiting for transfers between devices, gather_weights(): units = lax.all_gather(units, AXES, axis=0)  17.2 us
    unnamed x49, local copies, waits for them, and re-layouts  14.6 us
    pallas_call x1, Pallas kernels, call_weight_product(): pl.pallas_call(functools.partial(weight_product, parts), grid=(n_left //...  14.6 us
  transfers between devices with their start and end apart: 29, of which 12 were waited for; matrix products, arithmetic and copies ran while one was open for 8% of the time, Pallas kernels for 18%

profile of v3, /device:TPU:0, one launch (start us, length us, event | category | flops | bytes accessed | tf_op | source)
XLA Modules:
  0.0 453.0 jit_solution(2704183866354700505)
XLA Ops:
  12.9 1.5 pack_first.1
  14.3 3.0 collective-permute-start
  17.4 2.5 collective-permute-start.4
  21.8 1.7 collective-permute-start.1
  23.6 3.4 collective-permute-done.4
  27.0 10.8 %collective-permute-done.3 = bf16[80,768]{1,0:T(8,128)(2,1)S(1)} collective-permute-done((bf16[80,768]{1,0:T(8,128)(2,1)}, bf16[80,768]{1,0:T(8,128)(2,1)S(1)}, u32[]{:S(2)}, u32[]{:S(2)}) %collective-permute-start.3) | collective-permute-done | bytes 122912 | tf_op jit(solution)/shard_map/ppermute | solution.py:424
  37.8 1.6 collective-permute-start.5
  39.4 1.7 pad_maximum_fusion.1.refs_0_
  41.7 5.2 %collective-permute-done.5 = bf16[2,80,768]{2,1,0:T(8,128)(2,1)S(1)} collective-permute-done((bf16[2,80,768]{2,1,0:T(8,128)(2,1)S(1)}, bf16[2,80,768]{2,1,0:T(8,128)(2,1)S(1)}, u32[]{:S(2)}, u32[]{:S(2)}) %collective-permute-start.5) | collective-permute-done | bytes 245792 | tf_op jit(solution)/shard_map/ppermute | solution.py:424
  47.7 1.3 collective-permute-start.6
  49.5 13.0 %collective-permute-done.2.refs_1_ = bf16[4,80,768]{2,1,0:T(8,128)(2,1)} collective-permute-done((bf16[4,80,768]{2,1,0:T(8,128)(2,1)}, bf16[4,80,768]{2,1,0:T(8,128)(2,1)}, u32[]{:S(2)}, u32[]{:S(2)}) %collective-permute-start.2) | collective-permute-done | bytes 491552 | tf_op jit(solution)/shard_map/ppermute | solution.py:424
  63.1 2.1 copy.156.tok.refs_1_
  66.1 2.1 copy.157.refs_1_
  69.4 5.1 %assemble_first.1 = (bf16[768,768]{1,0:T(8,128)(2,1)}, bf16[768,768]{1,0:T(8,128)(2,1)}, bf16[768,768]{1,0:T(8,128)(2,1)}, f32[1,24,768]{2,1,0:T(8,128)}, f32[1,3072]{1,0:T(1,128)}) custom-call(s32[4]{0:T(128)} %pad_add_fusion.me, bf16[4,80,768]{2,1,0:T(8,128)(2,1)} %pad_maximum_fusion.1.refs_0_, bf16[4,80,768]{2,1,0:T(8,128)(2,1)} %collective-permute-done.2.refs_1_, ...), custom_call_target="tpu_custom_call" | custom-call | tf_op jit(solution)/shard_map/assemble_first/pallas_call | solution.py:578
  74.5 19.2 %attend_forward.2 = (bf16[2,512,768]{2,1,0:T(8,128)(2,1)}, bf16[2,512,768]{2,1,0:T(8,128)(2,1)}, bf16[2,512,768]{2,1,0:T(8,128)(2,1)}, bf16[2,512,768]{2,1,0:T(8...) custom-call(bf16[2,2,502,768]{3,2,1,0:T(8,128)(2,1)} %copy.156.tok.refs_1_, ...), custom_call_target="tpu_custom_call" | custom-call | flops 10066329600 | bytes 23592960 | tf_op jit(solution)/shard_map/attend_forward/pallas_call | solution.py:289
  93.7 17.2 %all-gather.3.cloned.1.call-done = bf16[288,24,768]{2,1,0:T(8,128)(2,1)} async-done(((bf16[9,24,768]{2,1,0:T(8,128)(2,1)}), bf16[288,24,768]{2,1,0:T(8,128)(2,1)}) %all-gather.3.cloned.1.call-update) | async-done | bytes 10616848 | tf_op jit(solution)/shard_map/all_gather | solution.py:784
  110.9 8.2 %assemble_rest.1 = (bf16[768,768]{1,0:T(8,128)(2,1)}, bf16[768,3072]{1,0:T(8,128)(2,1)}, bf16[3072,768]{1,0:T(8,128)(2,1)}) custom-call(bf16[32,9,24,768]{3,2,1,0:T(8,128)(2,1)} %bitcast.134), custom_call_target="tpu_custom_call" | custom-call | tf_op jit(solution)/shard_map/assemble_rest/pallas_call | solution.py:555
  119.1 29.5 %feed_forward.2 = (bf16[2,2,502,768]{3,2,1,0:T(8,128)(2,1)}, f32[2,16,768]{2,1,0:T(8,128)}, bf16[2,512,768]{2,1,0:T(8,128)(2,1)}, f32[2,512,128]{2,1,0:T(8,128)}...) custom-call(s32[2]{0:T(128)} %refs_0_.13, ...), custom_call_target="tpu_custom_call" | custom-call | flops 10871635968 | bytes 23592960 | tf_op jit(solution)/shard_map/feed_forward/pallas_call | solution.py:289
  148.6 18.2 %attend_forward.3 = (bf16[2,512,768]{2,1,0:T(8,128)(2,1)}, bf16[2,512,768]{2,1,0:T(8,128)(2,1)}, bf16[2,512,768]{2,1,0:T(8,128)(2,1)}, bf16[2,512,768]{2,1,0:T(8...) custom-call(bf16[2,2,502,768]{3,2,1,0:T(8,128)(2,1)} %copy.156.tok.refs_1_, ...), custom_call_target="tpu_custom_call" | custom-call | flops 10066329600 | bytes 23592960 | tf_op jit(solution)/shard_map/attend_forward/pallas_call | solution.py:289
  166.8 29.3 %feed_forward.3 = (bf16[2,2,502,768]{3,2,1,0:T(8,128)(2,1)}, f32[2,16,768]{2,1,0:T(8,128)}, bf16[2,512,768]{2,1,0:T(8,128)(2,1)}, f32[2,512,128]{2,1,0:T(8,128)}...) custom-call(s32[2]{0:T(128)} %refs_0_.13, ...), custom_call_target="tpu_custom_call", output_to_operand_aliasing={{0}: (9, {})} | custom-call | flops 10871635968 | bytes 23592960 | tf_op jit(solution)/shard_map/feed_forward/pallas_call | solution.py:289
  196.2 22.3 %feed_backward.2 = (bf16[2,512,768]{2,1,0:T(8,128)(2,1)}, bf16[2,512,3072]{2,1,0:T(8,128)(2,1)}, f32[2,512,768]{2,1,0:T(8,128)}, bf16[2,512,768]{2,1,0:T(8,128)(...) custom-call(s32[2]{0:T(128)} %refs_0_.13, bf16[2,2,502,768]{3,2,1,0:T(8,128)(2,1)} %copy.157.refs_1_, ...), custom_call_target="tpu_custom_call" | custom-call | flops 9663676416 | bytes 23592960 | tf_op jit(solution)/shard_map/feed_backward/pallas_call | solution.py:289
  218.5 29.0 %attend_backward.3 = (bf16[2,2,502,768]{3,2,1,0:T(8,128)(2,1)}, f32[2,16,768]{2,1,0:T(8,128)}, bf16[2,512,768]{2,1,0:T(8,128)(2,1)}, bf16[2,512,768]{2,1,0:T(8,1...) custom-call(s32[2]{0:T(128)} %refs_0_.13, f32[2,16,768]{2,1,0:T(8,128)} %pad_convert_fusion.refs_2_.refs_1_, ...), custom_call_target="tpu_custom_call" | custom-call | flops 17716740096 | bytes 31457280 | tf_op jit(solution)/shard_map/attend_backward/pallas_call | solution.py:289
  247.5 22.1 %feed_backward.3 = (bf16[2,512,768]{2,1,0:T(8,128)(2,1)}, bf16[2,512,3072]{2,1,0:T(8,128)(2,1)}, f32[2,512,768]{2,1,0:T(8,128)}, bf16[2,512,768]{2,1,0:T(8,128)(...) custom-call(s32[2]{0:T(128)} %refs_0_.13, bf16[2,2,502,768]{3,2,1,0:T(8,128)(2,1)} %copy.157.refs_1_, ...), custom_call_target="tpu_custom_call" | custom-call | flops 9663676416 | bytes 23592960 | tf_op jit(solution)/shard_map/feed_backward/pallas_call | solution.py:289
  269.6 14.6 %weight_product.1 = bf16[3072,768]{1,0:T(8,128)(2,1)} custom-call(bf16[2,512,3072]{2,1,0:T(8,128)(2,1)} %get-tuple-element.139.refs_0_, bf16[2,512,3072]{2,1,0:T(8,128)(2,1)} %get-tuple-element.140.refs_1_, bf16[2,512,768]{2,1,0:T(8,128)(2,1)} %get-tuple-element.141.refs_2_, bf16[2,512,768]{2,1,0:T(8,128)(2,1)} %get-tuple-element.142.refs_3_), custom_call_target="tpu_custom_call" | custom-call | flops 9663676416 | bytes 15728640 | tf_op jit(solution)/shard_map/weight_product/pallas_call | solution.py:396
  284.1 20.9 %product_up.1 = (bf16[4,2,2,5,24,768]{5,4,3,2,1,0:T(8,128)(2,1)}, bf16[4,2,2,5,24,768]{5,4,3,2,1,0:T(8,128)(2,1)}) custom-call(s32[4]{0:T(128)} %pad_add_fusion.me, bf16[2,512,768]{2,1,0:T(8,128)(2,1)} %get-tuple-element.143.refs_3_.refs_0_.refs_8_, bf16[2,512,768]{2,1,0:T(8,128)(2,1)} %get-tuple-element.117.refs_3_.refs_8_.refs_1_, ...), custom_call_target="tpu_custom_call" | custom-call | flops 12079595520 | bytes 27918336 | tf_op jit(solution)/shard_map/product_up/pallas_call | solution.py:703
  305.5 5.4 %collective-permute-done.11 = bf16[4,2,2,5,24,768]{5,4,3,2,1,0:T(8,128)(2,1)} collective-permute-done((bf16[4,2,2,5,24,768]{5,4,3,2,1,0:T(8,128)(2,1)}, bf16[4,2,2,5,24,768]{5,4,3,2,1,0:T(8,128)(2,1)}, u32[]{:S(2)}, u32[]{:S(2)}) %collective-permute-start.11) | collective-permute-done | bytes 2949152 | tf_op jit(solution)/shard_map/ppermute | solution.py:424
  310.9 2.2 fusion.1
  313.1 1.5 collective-permute-start.13
  314.6 2.3 fusion.23
  318.5 17.9 %attend_backward.4 = (bf16[2,2,502,768]{3,2,1,0:T(8,128)(2,1)}, f32[2,16,768]{2,1,0:T(8,128)}, bf16[2,512,768]{2,1,0:T(8,128)(2,1)}, bf16[2,512,768]{2,1,0:T(8,1...) custom-call(s32[2]{0:T(128)} %refs_0_.13, ...), custom_call_target="tpu_custom_call", output_to_operand_aliasing={{0}: (14, {})} | custom-call | flops 8858370048 | bytes 15728640 | tf_op jit(solution)/shard_map/attend_backward/pallas_call | solution.py:289
  336.4 1.9 bitcast_add_fusion
  339.1 1.5 collective-permute-start.15
  340.6 1.4 bitcast_add_fusion.1
  342.6 17.8 %attend_backward.5 = (bf16[2,2,502,768]{3,2,1,0:T(8,128)(2,1)}, f32[2,16,768]{2,1,0:T(8,128)}, bf16[2,512,768]{2,1,0:T(8,128)(2,1)}, bf16[2,512,768]{2,1,0:T(8,1...) custom-call(s32[2]{0:T(128)} %refs_0_.13, ...), custom_call_target="tpu_custom_call", output_to_operand_aliasing={{0}: (14, {}), {1}: (15, {}), {2}: (16, {}), {3}: (17, {}),... | custom-call | flops 8858370048 | bytes 15728640 | tf_op jit(solution)/shard_map/attend_backward/pallas_call | solution.py:289
  360.6 18.2 %product_first.1 = (bf16[4,2,2,80,768]{4,3,2,1,0:T(8,128)(2,1)}, bf16[4,2,2,80,768]{4,3,2,1,0:T(8,128)(2,1)}) custom-call(s32[4]{0:T(128)} %pad_add_fusion.me, f32[2,8,768]{2,1,0:T(8,128)} %get-tuple-element.131.refs_0_, f32[2,8,768]{2,1,0:T(8,128)} %get-tuple-element.165.refs_1_, f32[2,8,768]{2,1,0:T(8,128)} %get-tuple-element.166.refs_2_, ...), custom_call_target="tpu_custom_call" | custom-call | flops 7247757312 | bytes 16121856 | tf_op jit(solution)/shard_map/product_first/pallas_call | solution.py:751
  379.0 1.9 collective-permute-start.26
  381.8 1.6 collective-permute-start.24
  384.1 6.2 %collective-permute-done.26 = bf16[5,24,768]{2,1,0:T(8,128)(2,1)S(1)} collective-permute-done((bf16[5,24,768]{2,1,0:T(8,128)(2,1)S(1)}, bf16[5,24,768]{2,1,0:T(8,128)(2,1)S(1)}, u32[]{:S(2)}, u32[]{:S(2)}) %collective-permute-start.26) | collective-permute-done | bytes 184352 | tf_op jit(solution)/shard_map/ppermute | solution.py:424
  390.3 13.0 %collective-permute-done.25 = bf16[5,24,768]{2,1,0:T(8,128)(2,1)S(1)} collective-permute-done((bf16[5,24,768]{2,1,0:T(8,128)(2,1)S(1)}, bf16[5,24,768]{2,1,0:T(8,128)(2,1)S(1)}, u32[]{:S(2)}, u32[]{:S(2)}) %collective-permute-start.25) | collective-permute-done | bytes 184352 | tf_op jit(solution)/shard_map/ppermute | solution.py:424
  404.3 1.5 collective-permute-start.19
  407.3 10.7 %collective-permute-done.19 = bf16[2,2,80,768]{3,2,1,0:T(8,128)(2,1)S(1)} collective-permute-done((bf16[2,2,80,768]{3,2,1,0:T(8,128)(2,1)S(1)}, bf16[2,2,80,768]{3,2,1,0:T(8,128)(2,1)S(1)}, u32[]{:S(2)}, u32[]{:S(2)}) %collective-permute-start.19) | collective-permute-done | bytes 491552 | tf_op jit(solution)/shard_map/ppermute | solution.py:424
  418.2 1.5 collective-permute-start.20
  420.8 5.0 %collective-permute-done.20 = bf16[2,80,768]{2,1,0:T(8,128)(2,1)S(1)} collective-permute-done((bf16[2,80,768]{2,1,0:T(8,128)(2,1)S(1)}, bf16[2,80,768]{2,1,0:T(8,128)(2,1)S(1)}, u32[]{:S(2)}, u32[]{:S(2)}) %collective-permute-start.20) | collective-permute-done | bytes 245792 | tf_op jit(solution)/shard_map/ppermute | solution.py:424
  428.8 2.2 collective-permute-start.22
  431.0 2.2 collective-permute-start.23
  433.8 1.6 convert_element_type.237
  435.4 4.0 copy.174
  439.5 4.0 copy.176
  (123 shorter events, 26.9 us)
Async XLA Ops:
  7.2 4.3 copy-start.19
  7.2 4.3 copy-start.18
  7.2 4.3 copy-start.17
  7.2 4.3 copy-start.16
  7.2 4.3 copy-start.15
  7.2 4.3 copy-start.14
  7.3 4.3 copy-start.13
  7.3 4.3 copy-start.12
  7.3 4.3 copy-start.11
  7.3 4.5 copy-start.20
  7.3 103.6 %all-gather.3.cloned.1.call-start = ((), (), s32[]{:S(2)}) async-start(), calls=%async_computation.2 | async-start | bytes 10948608 | tf_op jit(solution)/shard_map/all_gather | solution.py:784
  11.4 51.7 %copy-start.9 = (bf16[2,10,768]{2,0,1:T(2,128)(2,1)S(1)}, bf16[2,10,768]{2,0,1:T(2,128)(2,1)}, u32[]{:S(2)}) copy-start(bf16[2,10,768]{2,0,1:T(2,128)(2,1)} %param.39) | copy-start | bytes 92164
  11.4 51.7 %copy-start.2 = (bf16[2,2,502,768]{3,1,2,0:T(2,128)(2,1)S(1)}, bf16[2,2,502,768]{3,1,2,0:T(2,128)(2,1)}, u32[]{:S(2)}) copy-start(bf16[2,2,502,768]{3,1,2,0:T(2,128)(2,1)} %param.20) | copy-start | bytes 9252868
  11.4 422.4 %reduce-scatter.2.cloned.1.call-start = ((), (), s32[]{:S(2)}) async-start(), calls=%async_computation.1 | async-start | bytes 4866048 | tf_op jit(solution)/shard_map/reduce_scatter | solution.py:865
  14.3 6.6 %collective-permute-start = (bf16[80,768]{1,0:T(8,128)(2,1)}, bf16[80,768]{1,0:T(8,128)(2,1)S(1)}, u32[]{:S(2)}, u32[]{:S(2)}) collective-permute-start(bf16[80,768]{1,0:T(8,128)(2,1)} %pack_first.1), channel_id=1, source_target_pairs={{0,8},{1,9},{2,10},{3,11},{4,12},{5,13},{6,14},{7,15},{8,0},{9,1},... | collective-permute-start | bytes 368648 | tf_op jit(solution)/shard_map/ppermute | solution.py:424
  17.4 9.6 %collective-permute-start.4 = (bf16[80,768]{1,0:T(8,128)(2,1)}, bf16[80,768]{1,0:T(8,128)(2,1)S(1)}, u32[]{:S(2)}, u32[]{:S(2)}) collective-permute-start(bf16[80,768]{1,0:T(8,128)(2,1)} %pack_first.1), channel_id=1, source_target_pairs={{0,24},{1,25},{2,26},{3,27},{4,28},{5,29},{6,30},{7,31},{8,16},{9,... | collective-permute-start | bytes 368648 | tf_op jit(solution)/shard_map/ppermute | solution.py:424
  19.8 18.0 %collective-permute-start.3 = (bf16[80,768]{1,0:T(8,128)(2,1)}, bf16[80,768]{1,0:T(8,128)(2,1)S(1)}, u32[]{:S(2)}, u32[]{:S(2)}) collective-permute-start(bf16[80,768]{1,0:T(8,128)(2,1)} %pack_first.1), channel_id=1, source_target_pairs={{0,16},{1,17},{2,18},{3,19},{4,20},{5,21},{6,22},{7,23},{8,24},{9,... | collective-permute-start | bytes 368648 | tf_op jit(solution)/shard_map/ppermute | solution.py:424
  21.8 17.6 %collective-permute-start.1 = (bf16[2,80,768]{2,1,0:T(8,128)(2,1)S(1)}, bf16[2,80,768]{2,1,0:T(8,128)(2,1)S(1)}, u32[]{:S(2)}, u32[]{:S(2)}) collective-permute-start(bf16[2,80,768]{2,1,0:T(8,128)(2,1)S(1)} %pad_maximum_fusion.3), channel_id=1, source_target_pairs={{0,4},{1,5},{2,6},{3,7},{4,0},{5,1},{6,2},{7,3},{8,12},{9,13},{10,... | collective-permute-start | bytes 737288 | tf_op jit(solution)/shard_map/ppermute | solution.py:424
  37.8 9.1 %collective-permute-start.5 = (bf16[2,80,768]{2,1,0:T(8,128)(2,1)S(1)}, bf16[2,80,768]{2,1,0:T(8,128)(2,1)S(1)}, u32[]{:S(2)}, u32[]{:S(2)}) collective-permute-start(bf16[2,80,768]{2,1,0:T(8,128)(2,1)S(1)} %pad_maximum_fusion.4), channel_id=1, source_target_pairs={{0,1},{1,0},{2,3},{3,2},{4,5},{5,4},{6,7},{7,6},{8,9},{9,8},{10,11... | collective-permute-start | bytes 737288 | tf_op jit(solution)/shard_map/ppermute | solution.py:424
  41.1 21.5 %collective-permute-start.2 = (bf16[4,80,768]{2,1,0:T(8,128)(2,1)}, bf16[4,80,768]{2,1,0:T(8,128)(2,1)}, u32[]{:S(2)}, u32[]{:S(2)}) collective-permute-start(bf16[4,80,768]{2,1,0:T(8,128)(2,1)} %pad_maximum_fusion.1.refs_0_), channel_id=1, source_target_pairs={{0,1},{1,0},{2,3},{3,2},{4,5},{5,4},{6,7},{7,6},{8,9},{9,8},{10,11... | collective-permute-start | bytes 1474568 | tf_op jit(solution)/shard_map/ppermute | solution.py:424
  47.7 14.9 %collective-permute-start.6 = (bf16[4,80,768]{2,1,0:T(8,128)(2,1)}, bf16[4,80,768]{2,1,0:T(8,128)(2,1)}, u32[]{:S(2)}, u32[]{:S(2)}) collective-permute-start(bf16[4,80,768]{2,1,0:T(8,128)(2,1)} %pad_maximum_fusion.2.refs_2_), channel_id=1, source_target_pairs={{0,4},{1,5},{2,6},{3,7},{4,0},{5,1},{6,2},{7,3},{8,12},{9,13},{10,... | collective-permute-start | bytes 1474568 | tf_op jit(solution)/shard_map/ppermute | solution.py:424
  49.0 20.4 %collective-permute-start.7 = (bf16[4,80,768]{2,1,0:T(8,128)(2,1)}, bf16[4,80,768]{2,1,0:T(8,128)(2,1)}, u32[]{:S(2)}, u32[]{:S(2)}) collective-permute-start(bf16[4,80,768]{2,1,0:T(8,128)(2,1)} %pad_maximum_fusion.1.refs_0_), channel_id=1, source_target_pairs={{0,2},{1,3},{2,0},{3,1},{4,6},{5,7},{6,4},{7,5},{8,10},{9,11},{10,... | collective-permute-start | bytes 1474568 | tf_op jit(solution)/shard_map/ppermute | solution.py:424
  49.0 20.4 %collective-permute-start.9 = (bf16[4,80,768]{2,1,0:T(8,128)(2,1)}, bf16[4,80,768]{2,1,0:T(8,128)(2,1)}, u32[]{:S(2)}, u32[]{:S(2)}) collective-permute-start(bf16[4,80,768]{2,1,0:T(8,128)(2,1)} %pad_maximum_fusion.2.refs_2_), channel_id=1, source_target_pairs={{0,2},{1,3},{2,0},{3,1},{4,6},{5,7},{6,4},{7,5},{8,10},{9,11},{10,... | collective-permute-start | bytes 1474568 | tf_op jit(solution)/shard_map/ppermute | solution.py:424
  62.6 6.8 %collective-permute-start.8 = (bf16[4,80,768]{2,1,0:T(8,128)(2,1)}, bf16[4,80,768]{2,1,0:T(8,128)(2,1)}, u32[]{:S(2)}, u32[]{:S(2)}) collective-permute-start(bf16[4,80,768]{2,1,0:T(8,128)(2,1)} %collective-permute-done.2.refs_1_), channel_id=1, source_target_pairs={{0,2},{1,3},{2,0},{3,1},{4,6},{5,7},{6,4},{7,5},{8,10},{9,11},{10,... | collective-permute-start | bytes 1474568 | tf_op jit(solution)/shard_map/ppermute | solution.py:424
  62.6 6.8 %collective-permute-start.10 = (bf16[4,80,768]{2,1,0:T(8,128)(2,1)}, bf16[4,80,768]{2,1,0:T(8,128)(2,1)}, u32[]{:S(2)}, u32[]{:S(2)}) collective-permute-start(bf16[4,80,768]{2,1,0:T(8,128)(2,1)} %collective-permute-done.6.refs_3_), channel_id=1, source_target_pairs={{0,2},{1,3},{2,0},{3,1},{4,6},{5,7},{6,4},{7,5},{8,10},{9,11},{10,... | collective-permute-start | bytes 1474568 | tf_op jit(solution)/shard_map/ppermute | solution.py:424
  305.1 5.8 %copy-start.4 = (bf16[4,2,2,5,24,768]{5,4,3,2,1,0:T(8,128)(2,1)S(1)}, bf16[4,2,2,5,24,768]{5,4,3,2,1,0:T(8,128)(2,1)}, u32[]{:S(2)}) copy-start(bf16[4,2,2,5,24,768]{5,4,3,2,1,0:T(8,128)(2,1)} %get-tuple-element.149) | copy-start | bytes 8847364
  305.1 5.8 %collective-permute-start.11 = (bf16[4,2,2,5,24,768]{5,4,3,2,1,0:T(8,128)(2,1)}, bf16[4,2,2,5,24,768]{5,4,3,2,1,0:T(8,128)(2,1)}, u32[]{:S(2)}, u32[]{:S(2)}) collective-permute-start(bf16[4,2,2,5,24,768]{5,4,3,2,1,0:T(8,128)(2,1)} %get-tuple-element.150), channel_id=1, source_target_pairs={{0,2},{1,3},{2,0},{3,1},{4,6},{5,7},{6,4},{7,5},{8,10},{9,11},{10,... | collective-permute-start | bytes 8847368 | tf_op jit(solution)/shard_map/ppermute | solution.py:424
  313.1 23.3 %collective-permute-start.13 = (bf16[2,2,5,24,768]{4,3,2,1,0:T(8,128)(2,1)}, bf16[2,2,5,24,768]{4,3,2,1,0:T(8,128)(2,1)}, u32[]{:S(2)}, u32[]{:S(2)}) collective-permute-start(bf16[2,2,5,24,768]{4,3,2,1,0:T(8,128)(2,1)} %fusion.1), channel_id=1, source_target_pairs={{0,4},{1,5},{2,6},{3,7},{4,0},{5,1},{6,2},{7,3},{8,12},{9,13},{10,... | collective-permute-start | bytes 2211848 | tf_op jit(solution)/shard_map/ppermute | solution.py:424
  317.9 22.6 %collective-permute-start.12 = (bf16[2,2,5,24,768]{4,3,2,0,1:T(8,128)(2,1)}, bf16[2,2,5,24,768]{4,3,2,0,1:T(8,128)(2,1)S(1)}, u32[]{:S(2)}, u32[]{:S(2)}) collective-permute-start(bf16[2,2,5,24,768]{4,3,2,0,1:T(8,128)(2,1)} %fusion), channel_id=1, source_target_pairs={{0,1},{1,0},{2,3},{3,2},{4,5},{5,4},{6,7},{7,6},{8,9},{9,8},{10,11... | collective-permute-start | bytes 2211848 | tf_op jit(solution)/shard_map/ppermute | solution.py:424
  336.4 4.2 copy-start.5
  339.1 21.3 %collective-permute-start.15 = (bf16[2,5,24,768]{3,2,1,0:T(8,128)(2,1)}, bf16[2,5,24,768]{3,2,1,0:T(8,128)(2,1)S(1)}, u32[]{:S(2)}, u32[]{:S(2)}) collective-permute-start(bf16[2,5,24,768]{3,2,1,0:T(8,128)(2,1)} %fusion.11), channel_id=1, source_target_pairs={{0,1},{1,0},{2,3},{3,2},{4,5},{5,4},{6,7},{7,6},{8,9},{9,8},{10,11... | collective-permute-start | bytes 1105928 | tf_op jit(solution)/shard_map/ppermute | solution.py:424
  342.0 18.5 %collective-permute-start.14 = (bf16[2,5,24,768]{3,2,1,0:T(8,128)(2,1)S(1)}, bf16[2,5,24,768]{3,2,1,0:T(8,128)(2,1)S(1)}, u32[]{:S(2)}, u32[]{:S(2)}) collective-permute-start(bf16[2,5,24,768]{3,2,1,0:T(8,128)(2,1)S(1)} %fusion.10), channel_id=1, source_target_pairs={{0,4},{1,5},{2,6},{3,7},{4,0},{5,1},{6,2},{7,3},{8,12},{9,13},{10,... | collective-permute-start | bytes 1105928 | tf_op jit(solution)/shard_map/ppermute | solution.py:424
  360.6 22.8 %copy-start.10 = (f32[2,16,768]{2,1,0:T(8,128)S(1)}, f32[2,16,768]{2,1,0:T(8,128)}, u32[]{:S(2)}) copy-start(f32[2,16,768]{2,1,0:T(8,128)} %get-tuple-element.186) | copy-start | bytes 294916
  378.9 25.3 %copy-start.6 = (bf16[4,2,2,80,768]{4,3,2,1,0:T(8,128)(2,1)S(1)}, bf16[4,2,2,80,768]{4,3,2,1,0:T(8,128)(2,1)}, u32[]{:S(2)}) copy-start(bf16[4,2,2,80,768]{4,3,2,1,0:T(8,128)(2,1)} %get-tuple-element.179) | copy-start | bytes 5898244
  378.9 25.3 %collective-permute-start.16 = (bf16[4,2,2,80,768]{4,3,2,1,0:T(8,128)(2,1)}, bf16[4,2,2,80,768]{4,3,2,1,0:T(8,128)(2,1)S(1)}, u32[]{:S(2)}, u32[]{:S(2)}) collective-permute-start(bf16[4,2,2,80,768]{4,3,2,1,0:T(8,128)(2,1)} %get-tuple-element.180), channel_id=1, source_target_pairs={{0,2},{1,3},{2,0},{3,1},{4,6},{5,7},{6,4},{7,5},{8,10},{9,11},{10,... | collective-permute-start | bytes 5898248 | tf_op jit(solution)/shard_map/ppermute | solution.py:424
  379.0 11.3 %collective-permute-start.26 = (bf16[5,24,768]{2,1,0:T(8,128)(2,1)S(1)}, bf16[5,24,768]{2,1,0:T(8,128)(2,1)S(1)}, u32[]{:S(2)}, u32[]{:S(2)}) collective-permute-start(bf16[5,24,768]{2,1,0:T(8,128)(2,1)S(1)} %get-tuple-element.290), channel_id=1, source_target_pairs={{0,24},{1,25},{2,26},{3,27},{4,28},{5,29},{6,30},{7,31},{8,16},{9,... | collective-permute-start | bytes 552968 | tf_op jit(solution)/shard_map/ppermute | solution.py:424
  380.9 22.4 %collective-permute-start.25 = (bf16[5,24,768]{2,1,0:T(8,128)(2,1)S(1)}, bf16[5,24,768]{2,1,0:T(8,128)(2,1)S(1)}, u32[]{:S(2)}, u32[]{:S(2)}) collective-permute-start(bf16[5,24,768]{2,1,0:T(8,128)(2,1)S(1)} %get-tuple-element.291), channel_id=1, source_target_pairs={{0,16},{1,17},{2,18},{3,19},{4,20},{5,21},{6,22},{7,23},{8,24},{9,... | collective-permute-start | bytes 552968 | tf_op jit(solution)/shard_map/ppermute | solution.py:424
  381.8 21.5 %collective-permute-start.24 = (bf16[5,24,768]{2,1,0:T(8,128)(2,1)S(1)}, bf16[5,24,768]{2,1,0:T(8,128)(2,1)S(1)}, u32[]{:S(2)}, u32[]{:S(2)}) collective-permute-start(bf16[5,24,768]{2,1,0:T(8,128)(2,1)S(1)} %fusion.20), channel_id=1, source_target_pairs={{0,8},{1,9},{2,10},{3,11},{4,12},{5,13},{6,14},{7,15},{8,0},{9,1},... | collective-permute-start | bytes 552968 | tf_op jit(solution)/shard_map/ppermute | solution.py:424
  404.3 13.7 %collective-permute-start.19 = (bf16[2,2,80,768]{3,2,1,0:T(8,128)(2,1)S(1)}, bf16[2,2,80,768]{3,2,1,0:T(8,128)(2,1)S(1)}, u32[]{:S(2)}, u32[]{:S(2)}) collective-permute-start(bf16[2,2,80,768]{3,2,1,0:T(8,128)(2,1)S(1)} %fusion.6), channel_id=1, source_target_pairs={{0,4},{1,5},{2,6},{3,7},{4,0},{5,1},{6,2},{7,3},{8,12},{9,13},{10,... | collective-permute-start | bytes 1474568 | tf_op jit(solution)/shard_map/ppermute | solution.py:424
  406.0 13.7 %collective-permute-start.17 = (bf16[2,2,80,768]{3,2,0,1:T(8,128)(2,1)S(1)}, bf16[2,2,80,768]{3,2,0,1:T(8,128)(2,1)S(1)}, u32[]{:S(2)}, u32[]{:S(2)}) collective-permute-start(bf16[2,2,80,768]{3,2,0,1:T(8,128)(2,1)S(1)} %fusion.5), channel_id=1, source_target_pairs={{0,1},{1,0},{2,3},{3,2},{4,5},{5,4},{6,7},{7,6},{8,9},{9,8},{10,11... | collective-permute-start | bytes 1474568 | tf_op jit(solution)/shard_map/ppermute | solution.py:424
  418.2 7.6 %collective-permute-start.20 = (bf16[2,80,768]{2,1,0:T(8,128)(2,1)S(1)}, bf16[2,80,768]{2,1,0:T(8,128)(2,1)S(1)}, u32[]{:S(2)}, u32[]{:S(2)}) collective-permute-start(bf16[2,80,768]{2,1,0:T(8,128)(2,1)S(1)} %fusion.16), channel_id=1, source_target_pairs={{0,1},{1,0},{2,3},{3,2},{4,5},{5,4},{6,7},{7,6},{8,9},{9,8},{10,11... | collective-permute-start | bytes 737288 | tf_op jit(solution)/shard_map/ppermute | solution.py:424
  419.9 15.5 %copy-start.1 = (bf16[2,2,502,768]{3,2,1,0:T(8,128)(2,1)S(1)}, bf16[2,2,502,768]{3,2,1,0:T(8,128)(2,1)}, u32[]{:S(2)}) copy-start(bf16[2,2,502,768]{3,2,1,0:T(8,128)(2,1)} %get-tuple-element.182) | copy-start | bytes 9252868
  419.9 7.3 %collective-permute-start.18 = (bf16[2,80,768]{2,1,0:T(8,128)(2,1)S(1)}, bf16[2,80,768]{2,1,0:T(8,128)(2,1)S(1)}, u32[]{:S(2)}, u32[]{:S(2)}) collective-permute-start(bf16[2,80,768]{2,1,0:T(8,128)(2,1)S(1)} %fusion.15), channel_id=1, source_target_pairs={{0,4},{1,5},{2,6},{3,7},{4,0},{5,1},{6,2},{7,3},{8,12},{9,13},{10,... | collective-permute-start | bytes 737288 | tf_op jit(solution)/shard_map/ppermute | solution.py:424
  428.7 14.7 %collective-permute-start.21 = (bf16[80,768]{1,0:T(8,128)(2,1)}, bf16[80,768]{1,0:T(8,128)(2,1)S(1)}, u32[]{:S(2)}, u32[]{:S(2)}) collective-permute-start(bf16[80,768]{1,0:T(8,128)(2,1)} %fusion.21), channel_id=1, source_target_pairs={{0,8},{1,9},{2,10},{3,11},{4,12},{5,13},{6,14},{7,15},{8,0},{9,1},... | collective-permute-start | bytes 368648 | tf_op jit(solution)/shard_map/ppermute | solution.py:424
  428.8 14.7 %collective-permute-start.22 = (bf16[80,768]{1,0:T(8,128)(2,1)}, bf16[80,768]{1,0:T(8,128)(2,1)S(1)}, u32[]{:S(2)}, u32[]{:S(2)}) collective-permute-start(bf16[80,768]{1,0:T(8,128)(2,1)} %get-tuple-element.189), channel_id=1, source_target_pairs={{0,16},{1,17},{2,18},{3,19},{4,20},{5,21},{6,22},{7,23},{8,24},{9,... | collective-permute-start | bytes 368648 | tf_op jit(solution)/shard_map/ppermute | solution.py:424
  431.0 12.5 %collective-permute-start.23 = (bf16[80,768]{1,0:T(8,128)(2,1)}, bf16[80,768]{1,0:T(8,128)(2,1)S(1)}, u32[]{:S(2)}, u32[]{:S(2)}) collective-permute-start(bf16[80,768]{1,0:T(8,128)(2,1)} %get-tuple-element.190), channel_id=1, source_target_pairs={{0,24},{1,25},{2,26},{3,27},{4,28},{5,29},{6,30},{7,31},{8,16},{9,... | collective-permute-start | bytes 368648 | tf_op jit(solution)/shard_map/ppermute | solution.py:424
  435.4 4.0 copy-start
  439.5 4.0 copy-start.8
  (2 other events, 3.8 us)
Sparse Core Ops, SparseCore 0:
  11.5 99.3 all-gather.2
  305.6 111.9 reduce-scatter.1

commit v4 on v3

--- a/solution.py
+++ b/solution.py
@@ -14,7 +14,6 @@
 NORM_EPS = 1e-06
 ROOT_HALF = 0.7071067811865476
 ROOT_TWO_PI = 0.3989422804014327
-VMEM_BYTES = 60 << 20
 
 
 def dot_nn(left, right):
@@ -206,21 +205,22 @@
         q2 = q[0, :, at]
         k2 = (k[0, :, at].astype(F32) * (count2 * 0.125)).astype(BF16)
         right = jnp.concatenate([v[0, :, at], ones], axis=1)
-        dq = dk = dv = None
+        d_turned = dop.T
+        q_turned = q2.T
+        dq = None
+        dk, dv = [], []
         for h in range(2):
             e_h = e[0, 2 * p + h]
-            d_h = dop * low_masks[h]
-            left = jnp.concatenate([d_h, pr * low_masks[h]], axis=1)
+            left = jnp.concatenate([dop * low_masks[h], pr * low_masks[h]], axis=1)
             ds = (e_h.astype(F32) * dot_nt(left, right)).astype(BF16)
             q_t = dot_nn(ds, k2 * low_masks[h])
-            k_t = dot_tn(ds, q2 * low_masks[h])
-            v_t = dot_tn(e_h, d_h)
             dq = q_t if dq is None else dq + q_t
-            dk = k_t if dk is None else dk + k_t
-            dv = v_t if dv is None else dv + v_t
+            own = slice(HEAD_DIM * h, HEAD_DIM * (h + 1))
+            dk.append(dot_nn(q_turned[own], ds))
+            dv.append(dot_nn(d_turned[own], e_h))
         dq_o[0, :, at] = dq.astype(BF16)
-        dk_o[0, :, at] = (dk * count2).astype(BF16)
-        dv_o[0, :, at] = (dv * count2).astype(BF16)
+        dk_o[0, :, at] = (jnp.concatenate(dk, axis=0).T * count2).astype(BF16)
+        dv_o[0, :, at] = (jnp.concatenate(dv, axis=0).T * count2).astype(BF16)
         return carry
 
     lax.fori_loop(0, HEADS // 2, pair, 0, unroll=True)
@@ -274,11 +274,11 @@
 SCALARS = pl.BlockSpec(memory_space=pltpu.SMEM)
 
 
-def params(**more):
-    return pltpu.CompilerParams(vmem_limit_bytes=VMEM_BYTES, **more)
-
-
-def launch(body, grid, args, in_specs, out_specs, out_shape, into=None, **more):
+def params(mib=60):
+    return pltpu.CompilerParams(vmem_limit_bytes=mib << 20)
+
+
+def launch(body, grid, args, in_specs, out_specs, out_shape, into=None, mib=60, **more):
     into = into or {}
     n_in = len(args)
     aliases = {n_in + k: o for k, o in enumerate(into)}
@@ -293,7 +293,7 @@
         out_specs=out_specs,
         out_shape=out_shape,
         input_output_aliases=aliases,
-        compiler_params=params(),
+        compiler_params=params(mib),
         **more,
     )(*args, *into.values())
 
@@ -458,17 +458,17 @@
     return (left.astype(F32) + right.astype(F32)).astype(BF16)
 
 
-def reduce_core(keep, send):
-    got = swap(send, 0, 0, 1, 0)
+def reduce_core(keep, send, *gate):
+    got = after(swap(send, 0, 0, 1, 0), *gate)
     send_a = add_low(keep[:2, :, 1], got[:2, :, 1])
     send_b = add_low(keep[2:, 1], got[2:, 1])
     return (send_a, send_b), (keep, got)
 
 
-def reduce_far(sends, held):
+def reduce_far(sends, held, *gate):
     keep, got = held
-    got_a = swap(sends[0], 0, 0, 0, 1)
-    got_b = swap(sends[1], 0, 1, 0, 0)
+    got_a = after(swap(sends[0], 0, 0, 0, 1), *gate)
+    got_b = after(swap(sends[1], 0, 1, 0, 0), *gate)
     a = keep[:2, :, 0].astype(F32) + got[:2, :, 0].astype(F32) + got_a.astype(F32)
     b = keep[2:, 0].astype(F32) + got[2:, 0].astype(F32) + got_b.astype(F32)
     return (a[:, 1].astype(BF16), b[:, 1].astype(BF16)), (a[:, 0], b[:, 0])
@@ -480,9 +480,9 @@
     return (a[1].astype(BF16), b[0].astype(BF16), b[1].astype(BF16)), a[0]
 
 
-def reduce_z(sends, held):
+def reduce_z(sends, held, *gate):
     for step, array in enumerate(sends):
-        held = held + swap(array, step + 1, 0, 0, 0).astype(F32)
+        held = held + after(swap(array, step + 1, 0, 0, 0), *gate).astype(F32)
     return held
 
 
@@ -673,18 +673,20 @@
         vec_s[0:2, :] = vat_sum[0:2]
         vec_s[2:6, :] = vec_sum[0:4]
         vec_s[16:18, :] = vec_sum[4:6]
-        bup_s[...] = sum(v[...].sum(axis=0) for v in vup)
+        bup_s[...] = jnp.broadcast_to(sum(v[...].sum(axis=0) for v in vup), bup_s.shape)
         width = acc.shape[2]
         blank = jnp.zeros((8, width - 512), F32)
 
-        def turned(array, shift):
-            return array if shift == 0 else pltpu.roll(array, array.shape[1] - shift, 1)
+        def window(ref, at):
+            low = min(at // 128 * 128, ref.shape[1] - 256)
+            two = ref[:, low : low + 256]
+            return (two if at == low else pltpu.roll(two, 256 - (at - low), 1))[:, :128]
 
         def value_of(*at):
             idx = spot(*at)
             rows = [acc[w, UNIT * idx : UNIT * (idx + 1), :] for w in range(3)]
-            vectors = turned(vec_s[...], UNIT * idx)[:, :128]
-            hidden = turned(jnp.broadcast_to(bup_s[...], (8, bup_s.shape[1])), 4 * UNIT * idx)[:, :128]
+            vectors = window(vec_s, UNIT * idx)
+            hidden = window(bup_s, 4 * UNIT * idx)
             tail = jnp.concatenate([vectors[0:8], vectors[8:16], vectors[16:24], hidden, blank], axis=1)
             return jnp.concatenate(rows + [tail], axis=0).astype(BF16)
 
@@ -758,7 +760,7 @@
             scratch_shapes=[
                 pltpu.VMEM((3, width, width), F32),
                 pltpu.VMEM((24, width), F32),
-                pltpu.VMEM(vup[0].shape[1:], F32),
+                pltpu.VMEM((8, vup[0].shape[2]), F32),
             ],
         ),
         out_shape=[jax.ShapeDtypeStruct(dims, BF16)] * 2,
@@ -772,7 +774,7 @@
     return lax.optimization_barrier(array.transpose(0, 2, 1, 3))
 
 
-def gather_weights(me, shards):
+def gather_weights(me, shards, *rows):
     mem, wq, wk, wv, wo, wup, wdown, bq, bv, bo, bup, bdown, g1, s1, g2, s2 = shards
     width = wq.shape[1]
     ff = wup.shape[1]
@@ -782,13 +784,17 @@
     up_blocks = wup.reshape(UNIT, ff // width, width).transpose(1, 0, 2)
     units = jnp.concatenate([wo[None], up_blocks, wdown.reshape(4, UNIT, width)], axis=0)
     units = lax.all_gather(units, AXES, axis=0)
-    first = gather_core(gather_far(*gather_near(*gather_z(call_pack_first(wq, wk, wv, vec, hidden)))))
+    a, b = gather_near(*gather_z(call_pack_first(wq, wk, wv, vec, hidden)))
+    rows = tuple(lax.optimization_barrier(after(r.transpose(0, 2, 1, 3), b).transpose(0, 2, 1, 3)) for r in rows)
+    far = gather_far(a, b)
+    *far, tokens, cotangent = lax.optimization_barrier((*far, *rows))
+    first = gather_core(tuple(far))
     square = ((width, width), BF16)
     wq, wk, wv, vec, bup = call_assemble(
         assemble_first, me, first, [square] * 3 + [((1, 24, width), F32), ((1, ff), F32)],
         "assemble_first", [pltpu.VMEM((width // UNIT, 32, 128), F32)],
     )
-    return (wq, wk, wv, vec, bup), units
+    return (wq, wk, wv, vec, bup), units, (tokens, cotangent)
 
 
 def gather_plain(shards):
@@ -826,8 +832,10 @@
     pad = 16 - shards[0].shape[1]
     planned = lax.axis_size("dp") == 16 and lax.axis_size("shard") == 2
     me = coordinates()
-    gathered = gather_weights(me, shards) if planned else gather_plain(shards)
-    (wq, wk, wv, vec, bup), rest = gathered
+    gathered = gather_weights(me, shards, tokens, cotangent) if planned else gather_plain(shards)
+    (wq, wk, wv, vec, bup), rest = gathered[:2]
+    if planned:
+        tokens, cotangent = gathered[2]
     mem = vec
     saved = []
     y = None
@@ -856,34 +864,28 @@
         into = {} if tg is None else {0: tg}
         back = functools.partial(call_attend_backward, s, segments, seg)
         tail = (q, k, v, e, o, li, wo, wq, wk, wv)
-        if s > 0 or not planned:
-            tg, dmem, dq, dk, dv, vat_s = back(segment_count, dmem, dr, db, *tail, into=into)
-        else:
+        if s == 0 and planned:
             o_all, db_all, h_all, du_all, a_all, df_all = list(zip(*pieces))[1:]
             down = call_weight_product(a_all, df_all, 768, 768, BF16)
             o_all = (after(o_all[0], down),) + tuple(o_all[1:])
             down = lax.psum_scatter(down, AXES, scatter_dimension=0, tiled=True).astype(F32)
-            up = reduce_core(*call_product_up(me, o_all, db_all, h_all, du_all))
-            gate = up[0]
-            up_far = reduce_far(*up)
-            part = back(segment_count, dmem, after(dr, *gate), db, *tail, first=0, many=1, into=into)
-            for item in range(1, items):
-                part = back(
-                    segment_count, dmem, after(dr, part[1], *up_far[0]), db, *tail,
-                    first=item, many=1, into=dict(enumerate(part)),
-                )
-            tg, dmem, dq, dk, dv, vat_s = part
-            up_near = reduce_near(*up_far)
+            keep_up, send_up = call_product_up(me, o_all, db_all, h_all, du_all)
+            up = reduce_core(keep_up, send_up)
+            dr = after(dr, *up[0])
+            up = reduce_far(*up)
+        tg, dmem, dq, dk, dv, vat_s = back(segment_count, dmem, dr, db, *tail, into=into)
         pieces[s] += (dq, dk, dv)
         vats.append(vat_s)
     pieces = tuple(zip(*pieces))
     if planned:
         x, dq, dk, dv = pieces[0], *pieces[7:]
-        x = (after(x[0], *up_near[0]),) + x[1:]
-        first = reduce_core(*call_product_first(me, vats, vecs, vups, dmem, x, dq, dk, dv))
-        up = reduce_z(*up_near)
+        x = (after(x[0], *up[0]),) + x[1:]
+        keep, send = call_product_first(me, vats, vecs, vups, dmem, x, dq, dk, dv)
+        up = reduce_near(*up)
+        first = reduce_core(keep, send)
         y = shown(after(y, *first[0]))
         first = reduce_far(*first)
+        up = reduce_z(*up, *first[0])
         tg = shown(after(tg, *first[0]))
         sends, held = reduce_near(*first)
         sends, y, tg = lax.optimization_barrier((sends, y, tg))

time: 461 us -> 450 us (0.976)
  Pallas kernels: 274 us -> 267 us
    ppermute x27, waiting for transfers between devices: 74.5 us -> 60.5 us  [swap(): return lax.ppermute(array, AXES, pairs)]
    reduce_scatter x1, waiting for transfers between devices: 0.01 us -> 8.12 us  [local(): lax.psum_scatter(down, AXES, scatter_dimension=0, tiled=True).astype(F32)]
    pallas_call x9 -> x8, Pallas kernels: 205 us -> 198 us  [launch(): pl.pallas_call(run if into else body, grid=grid, in_specs=list(in_specs)...]
    unnamed x49 -> x57, local copies, waits for them, and re-layouts: 14.6 us -> 15.4 us
  transfers between devices with their start and end apart: 29 -> 29, of which waited for: 12 -> 16; matrix products, arithmetic and copies ran while one was open for 8% -> 7% of each run, Pallas kernels for 18% -> 17%
where the time goes in v4:
time: 450 us; the launch traced here: 442 us
  Pallas kernels  267 us (59%)
  waiting for transfers between devices  88.7 us (20%)
  starting transfers between devices  30.6 us (7%)
  local copies, waits for them, and re-layouts  25.5 us (6%)
  between operations  15 us (3%)
  other arithmetic  14.9 us (3%)
    pallas_call x8, Pallas kernels, launch(): pl.pallas_call(run if into else body, grid=grid, in_specs=list(in_specs)...  198 us
    ppermute x27, waiting for transfers between devices, swap(): return lax.ppermute(array, AXES, pairs)  60.5 us
    ppermute x27, starting transfers between devices, swap(): return lax.ppermute(array, AXES, pairs)  30.5 us
    pallas_call x1, Pallas kernels, call_product_up(): pl.pallas_call(functools.partial(product_up, segments), grid_spec=pltpu.P...  20.7 us
    all_gather x1, waiting for transfers between devices, gather_weights(): units = lax.all_gather(units, AXES, axis=0)  20 us
    pallas_call x1, Pallas kernels, call_product_first(): pl.pallas_call(functools.partial(product_first, segments), grid_spec=pltp...  19.2 us
    unnamed x57, local copies, waits for them, and re-layouts  15.4 us
    pallas_call x1, Pallas kernels, call_weight_product(): pl.pallas_call(functools.partial(weight_product, parts), grid=(n_left //...  14.6 us
  transfers between devices with their start and end apart: 29, of which 16 were waited for; matrix products, arithmetic and copies ran while one was open for 7% of the time, Pallas kernels for 17%

profile of v4, /device:TPU:0, one launch (start us, length us, event | category | flops | bytes accessed | tf_op | source)
XLA Modules:
  0.0 441.6 jit_solution(16265944047553979498)
XLA Ops:
  12.9 1.5 pack_first.1
  14.4 3.0 collective-permute-start
  17.4 2.5 collective-permute-start.4
  21.9 1.7 collective-permute-start.1
  23.6 3.4 collective-permute-done.4
  27.0 10.8 %collective-permute-done.3 = bf16[80,768]{1,0:T(8,128)(2,1)S(1)} collective-permute-done((bf16[80,768]{1,0:T(8,128)(2,1)}, bf16[80,768]{1,0:T(8,128)(2,1)S(1)}, u32[]{:S(2)}, u32[]{:S(2)}) %collective-permute-start.3) | collective-permute-done | bytes 122912 | tf_op jit(solution)/shard_map/ppermute | solution.py:424
  37.9 1.6 collective-permute-start.5
  39.4 1.7 pad_maximum_fusion.1.refs_0_
  41.7 5.2 %collective-permute-done.5 = bf16[2,80,768]{2,1,0:T(8,128)(2,1)S(1)} collective-permute-done((bf16[2,80,768]{2,1,0:T(8,128)(2,1)S(1)}, bf16[2,80,768]{2,1,0:T(8,128)(2,1)S(1)}, u32[]{:S(2)}, u32[]{:S(2)}) %collective-permute-start.5) | collective-permute-done | bytes 245792 | tf_op jit(solution)/shard_map/ppermute | solution.py:424
  47.7 1.3 collective-permute-start.6
  49.1 2.1 copy.182
  51.1 2.1 copy.181
  53.2 9.4 %collective-permute-done.2.refs_1_ = bf16[4,80,768]{2,1,0:T(8,128)(2,1)} collective-permute-done((bf16[4,80,768]{2,1,0:T(8,128)(2,1)}, bf16[4,80,768]{2,1,0:T(8,128)(2,1)}, u32[]{:S(2)}, u32[]{:S(2)}) %collective-permute-start.2) | collective-permute-done | bytes 491552 | tf_op jit(solution)/shard_map/ppermute | solution.py:424
  67.7 5.1 %assemble_first.1 = (bf16[768,768]{1,0:T(8,128)(2,1)}, bf16[768,768]{1,0:T(8,128)(2,1)}, bf16[768,768]{1,0:T(8,128)(2,1)}, f32[1,24,768]{2,1,0:T(8,128)}, f32[1,3072]{1,0:T(1,128)}) custom-call(s32[4]{0:T(128)} %pad_add_fusion.me, bf16[4,80,768]{2,1,0:T(8,128)(2,1)} %pad_maximum_fusion.1.refs_0_, bf16[4,80,768]{2,1,0:T(8,128)(2,1)} %collective-permute-done.2.refs_1_, ...), custom_call_target="tpu_custom_call" | custom-call | tf_op jit(solution)/shard_map/assemble_first/pallas_call | solution.py:578
  72.7 18.2 %attend_forward.2 = (bf16[2,512,768]{2,1,0:T(8,128)(2,1)}, bf16[2,512,768]{2,1,0:T(8,128)(2,1)}, bf16[2,512,768]{2,1,0:T(8,128)(2,1)}, bf16[2,512,768]{2,1,0:T(8...) custom-call(bf16[2,2,502,768]{3,2,1,0:T(8,128)(2,1)} %copy.182, ...), custom_call_target="tpu_custom_call" | custom-call | flops 10066329600 | bytes 23592960 | tf_op jit(solution)/shard_map/attend_forward/pallas_call | solution.py:289
  90.9 20.0 %all-gather.3.cloned.1.call-done = bf16[288,24,768]{2,1,0:T(8,128)(2,1)} async-done(((bf16[9,24,768]{2,1,0:T(8,128)(2,1)}), bf16[288,24,768]{2,1,0:T(8,128)(2,1)}) %all-gather.3.cloned.1.call-update) | async-done | bytes 10616848 | tf_op jit(solution)/shard_map/all_gather | solution.py:786
  110.9 8.2 %assemble_rest.1 = (bf16[768,768]{1,0:T(8,128)(2,1)}, bf16[768,3072]{1,0:T(8,128)(2,1)}, bf16[3072,768]{1,0:T(8,128)(2,1)}) custom-call(bf16[32,9,24,768]{3,2,1,0:T(8,128)(2,1)} %bitcast.142), custom_call_target="tpu_custom_call" | custom-call | tf_op jit(solution)/shard_map/assemble_rest/pallas_call | solution.py:555
  119.2 29.6 %feed_forward.2 = (bf16[2,2,502,768]{3,2,1,0:T(8,128)(2,1)}, f32[2,16,768]{2,1,0:T(8,128)}, bf16[2,512,768]{2,1,0:T(8,128)(2,1)}, f32[2,512,128]{2,1,0:T(8,128)}...) custom-call(s32[2]{0:T(128)} %refs_0_.11, ...), custom_call_target="tpu_custom_call" | custom-call | flops 10871635968 | bytes 23592960 | tf_op jit(solution)/shard_map/feed_forward/pallas_call | solution.py:289
  148.8 18.2 %attend_forward.3 = (bf16[2,512,768]{2,1,0:T(8,128)(2,1)}, bf16[2,512,768]{2,1,0:T(8,128)(2,1)}, bf16[2,512,768]{2,1,0:T(8,128)(2,1)}, bf16[2,512,768]{2,1,0:T(8...) custom-call(bf16[2,2,502,768]{3,2,1,0:T(8,128)(2,1)} %copy.182, ...), custom_call_target="tpu_custom_call" | custom-call | flops 10066329600 | bytes 23592960 | tf_op jit(solution)/shard_map/attend_forward/pallas_call | solution.py:289
  167.0 29.3 %feed_forward.3 = (bf16[2,2,502,768]{3,2,1,0:T(8,128)(2,1)}, f32[2,16,768]{2,1,0:T(8,128)}, bf16[2,512,768]{2,1,0:T(8,128)(2,1)}, f32[2,512,128]{2,1,0:T(8,128)}...) custom-call(s32[2]{0:T(128)} %refs_0_.11, ...), custom_call_target="tpu_custom_call", output_to_operand_aliasing={{0}: (9, {})} | custom-call | flops 10871635968 | bytes 23592960 | tf_op jit(solution)/shard_map/feed_forward/pallas_call | solution.py:289
  196.3 22.1 %feed_backward.2 = (bf16[2,512,768]{2,1,0:T(8,128)(2,1)}, bf16[2,512,3072]{2,1,0:T(8,128)(2,1)}, f32[2,512,768]{2,1,0:T(8,128)}, bf16[2,512,768]{2,1,0:T(8,128)(...) custom-call(s32[2]{0:T(128)} %refs_0_.11, bf16[2,2,502,768]{3,2,1,0:T(8,128)(2,1)} %copy.181, ...), custom_call_target="tpu_custom_call" | custom-call | flops 9663676416 | bytes 23592960 | tf_op jit(solution)/shard_map/feed_backward/pallas_call | solution.py:289
  218.4 28.7 %attend_backward.2 = (bf16[2,2,502,768]{3,2,1,0:T(8,128)(2,1)}, f32[2,16,768]{2,1,0:T(8,128)}, bf16[2,512,768]{2,1,0:T(8,128)(2,1)}, bf16[2,512,768]{2,1,0:T(8,1...) custom-call(s32[2]{0:T(128)} %refs_0_.11, f32[2,16,768]{2,1,0:T(8,128)} %pad_convert_fusion.refs_2_.refs_1_, ...), custom_call_target="tpu_custom_call" | custom-call | flops 17716740096 | bytes 31457280 | tf_op jit(solution)/shard_map/attend_backward/pallas_call | solution.py:289
  247.1 22.3 %feed_backward.3 = (bf16[2,512,768]{2,1,0:T(8,128)(2,1)}, bf16[2,512,3072]{2,1,0:T(8,128)(2,1)}, f32[2,512,768]{2,1,0:T(8,128)}, bf16[2,512,768]{2,1,0:T(8,128)(...) custom-call(s32[2]{0:T(128)} %refs_0_.11, bf16[2,2,502,768]{3,2,1,0:T(8,128)(2,1)} %copy.181, ...), custom_call_target="tpu_custom_call" | custom-call | flops 9663676416 | bytes 23592960 | tf_op jit(solution)/shard_map/feed_backward/pallas_call | solution.py:289
  269.5 14.6 %weight_product.1 = bf16[3072,768]{1,0:T(8,128)(2,1)} custom-call(bf16[2,512,3072]{2,1,0:T(8,128)(2,1)} %get-tuple-element.151.refs_0_, bf16[2,512,3072]{2,1,0:T(8,128)(2,1)} %get-tuple-element.152.refs_1_, bf16[2,512,768]{2,1,0:T(8,128)(2,1)} %get-tuple-element.153.refs_2_, bf16[2,512,768]{2,1,0:T(8,128)(2,1)} %get-tuple-element.154.refs_3_), custom_call_target="tpu_custom_call" | custom-call | flops 9663676416 | bytes 15728640 | tf_op jit(solution)/shard_map/weight_product/pallas_call | solution.py:396
  284.1 20.7 %product_up.1 = (bf16[4,2,2,5,24,768]{5,4,3,2,1,0:T(8,128)(2,1)}, bf16[4,2,2,5,24,768]{5,4,3,2,1,0:T(8,128)(2,1)}) custom-call(s32[4]{0:T(128)} %pad_add_fusion.me, bf16[2,512,768]{2,1,0:T(8,128)(2,1)} %get-tuple-element.155.refs_3_.refs_0_.refs_8_, bf16[2,512,768]{2,1,0:T(8,128)(2,1)} %get-tuple-element.129.refs_3_.refs_8_.refs_1_, ...), custom_call_target="tpu_custom_call" | custom-call | flops 12079595520 | bytes 27918336 | tf_op jit(solution)/shard_map/product_up/pallas_call | solution.py:705
  305.0 5.4 %collective-permute-done.11 = bf16[4,2,2,5,24,768]{5,4,3,2,1,0:T(8,128)(2,1)} collective-permute-done((bf16[4,2,2,5,24,768]{5,4,3,2,1,0:T(8,128)(2,1)}, bf16[4,2,2,5,24,768]{5,4,3,2,1,0:T(8,128)(2,1)}, u32[]{:S(2)}, u32[]{:S(2)}) %collective-permute-start.11) | collective-permute-done | bytes 2949152 | tf_op jit(solution)/shard_map/ppermute | solution.py:424
  310.5 1.5 fusion.23
  313.2 1.5 collective-permute-start.13
  316.4 29.2 %attend_backward.3 = (bf16[2,2,502,768]{3,2,1,0:T(8,128)(2,1)}, f32[2,16,768]{2,1,0:T(8,128)}, bf16[2,512,768]{2,1,0:T(8,128)(2,1)}, bf16[2,512,768]{2,1,0:T(8,1...) custom-call(s32[2]{0:T(128)} %refs_0_.11, ...), custom_call_target="tpu_custom_call", output_to_operand_aliasing={{0}: (14, {})} | custom-call | flops 17716740096 | bytes 31457280 | tf_op jit(solution)/shard_map/attend_backward/pallas_call | solution.py:289
  345.6 1.6 bitcast_add_fusion
  348.0 1.6 bitcast_add_fusion.1
  349.7 19.2 %product_first.1 = (bf16[4,2,2,80,768]{4,3,2,1,0:T(8,128)(2,1)}, bf16[4,2,2,80,768]{4,3,2,1,0:T(8,128)(2,1)}) custom-call(s32[4]{0:T(128)} %pad_add_fusion.me, f32[2,8,768]{2,1,0:T(8,128)} %get-tuple-element.143.refs_0_, f32[2,8,768]{2,1,0:T(8,128)} %get-tuple-element.170.refs_1_, f32[2,8,768]{2,1,0:T(8,128)} %get-tuple-element.171.refs_2_, ...), custom_call_target="tpu_custom_call" | custom-call | flops 7247757312 | bytes 16121856 | tf_op jit(solution)/shard_map/product_first/pallas_call | solution.py:753
  369.0 1.5 collective-permute-start.22
  371.5 9.4 %collective-permute-done.22 = bf16[2,5,24,768]{3,2,1,0:T(8,128)(2,1)S(1)} collective-permute-done((bf16[2,5,24,768]{3,2,1,0:T(8,128)(2,1)S(1)}, bf16[2,5,24,768]{3,2,1,0:T(8,128)(2,1)S(1)}, u32[]{:S(2)}, u32[]{:S(2)}) %collective-permute-start.22) | collective-permute-done | bytes 368672 | tf_op jit(solution)/shard_map/ppermute | solution.py:424
  381.8 2.1 collective-permute-done.24
  384.1 1.8 collective-permute-start.25
  385.9 1.9 collective-permute-start.26
  388.5 1.8 collective-permute-start.15
  390.3 8.7 %collective-permute-done.17 = bf16[2,2,80,768]{3,2,1,0:T(8,128)(2,1)S(1)} collective-permute-done((bf16[2,2,80,768]{3,2,1,0:T(8,128)(2,1)S(1)}, bf16[2,2,80,768]{3,2,1,0:T(8,128)(2,1)S(1)}, u32[]{:S(2)}, u32[]{:S(2)}) %collective-permute-start.17) | collective-permute-done | bytes 491552 | tf_op jit(solution)/shard_map/ppermute | solution.py:424
  400.2 2.6 collective-permute-start.16
  403.6 1.8 collective-permute-done.18
  406.2 1.3 collective-permute-done.16
  409.4 1.5 collective-permute-start.20
  411.0 2.4 collective-permute-start.21
  414.0 8.1 %reduce-scatter.2.cloned.1.call-done = bf16[96,768]{1,0:T(8,128)(2,1)} async-done(((bf16[3072,768]{1,0:T(8,128)(2,1)}), bf16[96,768]{1,0:T(8,128)(2,1)}) %reduce-scatter.2.cloned.1.call-update) | async-done | bytes 147472 | tf_op jit(solution)/shard_map/reduce_scatter | solution.py:871
  422.1 1.6 convert_element_type.237
  423.8 4.0 copy.148
  427.8 4.0 copy.150
  (129 shorter events, 28.6 us)
Async XLA Ops:
  7.2 4.3 copy-start.23
  7.2 4.3 copy-start.22
  7.2 4.3 copy-start.21
  7.2 4.3 copy-start.20
  7.2 4.3 copy-start.19
  7.2 4.3 copy-start.18
  7.3 4.3 copy-start.17
  7.3 4.3 copy-start.16
  7.3 4.3 copy-start.15
  7.3 4.5 %copy-start.24 = (bf16[96]{0:T(256)(128)(2,1)S(1)}, bf16[96]{0:T(256)(128)(2,1)}, u32[]{:S(2)}) copy-start(bf16[96]{0:T(256)(128)(2,1)} %param.32) | copy-start | bytes 580
  7.3 103.7 %all-gather.3.cloned.1.call-start = ((), (), s32[]{:S(2)}) async-start(), calls=%async_computation.2 | async-start | bytes 10948608 | tf_op jit(solution)/shard_map/all_gather | solution.py:786
  11.4 37.6 %copy-start.2 = (bf16[2,2,502,768]{3,1,2,0:T(2,128)(2,1)S(1)}, bf16[2,2,502,768]{3,1,2,0:T(2,128)(2,1)}, u32[]{:S(2)}) copy-start(bf16[2,2,502,768]{3,1,2,0:T(2,128)(2,1)} %param.20) | copy-start | bytes 9252868
  11.4 410.7 %reduce-scatter.2.cloned.1.call-start = ((), (), s32[]{:S(2)}) async-start(), calls=%async_computation.1 | async-start | bytes 4866048 | tf_op jit(solution)/shard_map/reduce_scatter | solution.py:871
  14.4 6.6 %collective-permute-start = (bf16[80,768]{1,0:T(8,128)(2,1)}, bf16[80,768]{1,0:T(8,128)(2,1)S(1)}, u32[]{:S(2)}, u32[]{:S(2)}) collective-permute-start(bf16[80,768]{1,0:T(8,128)(2,1)} %pack_first.1), channel_id=1, source_target_pairs={{0,8},{1,9},{2,10},{3,11},{4,12},{5,13},{6,14},{7,15},{8,0},{9,1},... | collective-permute-start | bytes 368648 | tf_op jit(solution)/shard_map/ppermute | solution.py:424
  17.4 9.6 %collective-permute-start.4 = (bf16[80,768]{1,0:T(8,128)(2,1)}, bf16[80,768]{1,0:T(8,128)(2,1)S(1)}, u32[]{:S(2)}, u32[]{:S(2)}) collective-permute-start(bf16[80,768]{1,0:T(8,128)(2,1)} %pack_first.1), channel_id=1, source_target_pairs={{0,24},{1,25},{2,26},{3,27},{4,28},{5,29},{6,30},{7,31},{8,16},{9,... | collective-permute-start | bytes 368648 | tf_op jit(solution)/shard_map/ppermute | solution.py:424
  19.9 18.0 %collective-permute-start.3 = (bf16[80,768]{1,0:T(8,128)(2,1)}, bf16[80,768]{1,0:T(8,128)(2,1)S(1)}, u32[]{:S(2)}, u32[]{:S(2)}) collective-permute-start(bf16[80,768]{1,0:T(8,128)(2,1)} %pack_first.1), channel_id=1, source_target_pairs={{0,16},{1,17},{2,18},{3,19},{4,20},{5,21},{6,22},{7,23},{8,24},{9,... | collective-permute-start | bytes 368648 | tf_op jit(solution)/shard_map/ppermute | solution.py:424
  21.9 17.6 %collective-permute-start.1 = (bf16[2,80,768]{2,1,0:T(8,128)(2,1)S(1)}, bf16[2,80,768]{2,1,0:T(8,128)(2,1)S(1)}, u32[]{:S(2)}, u32[]{:S(2)}) collective-permute-start(bf16[2,80,768]{2,1,0:T(8,128)(2,1)S(1)} %pad_maximum_fusion.3), channel_id=1, source_target_pairs={{0,4},{1,5},{2,6},{3,7},{4,0},{5,1},{6,2},{7,3},{8,12},{9,13},{10,... | collective-permute-start | bytes 737288 | tf_op jit(solution)/shard_map/ppermute | solution.py:424
  37.9 9.1 %collective-permute-start.5 = (bf16[2,80,768]{2,1,0:T(8,128)(2,1)S(1)}, bf16[2,80,768]{2,1,0:T(8,128)(2,1)S(1)}, u32[]{:S(2)}, u32[]{:S(2)}) collective-permute-start(bf16[2,80,768]{2,1,0:T(8,128)(2,1)S(1)} %pad_maximum_fusion.4), channel_id=1, source_target_pairs={{0,1},{1,0},{2,3},{3,2},{4,5},{5,4},{6,7},{7,6},{8,9},{9,8},{10,11... | collective-permute-start | bytes 737288 | tf_op jit(solution)/shard_map/ppermute | solution.py:424
  41.1 21.5 %collective-permute-start.2 = (bf16[4,80,768]{2,1,0:T(8,128)(2,1)}, bf16[4,80,768]{2,1,0:T(8,128)(2,1)}, u32[]{:S(2)}, u32[]{:S(2)}) collective-permute-start(bf16[4,80,768]{2,1,0:T(8,128)(2,1)} %pad_maximum_fusion.1.refs_0_), channel_id=1, source_target_pairs={{0,1},{1,0},{2,3},{3,2},{4,5},{5,4},{6,7},{7,6},{8,9},{9,8},{10,11... | collective-permute-start | bytes 1474568 | tf_op jit(solution)/shard_map/ppermute | solution.py:424
  47.7 3.4 copy-start.3
  47.7 14.9 %collective-permute-start.6 = (bf16[4,80,768]{2,1,0:T(8,128)(2,1)}, bf16[4,80,768]{2,1,0:T(8,128)(2,1)}, u32[]{:S(2)}, u32[]{:S(2)}) collective-permute-start(bf16[4,80,768]{2,1,0:T(8,128)(2,1)} %pad_maximum_fusion.2.refs_2_), channel_id=1, source_target_pairs={{0,4},{1,5},{2,6},{3,7},{4,0},{5,1},{6,2},{7,3},{8,12},{9,13},{10,... | collective-permute-start | bytes 1474568 | tf_op jit(solution)/shard_map/ppermute | solution.py:424
  51.1 12.5 %copy-start.13 = (bf16[2,10,768]{2,0,1:T(2,128)(2,1)S(1)}, bf16[2,10,768]{2,0,1:T(2,128)(2,1)}, u32[]{:S(2)}) copy-start(bf16[2,10,768]{2,0,1:T(2,128)(2,1)} %param.39) | copy-start | bytes 92164
  62.6 2.3 collective-permute-start.7
  62.6 2.8 collective-permute-start.8
  63.1 3.0 collective-permute-start.9
  63.1 3.7 collective-permute-start.10
  304.7 5.7 %collective-permute-start.11 = (bf16[4,2,2,5,24,768]{5,4,3,2,1,0:T(8,128)(2,1)}, bf16[4,2,2,5,24,768]{5,4,3,2,1,0:T(8,128)(2,1)}, u32[]{:S(2)}, u32[]{:S(2)}) collective-permute-start(bf16[4,2,2,5,24,768]{5,4,3,2,1,0:T(8,128)(2,1)} %get-tuple-element.162), channel_id=1, source_target_pairs={{0,2},{1,3},{2,0},{3,1},{4,6},{5,7},{6,4},{7,5},{8,10},{9,11},{10,... | collective-permute-start | bytes 8847368 | tf_op jit(solution)/shard_map/ppermute | solution.py:424
  305.0 6.9 %copy-start.4 = (bf16[4,2,2,5,24,768]{5,4,3,2,1,0:T(8,128)(2,1)S(1)}, bf16[4,2,2,5,24,768]{5,4,3,2,1,0:T(8,128)(2,1)}, u32[]{:S(2)}) copy-start(bf16[4,2,2,5,24,768]{5,4,3,2,1,0:T(8,128)(2,1)} %get-tuple-element.161) | copy-start | bytes 8847364
  313.2 32.3 %collective-permute-start.13 = (bf16[2,2,5,24,768]{4,3,2,1,0:T(8,128)(2,1)S(1)}, bf16[2,2,5,24,768]{4,3,2,1,0:T(8,128)(2,1)S(1)}, u32[]{:S(2)}, u32[]{:S(2)}) collective-permute-start(bf16[2,2,5,24,768]{4,3,2,1,0:T(8,128)(2,1)S(1)} %fusion.1), channel_id=1, source_target_pairs={{0,4},{1,5},{2,6},{3,7},{4,0},{5,1},{6,2},{7,3},{8,12},{9,13},{10,... | collective-permute-start | bytes 2211848 | tf_op jit(solution)/shard_map/ppermute | solution.py:424
  315.8 31.3 %collective-permute-start.12 = (bf16[2,2,5,24,768]{4,3,2,0,1:T(8,128)(2,1)}, bf16[2,2,5,24,768]{4,3,2,0,1:T(8,128)(2,1)S(1)}, u32[]{:S(2)}, u32[]{:S(2)}) collective-permute-start(bf16[2,2,5,24,768]{4,3,2,0,1:T(8,128)(2,1)} %fusion), channel_id=1, source_target_pairs={{0,1},{1,0},{2,3},{3,2},{4,5},{5,4},{6,7},{7,6},{8,9},{9,8},{10,11... | collective-permute-start | bytes 2211848 | tf_op jit(solution)/shard_map/ppermute | solution.py:424
  349.7 20.8 %copy-start.14 = (f32[2,16,768]{2,1,0:T(8,128)S(1)}, f32[2,16,768]{2,1,0:T(8,128)}, u32[]{:S(2)}) copy-start(f32[2,16,768]{2,1,0:T(8,128)} %get-tuple-element.191) | copy-start | bytes 294916
  368.9 18.8 %collective-permute-start.14 = (bf16[4,2,2,80,768]{4,3,2,1,0:T(8,128)(2,1)}, bf16[4,2,2,80,768]{4,3,2,1,0:T(8,128)(2,1)S(1)}, u32[]{:S(2)}, u32[]{:S(2)}) collective-permute-start(bf16[4,2,2,80,768]{4,3,2,1,0:T(8,128)(2,1)} %get-tuple-element.185), channel_id=1, source_target_pairs={{0,2},{1,3},{2,0},{3,1},{4,6},{5,7},{6,4},{7,5},{8,10},{9,11},{10,... | collective-permute-start | bytes 5898248 | tf_op jit(solution)/shard_map/ppermute | solution.py:424
  369.0 11.8 %collective-permute-start.22 = (bf16[2,5,24,768]{3,2,1,0:T(8,128)(2,1)S(1)}, bf16[2,5,24,768]{3,2,1,0:T(8,128)(2,1)S(1)}, u32[]{:S(2)}, u32[]{:S(2)}) collective-permute-start(bf16[2,5,24,768]{3,2,1,0:T(8,128)(2,1)S(1)} %get-tuple-element.315), channel_id=1, source_target_pairs={{0,4},{1,5},{2,6},{3,7},{4,0},{5,1},{6,2},{7,3},{8,12},{9,13},{10,... | collective-permute-start | bytes 1105928 | tf_op jit(solution)/shard_map/ppermute | solution.py:424
  371.2 16.6 %copy-start.5 = (bf16[4,2,2,80,768]{4,3,2,1,0:T(8,128)(2,1)S(1)}, bf16[4,2,2,80,768]{4,3,2,1,0:T(8,128)(2,1)}, u32[]{:S(2)}) copy-start(bf16[4,2,2,80,768]{4,3,2,1,0:T(8,128)(2,1)} %get-tuple-element.184) | copy-start | bytes 5898244
  371.2 12.8 %collective-permute-start.24 = (bf16[2,5,24,768]{3,2,1,0:T(8,128)(2,1)S(1)}, bf16[2,5,24,768]{3,2,1,0:T(8,128)(2,1)S(1)}, u32[]{:S(2)}, u32[]{:S(2)}) collective-permute-start(bf16[2,5,24,768]{3,2,1,0:T(8,128)(2,1)S(1)} %get-tuple-element.316), channel_id=1, source_target_pairs={{0,1},{1,0},{2,3},{3,2},{4,5},{5,4},{6,7},{7,6},{8,9},{9,8},{10,11... | collective-permute-start | bytes 1105928 | tf_op jit(solution)/shard_map/ppermute | solution.py:424
  381.0 21.8 %collective-permute-start.23 = (bf16[5,24,768]{2,1,0:T(8,128)(2,1)S(1)}, bf16[5,24,768]{2,1,0:T(8,128)(2,1)S(1)}, u32[]{:S(2)}, u32[]{:S(2)}) collective-permute-start(bf16[5,24,768]{2,1,0:T(8,128)(2,1)S(1)} %fusion.20), channel_id=1, source_target_pairs={{0,8},{1,9},{2,10},{3,11},{4,12},{5,13},{6,14},{7,15},{8,0},{9,1},... | collective-permute-start | bytes 552968 | tf_op jit(solution)/shard_map/ppermute | solution.py:424
  384.1 18.7 %collective-permute-start.25 = (bf16[5,24,768]{2,1,0:T(8,128)(2,1)S(1)}, bf16[5,24,768]{2,1,0:T(8,128)(2,1)S(1)}, u32[]{:S(2)}, u32[]{:S(2)}) collective-permute-start(bf16[5,24,768]{2,1,0:T(8,128)(2,1)S(1)} %get-tuple-element.298), channel_id=1, source_target_pairs={{0,16},{1,17},{2,18},{3,19},{4,20},{5,21},{6,22},{7,23},{8,24},{9,... | collective-permute-start | bytes 552968 | tf_op jit(solution)/shard_map/ppermute | solution.py:424
  385.9 16.9 %collective-permute-start.26 = (bf16[5,24,768]{2,1,0:T(8,128)(2,1)S(1)}, bf16[5,24,768]{2,1,0:T(8,128)(2,1)S(1)}, u32[]{:S(2)}, u32[]{:S(2)}) collective-permute-start(bf16[5,24,768]{2,1,0:T(8,128)(2,1)S(1)} %get-tuple-element.299), channel_id=1, source_target_pairs={{0,24},{1,25},{2,26},{3,27},{4,28},{5,29},{6,30},{7,31},{8,16},{9,... | collective-permute-start | bytes 552968 | tf_op jit(solution)/shard_map/ppermute | solution.py:424
  387.9 11.1 %collective-permute-start.17 = (bf16[2,2,80,768]{3,2,1,0:T(8,128)(2,1)S(1)}, bf16[2,2,80,768]{3,2,1,0:T(8,128)(2,1)S(1)}, u32[]{:S(2)}, u32[]{:S(2)}) collective-permute-start(bf16[2,2,80,768]{3,2,1,0:T(8,128)(2,1)S(1)} %fusion.6), channel_id=1, source_target_pairs={{0,4},{1,5},{2,6},{3,7},{4,0},{5,1},{6,2},{7,3},{8,12},{9,13},{10,... | collective-permute-start | bytes 1474568 | tf_op jit(solution)/shard_map/ppermute | solution.py:424
  388.5 11.5 %collective-permute-start.15 = (bf16[2,2,80,768]{3,2,0,1:T(8,128)(2,1)S(1)}, bf16[2,2,80,768]{3,2,0,1:T(8,128)(2,1)S(1)}, u32[]{:S(2)}, u32[]{:S(2)}) collective-permute-start(bf16[2,2,80,768]{3,2,0,1:T(8,128)(2,1)S(1)} %fusion.5), channel_id=1, source_target_pairs={{0,1},{1,0},{2,3},{3,2},{4,5},{5,4},{6,7},{7,6},{8,9},{9,8},{10,11... | collective-permute-start | bytes 1474568 | tf_op jit(solution)/shard_map/ppermute | solution.py:424
  399.2 6.3 %collective-permute-start.18 = (bf16[2,80,768]{2,1,0:T(8,128)(2,1)S(1)}, bf16[2,80,768]{2,1,0:T(8,128)(2,1)S(1)}, u32[]{:S(2)}, u32[]{:S(2)}) collective-permute-start(bf16[2,80,768]{2,1,0:T(8,128)(2,1)S(1)} %fusion.16), channel_id=1, source_target_pairs={{0,1},{1,0},{2,3},{3,2},{4,5},{5,4},{6,7},{7,6},{8,9},{9,8},{10,11... | collective-permute-start | bytes 737288 | tf_op jit(solution)/shard_map/ppermute | solution.py:424
  400.2 7.3 %collective-permute-start.16 = (bf16[2,80,768]{2,1,0:T(8,128)(2,1)S(1)}, bf16[2,80,768]{2,1,0:T(8,128)(2,1)S(1)}, u32[]{:S(2)}, u32[]{:S(2)}) collective-permute-start(bf16[2,80,768]{2,1,0:T(8,128)(2,1)S(1)} %fusion.15), channel_id=1, source_target_pairs={{0,4},{1,5},{2,6},{3,7},{4,0},{5,1},{6,2},{7,3},{8,12},{9,13},{10,... | collective-permute-start | bytes 737288 | tf_op jit(solution)/shard_map/ppermute | solution.py:424
  402.9 20.9 %copy-start.1 = (bf16[2,2,502,768]{3,2,1,0:T(8,128)(2,1)S(1)}, bf16[2,2,502,768]{3,2,1,0:T(8,128)(2,1)}, u32[]{:S(2)}) copy-start(bf16[2,2,502,768]{3,2,1,0:T(8,128)(2,1)} %get-tuple-element.187) | copy-start | bytes 9252868
  409.0 22.8 %collective-permute-start.19 = (bf16[80,768]{1,0:T(8,128)(2,1)}, bf16[80,768]{1,0:T(8,128)(2,1)S(1)}, u32[]{:S(2)}, u32[]{:S(2)}) collective-permute-start(bf16[80,768]{1,0:T(8,128)(2,1)} %fusion.21), channel_id=1, source_target_pairs={{0,8},{1,9},{2,10},{3,11},{4,12},{5,13},{6,14},{7,15},{8,0},{9,1},... | collective-permute-start | bytes 368648 | tf_op jit(solution)/shard_map/ppermute | solution.py:424
  409.4 22.4 %collective-permute-start.20 = (bf16[80,768]{1,0:T(8,128)(2,1)}, bf16[80,768]{1,0:T(8,128)(2,1)S(1)}, u32[]{:S(2)}, u32[]{:S(2)}) collective-permute-start(bf16[80,768]{1,0:T(8,128)(2,1)} %get-tuple-element.194), channel_id=1, source_target_pairs={{0,16},{1,17},{2,18},{3,19},{4,20},{5,21},{6,22},{7,23},{8,24},{9,... | collective-permute-start | bytes 368648 | tf_op jit(solution)/shard_map/ppermute | solution.py:424
  411.0 20.9 %collective-permute-start.21 = (bf16[80,768]{1,0:T(8,128)(2,1)}, bf16[80,768]{1,0:T(8,128)(2,1)S(1)}, u32[]{:S(2)}, u32[]{:S(2)}) collective-permute-start(bf16[80,768]{1,0:T(8,128)(2,1)} %get-tuple-element.195), channel_id=1, source_target_pairs={{0,24},{1,25},{2,26},{3,27},{4,28},{5,29},{6,30},{7,31},{8,16},{9,... | collective-permute-start | bytes 368648 | tf_op jit(solution)/shard_map/ppermute | solution.py:424
  423.8 4.0 copy-start
  427.8 4.0 copy-start.7
  (6 other events, 6.5 us)
Sparse Core Ops, SparseCore 0:
  11.6 99.3 all-gather.2
  305.1 116.9 reduce-scatter.1

commit v5 on v4

--- a/solution.py
+++ b/solution.py
@@ -4,6 +4,7 @@
 import jax.numpy as jnp
 from jax import lax
 from jax.experimental import pallas as pl
+from jax.experimental.layout import Layout, with_layout_constraint
 from jax.experimental.pallas import tpu as pltpu
 from jax.sharding import PartitionSpec as P
 
@@ -771,7 +772,8 @@
 
 
 def shown(array):
-    return lax.optimization_barrier(array.transpose(0, 2, 1, 3))
+    turned = with_layout_constraint(array.transpose(0, 2, 1, 3), Layout(major_to_minor=(0, 1, 2, 3)))
+    return lax.optimization_barrier(turned)
 
 
 def gather_weights(me, shards, *rows):

time: 450 us -> 443 us (0.984)
  waiting for transfers between devices: 88.7 us -> 81.7 us
    unnamed x57 -> x51, local copies, waits for them, and re-layouts: 15.4 us -> 6.59 us
    optimization_barrier x0 -> x2, local copies, waits for them, and re-layouts: none -> 8.04 us  [after(): return lax.optimization_barrier((array,) + others)[0]]
    ppermute x27, waiting for transfers between devices: 60.5 us -> 53.3 us  [swap(): return lax.ppermute(array, AXES, pairs)]
  transfers between devices with their start and end apart: 29 -> 29, of which waited for: 16 -> 14; matrix products, arithmetic and copies ran while one was open for 7% -> 7% of each run, Pallas kernels for 17% -> 17%
where the time goes in v5:
time: 443 us; the launch traced here: 435 us
  Pallas kernels  267 us (60%)
  waiting for transfers between devices  81.7 us (18%)
  starting transfers between devices  32.2 us (7%)
  local copies, waits for them, and re-layouts  23.4 us (5%)
  between operations  15.1 us (3%)
  other arithmetic  14.9 us (3%)
    pallas_call x8, Pallas kernels, launch(): pl.pallas_call(run if into else body, grid=grid, in_specs=list(in_specs)...  198 us
    ppermute x27, waiting for transfers between devices, swap(): return lax.ppermute(array, AXES, pairs)  53.3 us
    ppermute x27, starting transfers between devices, swap(): return lax.ppermute(array, AXES, pairs)  32.2 us
    pallas_call x1, Pallas kernels, call_product_up(): pl.pallas_call(functools.partial(product_up, segments), grid_spec=pltpu.P...  20.9 us
    all_gather x1, waiting for transfers between devices, gather_weights(): units = lax.all_gather(units, AXES, axis=0)  20 us
    pallas_call x1, Pallas kernels, call_product_first(): pl.pallas_call(functools.partial(product_first, segments), grid_spec=pltp...  19.2 us
    pallas_call x1, Pallas kernels, call_weight_product(): pl.pallas_call(functools.partial(weight_product, parts), grid=(n_left //...  14.8 us
  transfers between devices with their start and end apart: 29, of which 14 were waited for; matrix products, arithmetic and copies ran while one was open for 7% of the time, Pallas kernels for 17%

profile of v5, /device:TPU:0, one launch (start us, length us, event | category | flops | bytes accessed | tf_op | source)
XLA Modules:
  0.0 434.6 jit_solution(9751363449294924393)
XLA Ops:
  12.9 1.5 pack_first.1
  14.4 3.0 collective-permute-start
  17.4 2.5 collective-permute-start.4
  21.9 1.7 collective-permute-start.1
  23.6 3.4 collective-permute-done.4
  27.0 10.8 %collective-permute-done.3 = bf16[80,768]{1,0:T(8,128)(2,1)S(1)} collective-permute-done((bf16[80,768]{1,0:T(8,128)(2,1)}, bf16[80,768]{1,0:T(8,128)(2,1)S(1)}, u32[]{:S(2)}, u32[]{:S(2)}) %collective-permute-start.3) | collective-permute-done | bytes 122912 | tf_op jit(solution)/shard_map/ppermute | solution.py:425
  37.9 1.6 collective-permute-start.5
  39.4 1.7 pad_maximum_fusion.1.refs_0_
  41.7 5.2 %collective-permute-done.5 = bf16[2,80,768]{2,1,0:T(8,128)(2,1)S(1)} collective-permute-done((bf16[2,80,768]{2,1,0:T(8,128)(2,1)S(1)}, bf16[2,80,768]{2,1,0:T(8,128)(2,1)S(1)}, u32[]{:S(2)}, u32[]{:S(2)}) %collective-permute-start.5) | collective-permute-done | bytes 245792 | tf_op jit(solution)/shard_map/ppermute | solution.py:425
  47.7 1.3 collective-permute-start.6
  49.1 2.1 copy.184
  51.1 2.0 copy.183
  53.2 9.4 %collective-permute-done.2.refs_1_ = bf16[4,80,768]{2,1,0:T(8,128)(2,1)} collective-permute-done((bf16[4,80,768]{2,1,0:T(8,128)(2,1)}, bf16[4,80,768]{2,1,0:T(8,128)(2,1)}, u32[]{:S(2)}, u32[]{:S(2)}) %collective-permute-start.2) | collective-permute-done | bytes 491552 | tf_op jit(solution)/shard_map/ppermute | solution.py:425
  67.7 5.1 %assemble_first.1 = (bf16[768,768]{1,0:T(8,128)(2,1)}, bf16[768,768]{1,0:T(8,128)(2,1)}, bf16[768,768]{1,0:T(8,128)(2,1)}, f32[1,24,768]{2,1,0:T(8,128)}, f32[1,3072]{1,0:T(1,128)}) custom-call(s32[4]{0:T(128)} %pad_add_fusion.me, bf16[4,80,768]{2,1,0:T(8,128)(2,1)} %pad_maximum_fusion.1.refs_0_, bf16[4,80,768]{2,1,0:T(8,128)(2,1)} %collective-permute-done.2.refs_1_, ...), custom_call_target="tpu_custom_call" | custom-call | tf_op jit(solution)/shard_map/assemble_first/pallas_call | solution.py:579
  72.7 18.2 %attend_forward.2 = (bf16[2,512,768]{2,1,0:T(8,128)(2,1)}, bf16[2,512,768]{2,1,0:T(8,128)(2,1)}, bf16[2,512,768]{2,1,0:T(8,128)(2,1)}, bf16[2,512,768]{2,1,0:T(8...) custom-call(bf16[2,2,502,768]{3,2,1,0:T(8,128)(2,1)} %copy.184, ...), custom_call_target="tpu_custom_call" | custom-call | flops 10066329600 | bytes 23592960 | tf_op jit(solution)/shard_map/attend_forward/pallas_call | solution.py:290
  90.9 20.0 %all-gather.3.cloned.1.call-done = bf16[288,24,768]{2,1,0:T(8,128)(2,1)} async-done(((bf16[9,24,768]{2,1,0:T(8,128)(2,1)}), bf16[288,24,768]{2,1,0:T(8,128)(2,1)}) %all-gather.3.cloned.1.call-update) | async-done | bytes 10616848 | tf_op jit(solution)/shard_map/all_gather | solution.py:788
  110.9 8.2 %assemble_rest.1 = (bf16[768,768]{1,0:T(8,128)(2,1)}, bf16[768,3072]{1,0:T(8,128)(2,1)}, bf16[3072,768]{1,0:T(8,128)(2,1)}) custom-call(bf16[32,9,24,768]{3,2,1,0:T(8,128)(2,1)} %bitcast.146), custom_call_target="tpu_custom_call" | custom-call | tf_op jit(solution)/shard_map/assemble_rest/pallas_call | solution.py:556
  119.2 29.6 %feed_forward.2 = (bf16[2,2,502,768]{3,2,1,0:T(8,128)(2,1)}, f32[2,16,768]{2,1,0:T(8,128)}, bf16[2,512,768]{2,1,0:T(8,128)(2,1)}, f32[2,512,128]{2,1,0:T(8,128)}...) custom-call(s32[2]{0:T(128)} %refs_0_.11, ...), custom_call_target="tpu_custom_call" | custom-call | flops 10871635968 | bytes 23592960 | tf_op jit(solution)/shard_map/feed_forward/pallas_call | solution.py:290
  148.8 18.2 %attend_forward.3 = (bf16[2,512,768]{2,1,0:T(8,128)(2,1)}, bf16[2,512,768]{2,1,0:T(8,128)(2,1)}, bf16[2,512,768]{2,1,0:T(8,128)(2,1)}, bf16[2,512,768]{2,1,0:T(8...) custom-call(bf16[2,2,502,768]{3,2,1,0:T(8,128)(2,1)} %copy.184, ...), custom_call_target="tpu_custom_call" | custom-call | flops 10066329600 | bytes 23592960 | tf_op jit(solution)/shard_map/attend_forward/pallas_call | solution.py:290
  167.0 29.3 %feed_forward.3 = (bf16[2,2,502,768]{3,2,1,0:T(8,128)(2,1)}, f32[2,16,768]{2,1,0:T(8,128)}, bf16[2,512,768]{2,1,0:T(8,128)(2,1)}, f32[2,512,128]{2,1,0:T(8,128)}...) custom-call(s32[2]{0:T(128)} %refs_0_.11, ...), custom_call_target="tpu_custom_call", output_to_operand_aliasing={{0}: (9, {})} | custom-call | flops 10871635968 | bytes 23592960 | tf_op jit(solution)/shard_map/feed_forward/pallas_call | solution.py:290
  196.3 22.1 %feed_backward.2 = (bf16[2,512,768]{2,1,0:T(8,128)(2,1)}, bf16[2,512,3072]{2,1,0:T(8,128)(2,1)}, f32[2,512,768]{2,1,0:T(8,128)}, bf16[2,512,768]{2,1,0:T(8,128)(...) custom-call(s32[2]{0:T(128)} %refs_0_.11, bf16[2,2,502,768]{3,2,1,0:T(8,128)(2,1)} %copy.183, ...), custom_call_target="tpu_custom_call" | custom-call | flops 9663676416 | bytes 23592960 | tf_op jit(solution)/shard_map/feed_backward/pallas_call | solution.py:290
  218.4 28.7 %attend_backward.2 = (bf16[2,2,502,768]{3,2,1,0:T(8,128)(2,1)}, f32[2,16,768]{2,1,0:T(8,128)}, bf16[2,512,768]{2,1,0:T(8,128)(2,1)}, bf16[2,512,768]{2,1,0:T(8,1...) custom-call(s32[2]{0:T(128)} %refs_0_.11, f32[2,16,768]{2,1,0:T(8,128)} %pad_convert_fusion.refs_2_.refs_1_, ...), custom_call_target="tpu_custom_call" | custom-call | flops 17716740096 | bytes 31457280 | tf_op jit(solution)/shard_map/attend_backward/pallas_call | solution.py:290
  247.1 22.3 %feed_backward.3 = (bf16[2,512,768]{2,1,0:T(8,128)(2,1)}, bf16[2,512,3072]{2,1,0:T(8,128)(2,1)}, f32[2,512,768]{2,1,0:T(8,128)}, bf16[2,512,768]{2,1,0:T(8,128)(...) custom-call(s32[2]{0:T(128)} %refs_0_.11, bf16[2,2,502,768]{3,2,1,0:T(8,128)(2,1)} %copy.183, ...), custom_call_target="tpu_custom_call" | custom-call | flops 9663676416 | bytes 23592960 | tf_op jit(solution)/shard_map/feed_backward/pallas_call | solution.py:290
  269.5 14.8 %weight_product.1 = bf16[3072,768]{1,0:T(8,128)(2,1)} custom-call(bf16[2,512,3072]{2,1,0:T(8,128)(2,1)} %get-tuple-element.151.refs_0_, bf16[2,512,3072]{2,1,0:T(8,128)(2,1)} %get-tuple-element.152.refs_1_, bf16[2,512,768]{2,1,0:T(8,128)(2,1)} %get-tuple-element.153.refs_2_, bf16[2,512,768]{2,1,0:T(8,128)(2,1)} %get-tuple-element.154.refs_3_), custom_call_target="tpu_custom_call" | custom-call | flops 9663676416 | bytes 15728640 | tf_op jit(solution)/shard_map/weight_product/pallas_call | solution.py:397
  284.3 20.9 %product_up.1 = (bf16[4,2,2,5,24,768]{5,4,3,2,1,0:T(8,128)(2,1)}, bf16[4,2,2,5,24,768]{5,4,3,2,1,0:T(8,128)(2,1)}) custom-call(s32[4]{0:T(128)} %pad_add_fusion.me, bf16[2,512,768]{2,1,0:T(8,128)(2,1)} %get-tuple-element.155.refs_3_.refs_0_.refs_8_, bf16[2,512,768]{2,1,0:T(8,128)(2,1)} %get-tuple-element.129.refs_3_.refs_8_.refs_1_, ...), custom_call_target="tpu_custom_call" | custom-call | flops 12079595520 | bytes 27918336 | tf_op jit(solution)/shard_map/product_up/pallas_call | solution.py:706
  305.5 5.4 %collective-permute-done.11 = bf16[4,2,2,5,24,768]{5,4,3,2,1,0:T(8,128)(2,1)} collective-permute-done((bf16[4,2,2,5,24,768]{5,4,3,2,1,0:T(8,128)(2,1)}, bf16[4,2,2,5,24,768]{5,4,3,2,1,0:T(8,128)(2,1)}, u32[]{:S(2)}, u32[]{:S(2)}) %collective-permute-start.11) | collective-permute-done | bytes 2949152 | tf_op jit(solution)/shard_map/ppermute | solution.py:425
  310.9 1.5 fusion.23
  312.4 1.3 fusion.1
  313.7 1.5 collective-permute-start.13
  315.2 1.0 fusion
  316.8 29.2 %attend_backward.3 = (bf16[2,2,502,768]{3,2,1,0:T(8,128)(2,1)}, f32[2,16,768]{2,1,0:T(8,128)}, bf16[2,512,768]{2,1,0:T(8,128)(2,1)}, bf16[2,512,768]{2,1,0:T(8,1...) custom-call(s32[2]{0:T(128)} %refs_0_.11, ...), custom_call_target="tpu_custom_call", output_to_operand_aliasing={{0}: (14, {})} | custom-call | flops 17716740096 | bytes 31457280 | tf_op jit(solution)/shard_map/attend_backward/pallas_call | solution.py:290
  346.0 1.6 bitcast_add_fusion
  348.5 1.6 bitcast_add_fusion.1
  350.1 19.2 %product_first.1 = (bf16[4,2,2,80,768]{4,3,2,1,0:T(8,128)(2,1)}, bf16[4,2,2,80,768]{4,3,2,1,0:T(8,128)(2,1)}) custom-call(s32[4]{0:T(128)} %pad_add_fusion.me, f32[2,8,768]{2,1,0:T(8,128)} %get-tuple-element.143.refs_0_, f32[2,8,768]{2,1,0:T(8,128)} %get-tuple-element.170.refs_1_, f32[2,8,768]{2,1,0:T(8,128)} %get-tuple-element.171.refs_2_, ...), custom_call_target="tpu_custom_call" | custom-call | flops 7247757312 | bytes 16121856 | tf_op jit(solution)/shard_map/product_first/pallas_call | solution.py:754
  369.5 1.5 collective-permute-start.22
  371.9 9.4 %collective-permute-done.22 = bf16[2,5,24,768]{3,2,1,0:T(8,128)(2,1)S(1)} collective-permute-done((bf16[2,5,24,768]{3,2,1,0:T(8,128)(2,1)S(1)}, bf16[2,5,24,768]{3,2,1,0:T(8,128)(2,1)S(1)}, u32[]{:S(2)}, u32[]{:S(2)}) %collective-permute-start.22) | collective-permute-done | bytes 368672 | tf_op jit(solution)/shard_map/ppermute | solution.py:425
  382.3 2.1 collective-permute-done.24
  384.5 1.8 collective-permute-start.25
  386.3 1.9 collective-permute-start.26
  388.9 1.8 collective-permute-start.15
  390.7 4.0 copy.186
  394.7 4.7 %collective-permute-done.17 = bf16[2,2,80,768]{3,2,1,0:T(8,128)(2,1)S(1)} collective-permute-done((bf16[2,2,80,768]{3,2,1,0:T(8,128)(2,1)S(1)}, bf16[2,2,80,768]{3,2,1,0:T(8,128)(2,1)S(1)}, u32[]{:S(2)}, u32[]{:S(2)}) %collective-permute-start.17) | collective-permute-done | bytes 491552 | tf_op jit(solution)/shard_map/ppermute | solution.py:425
  400.5 2.7 collective-permute-start.16
  403.3 4.0 copy.185
  408.2 3.6 collective-permute-start.19
  411.8 2.4 collective-permute-start.21
  414.9 8.3 %reduce-scatter.2.cloned.1.call-done = bf16[96,768]{1,0:T(8,128)(2,1)} async-done(((bf16[3072,768]{1,0:T(8,128)(2,1)}), bf16[96,768]{1,0:T(8,128)(2,1)}) %reduce-scatter.2.cloned.1.call-update) | async-done | bytes 147472 | tf_op jit(solution)/shard_map/reduce_scatter | solution.py:873
  423.2 1.6 convert_element_type.237
  (125 shorter events, 23.6 us)
Async XLA Ops:
  7.2 4.3 copy-start.21
  7.2 4.3 copy-start.20
  7.2 4.3 copy-start.19
  7.2 4.3 copy-start.18
  7.2 4.3 copy-start.17
  7.2 4.3 copy-start.16
  7.3 4.3 copy-start.15
  7.3 4.3 copy-start.14
  7.3 4.3 copy-start.13
  7.3 4.5 %copy-start.22 = (bf16[96]{0:T(256)(128)(2,1)S(1)}, bf16[96]{0:T(256)(128)(2,1)}, u32[]{:S(2)}) copy-start(bf16[96]{0:T(256)(128)(2,1)} %param.32) | copy-start | bytes 580
  7.3 103.7 %all-gather.3.cloned.1.call-start = ((), (), s32[]{:S(2)}) async-start(), calls=%async_computation.2 | async-start | bytes 10948608 | tf_op jit(solution)/shard_map/all_gather | solution.py:788
  11.4 37.6 %copy-start.2 = (bf16[2,2,502,768]{3,1,2,0:T(2,128)(2,1)S(1)}, bf16[2,2,502,768]{3,1,2,0:T(2,128)(2,1)}, u32[]{:S(2)}) copy-start(bf16[2,2,502,768]{3,1,2,0:T(2,128)(2,1)} %param.20) | copy-start | bytes 9252868
  11.4 411.8 %reduce-scatter.2.cloned.1.call-start = ((), (), s32[]{:S(2)}) async-start(), calls=%async_computation.1 | async-start | bytes 4866048 | tf_op jit(solution)/shard_map/reduce_scatter | solution.py:873
  14.4 6.6 %collective-permute-start = (bf16[80,768]{1,0:T(8,128)(2,1)}, bf16[80,768]{1,0:T(8,128)(2,1)S(1)}, u32[]{:S(2)}, u32[]{:S(2)}) collective-permute-start(bf16[80,768]{1,0:T(8,128)(2,1)} %pack_first.1), channel_id=1, source_target_pairs={{0,8},{1,9},{2,10},{3,11},{4,12},{5,13},{6,14},{7,15},{8,0},{9,1},... | collective-permute-start | bytes 368648 | tf_op jit(solution)/shard_map/ppermute | solution.py:425
  17.4 9.6 %collective-permute-start.4 = (bf16[80,768]{1,0:T(8,128)(2,1)}, bf16[80,768]{1,0:T(8,128)(2,1)S(1)}, u32[]{:S(2)}, u32[]{:S(2)}) collective-permute-start(bf16[80,768]{1,0:T(8,128)(2,1)} %pack_first.1), channel_id=1, source_target_pairs={{0,24},{1,25},{2,26},{3,27},{4,28},{5,29},{6,30},{7,31},{8,16},{9,... | collective-permute-start | bytes 368648 | tf_op jit(solution)/shard_map/ppermute | solution.py:425
  19.9 18.0 %collective-permute-start.3 = (bf16[80,768]{1,0:T(8,128)(2,1)}, bf16[80,768]{1,0:T(8,128)(2,1)S(1)}, u32[]{:S(2)}, u32[]{:S(2)}) collective-permute-start(bf16[80,768]{1,0:T(8,128)(2,1)} %pack_first.1), channel_id=1, source_target_pairs={{0,16},{1,17},{2,18},{3,19},{4,20},{5,21},{6,22},{7,23},{8,24},{9,... | collective-permute-start | bytes 368648 | tf_op jit(solution)/shard_map/ppermute | solution.py:425
  21.9 17.6 %collective-permute-start.1 = (bf16[2,80,768]{2,1,0:T(8,128)(2,1)S(1)}, bf16[2,80,768]{2,1,0:T(8,128)(2,1)S(1)}, u32[]{:S(2)}, u32[]{:S(2)}) collective-permute-start(bf16[2,80,768]{2,1,0:T(8,128)(2,1)S(1)} %pad_maximum_fusion.3), channel_id=1, source_target_pairs={{0,4},{1,5},{2,6},{3,7},{4,0},{5,1},{6,2},{7,3},{8,12},{9,13},{10,... | collective-permute-start | bytes 737288 | tf_op jit(solution)/shard_map/ppermute | solution.py:425
  37.9 9.1 %collective-permute-start.5 = (bf16[2,80,768]{2,1,0:T(8,128)(2,1)S(1)}, bf16[2,80,768]{2,1,0:T(8,128)(2,1)S(1)}, u32[]{:S(2)}, u32[]{:S(2)}) collective-permute-start(bf16[2,80,768]{2,1,0:T(8,128)(2,1)S(1)} %pad_maximum_fusion.4), channel_id=1, source_target_pairs={{0,1},{1,0},{2,3},{3,2},{4,5},{5,4},{6,7},{7,6},{8,9},{9,8},{10,11... | collective-permute-start | bytes 737288 | tf_op jit(solution)/shard_map/ppermute | solution.py:425
  41.1 21.5 %collective-permute-start.2 = (bf16[4,80,768]{2,1,0:T(8,128)(2,1)}, bf16[4,80,768]{2,1,0:T(8,128)(2,1)}, u32[]{:S(2)}, u32[]{:S(2)}) collective-permute-start(bf16[4,80,768]{2,1,0:T(8,128)(2,1)} %pad_maximum_fusion.1.refs_0_), channel_id=1, source_target_pairs={{0,1},{1,0},{2,3},{3,2},{4,5},{5,4},{6,7},{7,6},{8,9},{9,8},{10,11... | collective-permute-start | bytes 1474568 | tf_op jit(solution)/shard_map/ppermute | solution.py:425
  47.7 3.4 copy-start.3
  47.7 14.9 %collective-permute-start.6 = (bf16[4,80,768]{2,1,0:T(8,128)(2,1)}, bf16[4,80,768]{2,1,0:T(8,128)(2,1)}, u32[]{:S(2)}, u32[]{:S(2)}) collective-permute-start(bf16[4,80,768]{2,1,0:T(8,128)(2,1)} %pad_maximum_fusion.2.refs_2_), channel_id=1, source_target_pairs={{0,4},{1,5},{2,6},{3,7},{4,0},{5,1},{6,2},{7,3},{8,12},{9,13},{10,... | collective-permute-start | bytes 1474568 | tf_op jit(solution)/shard_map/ppermute | solution.py:425
  51.1 12.5 %copy-start.11 = (bf16[2,10,768]{2,0,1:T(2,128)(2,1)S(1)}, bf16[2,10,768]{2,0,1:T(2,128)(2,1)}, u32[]{:S(2)}) copy-start(bf16[2,10,768]{2,0,1:T(2,128)(2,1)} %param.39) | copy-start | bytes 92164
  62.6 2.3 collective-permute-start.7
  62.6 2.8 collective-permute-start.8
  63.1 3.0 collective-permute-start.9
  63.1 3.7 collective-permute-start.10
  64.9 1.9 copy-start.7
  305.2 5.7 %collective-permute-start.11 = (bf16[4,2,2,5,24,768]{5,4,3,2,1,0:T(8,128)(2,1)}, bf16[4,2,2,5,24,768]{5,4,3,2,1,0:T(8,128)(2,1)}, u32[]{:S(2)}, u32[]{:S(2)}) collective-permute-start(bf16[4,2,2,5,24,768]{5,4,3,2,1,0:T(8,128)(2,1)} %get-tuple-element.162), channel_id=1, source_target_pairs={{0,2},{1,3},{2,0},{3,1},{4,6},{5,7},{6,4},{7,5},{8,10},{9,11},{10,... | collective-permute-start | bytes 8847368 | tf_op jit(solution)/shard_map/ppermute | solution.py:425
  305.5 6.9 %copy-start.4 = (bf16[4,2,2,5,24,768]{5,4,3,2,1,0:T(8,128)(2,1)S(1)}, bf16[4,2,2,5,24,768]{5,4,3,2,1,0:T(8,128)(2,1)}, u32[]{:S(2)}) copy-start(bf16[4,2,2,5,24,768]{5,4,3,2,1,0:T(8,128)(2,1)} %get-tuple-element.161) | copy-start | bytes 8847364
  313.7 32.3 %collective-permute-start.13 = (bf16[2,2,5,24,768]{4,3,2,1,0:T(8,128)(2,1)S(1)}, bf16[2,2,5,24,768]{4,3,2,1,0:T(8,128)(2,1)S(1)}, u32[]{:S(2)}, u32[]{:S(2)}) collective-permute-start(bf16[2,2,5,24,768]{4,3,2,1,0:T(8,128)(2,1)S(1)} %fusion.1), channel_id=1, source_target_pairs={{0,4},{1,5},{2,6},{3,7},{4,0},{5,1},{6,2},{7,3},{8,12},{9,13},{10,... | collective-permute-start | bytes 2211848 | tf_op jit(solution)/shard_map/ppermute | solution.py:425
  316.3 31.3 %collective-permute-start.12 = (bf16[2,2,5,24,768]{4,3,2,0,1:T(8,128)(2,1)}, bf16[2,2,5,24,768]{4,3,2,0,1:T(8,128)(2,1)S(1)}, u32[]{:S(2)}, u32[]{:S(2)}) collective-permute-start(bf16[2,2,5,24,768]{4,3,2,0,1:T(8,128)(2,1)} %fusion), channel_id=1, source_target_pairs={{0,1},{1,0},{2,3},{3,2},{4,5},{5,4},{6,7},{7,6},{8,9},{9,8},{10,11... | collective-permute-start | bytes 2211848 | tf_op jit(solution)/shard_map/ppermute | solution.py:425
  350.1 20.8 %copy-start.12 = (f32[2,16,768]{2,1,0:T(8,128)S(1)}, f32[2,16,768]{2,1,0:T(8,128)}, u32[]{:S(2)}) copy-start(f32[2,16,768]{2,1,0:T(8,128)} %get-tuple-element.191) | copy-start | bytes 294916
  369.4 18.8 %collective-permute-start.14 = (bf16[4,2,2,80,768]{4,3,2,1,0:T(8,128)(2,1)}, bf16[4,2,2,80,768]{4,3,2,1,0:T(8,128)(2,1)S(1)}, u32[]{:S(2)}, u32[]{:S(2)}) collective-permute-start(bf16[4,2,2,80,768]{4,3,2,1,0:T(8,128)(2,1)} %get-tuple-element.185), channel_id=1, source_target_pairs={{0,2},{1,3},{2,0},{3,1},{4,6},{5,7},{6,4},{7,5},{8,10},{9,11},{10,... | collective-permute-start | bytes 5898248 | tf_op jit(solution)/shard_map/ppermute | solution.py:425
  369.5 11.8 %collective-permute-start.22 = (bf16[2,5,24,768]{3,2,1,0:T(8,128)(2,1)S(1)}, bf16[2,5,24,768]{3,2,1,0:T(8,128)(2,1)S(1)}, u32[]{:S(2)}, u32[]{:S(2)}) collective-permute-start(bf16[2,5,24,768]{3,2,1,0:T(8,128)(2,1)S(1)} %get-tuple-element.315), channel_id=1, source_target_pairs={{0,4},{1,5},{2,6},{3,7},{4,0},{5,1},{6,2},{7,3},{8,12},{9,13},{10,... | collective-permute-start | bytes 1105928 | tf_op jit(solution)/shard_map/ppermute | solution.py:425
  371.6 16.6 %copy-start.5 = (bf16[4,2,2,80,768]{4,3,2,1,0:T(8,128)(2,1)S(1)}, bf16[4,2,2,80,768]{4,3,2,1,0:T(8,128)(2,1)}, u32[]{:S(2)}) copy-start(bf16[4,2,2,80,768]{4,3,2,1,0:T(8,128)(2,1)} %get-tuple-element.184) | copy-start | bytes 5898244
  371.6 12.8 %collective-permute-start.24 = (bf16[2,5,24,768]{3,2,1,0:T(8,128)(2,1)S(1)}, bf16[2,5,24,768]{3,2,1,0:T(8,128)(2,1)S(1)}, u32[]{:S(2)}, u32[]{:S(2)}) collective-permute-start(bf16[2,5,24,768]{3,2,1,0:T(8,128)(2,1)S(1)} %get-tuple-element.316), channel_id=1, source_target_pairs={{0,1},{1,0},{2,3},{3,2},{4,5},{5,4},{6,7},{7,6},{8,9},{9,8},{10,11... | collective-permute-start | bytes 1105928 | tf_op jit(solution)/shard_map/ppermute | solution.py:425
  381.4 21.8 %collective-permute-start.23 = (bf16[5,24,768]{2,1,0:T(8,128)(2,1)S(1)}, bf16[5,24,768]{2,1,0:T(8,128)(2,1)S(1)}, u32[]{:S(2)}, u32[]{:S(2)}) collective-permute-start(bf16[5,24,768]{2,1,0:T(8,128)(2,1)S(1)} %fusion.20), channel_id=1, source_target_pairs={{0,8},{1,9},{2,10},{3,11},{4,12},{5,13},{6,14},{7,15},{8,0},{9,1},... | collective-permute-start | bytes 552968 | tf_op jit(solution)/shard_map/ppermute | solution.py:425
  384.5 18.7 %collective-permute-start.25 = (bf16[5,24,768]{2,1,0:T(8,128)(2,1)S(1)}, bf16[5,24,768]{2,1,0:T(8,128)(2,1)S(1)}, u32[]{:S(2)}, u32[]{:S(2)}) collective-permute-start(bf16[5,24,768]{2,1,0:T(8,128)(2,1)S(1)} %get-tuple-element.298), channel_id=1, source_target_pairs={{0,16},{1,17},{2,18},{3,19},{4,20},{5,21},{6,22},{7,23},{8,24},{9,... | collective-permute-start | bytes 552968 | tf_op jit(solution)/shard_map/ppermute | solution.py:425
  386.3 16.9 %collective-permute-start.26 = (bf16[5,24,768]{2,1,0:T(8,128)(2,1)S(1)}, bf16[5,24,768]{2,1,0:T(8,128)(2,1)S(1)}, u32[]{:S(2)}, u32[]{:S(2)}) collective-permute-start(bf16[5,24,768]{2,1,0:T(8,128)(2,1)S(1)} %get-tuple-element.299), channel_id=1, source_target_pairs={{0,24},{1,25},{2,26},{3,27},{4,28},{5,29},{6,30},{7,31},{8,16},{9,... | collective-permute-start | bytes 552968 | tf_op jit(solution)/shard_map/ppermute | solution.py:425
  388.3 2.4 copy-start.1
  388.3 11.1 %collective-permute-start.17 = (bf16[2,2,80,768]{3,2,1,0:T(8,128)(2,1)S(1)}, bf16[2,2,80,768]{3,2,1,0:T(8,128)(2,1)S(1)}, u32[]{:S(2)}, u32[]{:S(2)}) collective-permute-start(bf16[2,2,80,768]{3,2,1,0:T(8,128)(2,1)S(1)} %fusion.6), channel_id=1, source_target_pairs={{0,4},{1,5},{2,6},{3,7},{4,0},{5,1},{6,2},{7,3},{8,12},{9,13},{10,... | collective-permute-start | bytes 1474568 | tf_op jit(solution)/shard_map/ppermute | solution.py:425
  388.9 11.5 %collective-permute-start.15 = (bf16[2,2,80,768]{3,2,0,1:T(8,128)(2,1)S(1)}, bf16[2,2,80,768]{3,2,0,1:T(8,128)(2,1)S(1)}, u32[]{:S(2)}, u32[]{:S(2)}) collective-permute-start(bf16[2,2,80,768]{3,2,0,1:T(8,128)(2,1)S(1)} %fusion.5), channel_id=1, source_target_pairs={{0,1},{1,0},{2,3},{3,2},{4,5},{5,4},{6,7},{7,6},{8,9},{9,8},{10,11... | collective-permute-start | bytes 1474568 | tf_op jit(solution)/shard_map/ppermute | solution.py:425
  399.6 8.5 %collective-permute-start.18 = (bf16[2,80,768]{2,1,0:T(8,128)(2,1)S(1)}, bf16[2,80,768]{2,1,0:T(8,128)(2,1)S(1)}, u32[]{:S(2)}, u32[]{:S(2)}) collective-permute-start(bf16[2,80,768]{2,1,0:T(8,128)(2,1)S(1)} %fusion.16), channel_id=1, source_target_pairs={{0,1},{1,0},{2,3},{3,2},{4,5},{5,4},{6,7},{7,6},{8,9},{9,8},{10,11... | collective-permute-start | bytes 737288 | tf_op jit(solution)/shard_map/ppermute | solution.py:425
  400.3 3.0 copy-start
  400.5 7.6 %collective-permute-start.16 = (bf16[2,80,768]{2,1,0:T(8,128)(2,1)S(1)}, bf16[2,80,768]{2,1,0:T(8,128)(2,1)S(1)}, u32[]{:S(2)}, u32[]{:S(2)}) collective-permute-start(bf16[2,80,768]{2,1,0:T(8,128)(2,1)S(1)} %fusion.15), channel_id=1, source_target_pairs={{0,4},{1,5},{2,6},{3,7},{4,0},{5,1},{6,2},{7,3},{8,12},{9,13},{10,... | collective-permute-start | bytes 737288 | tf_op jit(solution)/shard_map/ppermute | solution.py:425
  408.2 16.6 %collective-permute-start.19 = (bf16[80,768]{1,0:T(8,128)(2,1)S(1)}, bf16[80,768]{1,0:T(8,128)(2,1)S(1)}, u32[]{:S(2)}, u32[]{:S(2)}) collective-permute-start(bf16[80,768]{1,0:T(8,128)(2,1)S(1)} %fusion.21), channel_id=1, source_target_pairs={{0,8},{1,9},{2,10},{3,11},{4,12},{5,13},{6,14},{7,15},{8,0},{9,1},... | collective-permute-start | bytes 368648 | tf_op jit(solution)/shard_map/ppermute | solution.py:425
  411.8 13.0 %collective-permute-start.20 = (bf16[80,768]{1,0:T(8,128)(2,1)S(1)}, bf16[80,768]{1,0:T(8,128)(2,1)S(1)}, u32[]{:S(2)}, u32[]{:S(2)}) collective-permute-start(bf16[80,768]{1,0:T(8,128)(2,1)S(1)} %get-tuple-element.194), channel_id=1, source_target_pairs={{0,16},{1,17},{2,18},{3,19},{4,20},{5,21},{6,22},{7,23},{8,24},{9,... | collective-permute-start | bytes 368648 | tf_op jit(solution)/shard_map/ppermute | solution.py:425
  411.8 13.0 %collective-permute-start.21 = (bf16[80,768]{1,0:T(8,128)(2,1)S(1)}, bf16[80,768]{1,0:T(8,128)(2,1)S(1)}, u32[]{:S(2)}, u32[]{:S(2)}) collective-permute-start(bf16[80,768]{1,0:T(8,128)(2,1)S(1)} %get-tuple-element.195), channel_id=1, source_target_pairs={{0,24},{1,25},{2,26},{3,27},{4,28},{5,29},{6,30},{7,31},{8,16},{9,... | collective-permute-start | bytes 368648 | tf_op jit(solution)/shard_map/ppermute | solution.py:425
  (4 other events, 3.8 us)
Sparse Core Ops, SparseCore 0:
  11.6 99.3 all-gather.2
  305.6 117.5 reduce-scatter.1

commit v6 on v5

--- a/solution.py
+++ b/solution.py
@@ -505,15 +505,15 @@
                 send(2 + j, i, dc, (buf, j), (buf, 2 + j))
 
 
-def pack_first(wq, wk, wv, vec, bup, out):
+def pack_first(wq, wk, wv, wo, vec, bup, out):
     blocks = [vec[8 * c : 8 * c + 8, :] for c in range(3)] + [jnp.broadcast_to(bup[...], (8, 128))]
     width = out.shape[1]
     tail = jnp.concatenate(blocks + [jnp.zeros((8, width - 512), F32)], axis=1)
-    out[...] = jnp.concatenate([w[...].astype(F32) for w in (wq, wk, wv)] + [tail], axis=0).astype(BF16)
+    out[...] = jnp.concatenate([w[...].astype(F32) for w in (wq, wk, wv, wo)] + [tail], axis=0).astype(BF16)
 
 
 def assemble_first(me, *refs):
-    bufs, (wq, wk, wv, vec, bup, small) = refs[:8], refs[8:]
+    bufs, (wq, wk, wv, wo, vec, bup, small) = refs[:8], refs[8:]
     mx = me[3]
 
     def emit(dp, near, far):
@@ -522,13 +522,13 @@
         low = jnp.where(mx == 0, n, f)
         high = jnp.where(mx == 0, f, n)
         at = pl.ds(pl.multiple_of(dp * 48, 16), 48)
-        for w, ref in enumerate((wq, wk, wv)):
+        for w, ref in enumerate((wq, wk, wv, wo)):
             ref[at, :] = jnp.concatenate(
                 [low[UNIT * w : UNIT * (w + 1)], high[UNIT * w : UNIT * (w + 1)]], axis=0
             ).astype(BF16)
         for x, rows in enumerate((low, high)):
             for c in range(4):
-                small[dp * 2 + x, 8 * c : 8 * c + 8, :] = rows[3 * UNIT :, 128 * c : 128 * c + 128]
+                small[dp * 2 + x, 8 * c : 8 * c + 8, :] = rows[4 * UNIT :, 128 * c : 128 * c + 128]
 
     unit_pairs(me, bufs, emit)
     for idx in range(small.shape[0]):
@@ -536,17 +536,14 @@
         bup[:, 4 * UNIT * idx : 4 * UNIT * (idx + 1)] = small[idx, 24:25, : 4 * UNIT]
 
 
-def assemble_rest(units, wo, wup, wdown):
+def assemble_rest(units, wup, wdown):
     count = units.shape[0]
-    width = wo.shape[1]
-    for w in range(5):
+    width = units.shape[3]
+    for w in range(4):
         rows = jnp.concatenate([units[i, w].astype(F32) for i in range(count)], axis=0).astype(BF16)
-        if w == 0:
-            wo[...] = rows
-        else:
-            wup[:, (w - 1) * width : w * width] = rows
+        wup[:, w * width : (w + 1) * width] = rows
     for i in range(0, count):
-        rows = jnp.concatenate([units[i, w].astype(F32) for w in range(5, 9)], axis=0)
+        rows = jnp.concatenate([units[i, w].astype(F32) for w in range(4, 8)], axis=0)
         wdown[4 * UNIT * i : 4 * UNIT * (i + 1), :] = rows.astype(BF16)
 
 
@@ -558,20 +555,19 @@
         grid=(devices // step,),
         in_specs=[pl.BlockSpec((step, blocks, rows, width), lambda i: (i, 0, 0, 0))],
         out_specs=[
-            pl.BlockSpec((step * rows, width), lambda i: (i, 0)),
             pl.BlockSpec((step * rows, ff), lambda i: (i, 0)),
             pl.BlockSpec((step * rows * 4, width), lambda i: (i, 0)),
         ],
-        out_shape=[jax.ShapeDtypeStruct(d, BF16) for d in ((width, width), (width, ff), (ff, width))],
+        out_shape=[jax.ShapeDtypeStruct(d, BF16) for d in ((width, ff), (ff, width))],
         compiler_params=params(),
         name="assemble_rest",
     )(units)
 
 
-def call_pack_first(wq, wk, wv, vec, bup):
+def call_pack_first(wq, wk, wv, wo, vec, bup):
     return pl.pallas_call(
-        pack_first, out_shape=jax.ShapeDtypeStruct((3 * UNIT + 8, wq.shape[1]), BF16), name="pack_first"
-    )(wq, wk, wv, vec, bup)
+        pack_first, out_shape=jax.ShapeDtypeStruct((4 * UNIT + 8, wq.shape[1]), BF16), name="pack_first"
+    )(wq, wk, wv, wo, vec, bup)
 
 
 def call_assemble(body, me, bufs, outs, name, scratch=()):
@@ -784,19 +780,19 @@
     vec = jnp.pad(vec, ((0, 6), (0, 128 - UNIT))).astype(F32)
     hidden = jnp.pad(bup[None], ((0, 0), (0, 128 - 4 * UNIT))).astype(F32)
     up_blocks = wup.reshape(UNIT, ff // width, width).transpose(1, 0, 2)
-    units = jnp.concatenate([wo[None], up_blocks, wdown.reshape(4, UNIT, width)], axis=0)
+    units = jnp.concatenate([up_blocks, wdown.reshape(4, UNIT, width)], axis=0)
     units = lax.all_gather(units, AXES, axis=0)
-    a, b = gather_near(*gather_z(call_pack_first(wq, wk, wv, vec, hidden)))
+    a, b = gather_near(*gather_z(call_pack_first(wq, wk, wv, wo, vec, hidden)))
     rows = tuple(lax.optimization_barrier(after(r.transpose(0, 2, 1, 3), b).transpose(0, 2, 1, 3)) for r in rows)
     far = gather_far(a, b)
     *far, tokens, cotangent = lax.optimization_barrier((*far, *rows))
     first = gather_core(tuple(far))
     square = ((width, width), BF16)
-    wq, wk, wv, vec, bup = call_assemble(
-        assemble_first, me, first, [square] * 3 + [((1, 24, width), F32), ((1, ff), F32)],
+    wq, wk, wv, wo, vec, bup = call_assemble(
+        assemble_first, me, first, [square] * 4 + [((1, 24, width), F32), ((1, ff), F32)],
         "assemble_first", [pltpu.VMEM((width // UNIT, 32, 128), F32)],
     )
-    return (wq, wk, wv, vec, bup), units, (tokens, cotangent)
+    return (wq, wk, wv, vec, bup), (wo, units), (tokens, cotangent)
 
 
 def gather_plain(shards):
@@ -845,7 +841,7 @@
         part = call_attend_forward(s, tokens, mem, wq, wk, wv, vec)
         if s == 0:
             if planned:
-                rest = call_assemble_rest(after(rest, part[0]), 4 * width)
+                rest = (rest[0], *call_assemble_rest(after(rest[1], part[0]), 4 * width))
             wo, wup, wdown = rest
         o = part[5]
         y, mem, *more = call_feed_forward(s, segment_count, tokens, mem, o, wo, wup, wdown, vec, bup, y)

time: 443 us -> 441 us (level)
    ppermute x27, waiting for transfers between devices: 53.3 us -> 62.5 us  [swap(): return lax.ppermute(array, AXES, pairs)]
    all_gather x1, waiting for transfers between devices: 20 us -> 11.8 us  [gather_weights(): units = lax.all_gather(units, AXES, axis=0)]
  transfers between devices with their start and end apart: 29 -> 29, of which waited for: 14 -> 15; matrix products, arithmetic and copies ran while one was open for 7% -> 7% of each run, Pallas kernels for 17% -> 17%
where the time goes in v6:
time: 441 us; the launch traced here: 432 us
  Pallas kernels  268 us (61%)
  waiting for transfers between devices  82.9 us (19%)
  starting transfers between devices  32.1 us (7%)
  local copies, waits for them, and re-layouts  21.6 us (5%)
  between operations  15.1 us (3%)
  other arithmetic  13.2 us (3%)
    pallas_call x8, Pallas kernels, launch(): pl.pallas_call(run if into else body, grid=grid, in_specs=list(in_specs)...  198 us
    ppermute x27, waiting for transfers between devices, swap(): return lax.ppermute(array, AXES, pairs)  62.5 us
    ppermute x27, starting transfers between devices, swap(): return lax.ppermute(array, AXES, pairs)  32 us
    pallas_call x1, Pallas kernels, call_product_up(): pl.pallas_call(functools.partial(product_up, segments), grid_spec=pltpu.P...  20.7 us
    pallas_call x1, Pallas kernels, call_product_first(): pl.pallas_call(functools.partial(product_first, segments), grid_spec=pltp...  19.2 us
    pallas_call x1, Pallas kernels, call_weight_product(): pl.pallas_call(functools.partial(weight_product, parts), grid=(n_left //...  14.6 us
    all_gather x1, waiting for transfers between devices, gather_weights(): units = lax.all_gather(units, AXES, axis=0)  11.8 us
  transfers between devices with their start and end apart: 29, of which 15 were waited for; matrix products, arithmetic and copies ran while one was open for 7% of the time, Pallas kernels for 17%

profile of v6, /device:TPU:0, one launch (start us, length us, event | category | flops | bytes accessed | tf_op | source)
XLA Modules:
  0.0 432.5 jit_solution(14885961170716985207)
XLA Ops:
  11.7 1.5 pack_first.1
  13.2 3.0 collective-permute-start
  16.3 2.5 collective-permute-start.4
  18.9 2.2 collective-permute-done
  22.0 1.6 collective-permute-start.1
  23.6 3.8 collective-permute-done.4
  27.4 11.8 %collective-permute-done.3 = bf16[104,768]{1,0:T(8,128)(2,1)S(1)} collective-permute-done((bf16[104,768]{1,0:T(8,128)(2,1)}, bf16[104,768]{1,0:T(8,128)(2,1)S(1)}, u32[]{:S(2)}, u32[]{:S(2)}) %collective-permute-start.3) | collective-permute-done | bytes 159776 | tf_op jit(solution)/shard_map/ppermute | solution.py:425
  39.3 1.6 collective-permute-start.5
  42.5 9.4 %collective-permute-done.5 = bf16[2,104,768]{2,1,0:T(8,128)(2,1)S(1)} collective-permute-done((bf16[2,104,768]{2,1,0:T(8,128)(2,1)S(1)}, bf16[2,104,768]{2,1,0:T(8,128)(2,1)S(1)}, u32[]{:S(2)}, u32[]{:S(2)}) %collective-permute-start.5) | collective-permute-done | bytes 319520 | tf_op jit(solution)/shard_map/ppermute | solution.py:425
  52.0 1.5 collective-permute-start.6
  53.4 2.1 copy.183
  55.5 2.1 copy.182
  57.5 10.8 %collective-permute-done.2.refs_1_ = bf16[4,104,768]{2,1,0:T(8,128)(2,1)S(1)} collective-permute-done((bf16[4,104,768]{2,1,0:T(8,128)(2,1)S(1)}, bf16[4,104,768]{2,1,0:T(8,128)(2,1)S(1)}, u32[]{:S(2)}, u32[]{:S(2)}) %collective-permute-start.2) | collective-permute-done | bytes 639008 | tf_op jit(solution)/shard_map/ppermute | solution.py:425
  73.4 6.2 %assemble_first.1 = (bf16[768,768]{1,0:T(8,128)(2,1)}, bf16[768,768]{1,0:T(8,128)(2,1)}, bf16[768,768]{1,0:T(8,128)(2,1)}, bf16[768,768]{1,0:T(8,128)(2,1)}, f32[1,24,768]{2,1,0:T(8,128)}, /*index=5*/f32[1,3072]{1,0:T(1,128)}) custom-call(s32[4]{0:T(128)} %pad_add_fusion.me, bf16[4,104,768]{2,1,0:T(8,128)(2,1)} %copy-done.5, bf16[4,104,768]{2,1,0:T(8,128)(2,1)} %copy-done.9, ...), custom_call_target="tpu_custom_call" | custom-call | tf_op jit(solution)/shard_map/assemble_first/pallas_call | solution.py:575
  79.6 18.3 %attend_forward.2 = (bf16[2,512,768]{2,1,0:T(8,128)(2,1)}, bf16[2,512,768]{2,1,0:T(8,128)(2,1)}, bf16[2,512,768]{2,1,0:T(8,128)(2,1)}, bf16[2,512,768]{2,1,0:T(8...) custom-call(bf16[2,2,502,768]{3,2,1,0:T(8,128)(2,1)} %copy.183, ...), custom_call_target="tpu_custom_call" | custom-call | flops 10066329600 | bytes 23592960 | tf_op jit(solution)/shard_map/attend_forward/pallas_call | solution.py:290
  97.9 11.8 %all-gather.3.cloned.1.call-done = bf16[256,24,768]{2,1,0:T(8,128)(2,1)} async-done(((bf16[8,24,768]{2,1,0:T(8,128)(2,1)}), bf16[256,24,768]{2,1,0:T(8,128)(2,1)}) %all-gather.3.cloned.1.call-update) | async-done | bytes 9437200 | tf_op jit(solution)/shard_map/all_gather | solution.py:784
  109.7 7.6 %assemble_rest.1 = (bf16[768,3072]{1,0:T(8,128)(2,1)}, bf16[3072,768]{1,0:T(8,128)(2,1)}) custom-call(bf16[32,8,24,768]{3,2,1,0:T(8,128)(2,1)} %bitcast.145), custom_call_target="tpu_custom_call" | custom-call | tf_op jit(solution)/shard_map/assemble_rest/pallas_call | solution.py:553
  117.3 29.6 %feed_forward.2 = (bf16[2,2,502,768]{3,2,1,0:T(8,128)(2,1)}, f32[2,16,768]{2,1,0:T(8,128)}, bf16[2,512,768]{2,1,0:T(8,128)(2,1)}, f32[2,512,128]{2,1,0:T(8,128)}...) custom-call(s32[2]{0:T(128)} %refs_0_.11, ...), custom_call_target="tpu_custom_call" | custom-call | flops 10871635968 | bytes 23592960 | tf_op jit(solution)/shard_map/feed_forward/pallas_call | solution.py:290
  146.9 18.2 %attend_forward.3 = (bf16[2,512,768]{2,1,0:T(8,128)(2,1)}, bf16[2,512,768]{2,1,0:T(8,128)(2,1)}, bf16[2,512,768]{2,1,0:T(8,128)(2,1)}, bf16[2,512,768]{2,1,0:T(8...) custom-call(bf16[2,2,502,768]{3,2,1,0:T(8,128)(2,1)} %copy.183, ...), custom_call_target="tpu_custom_call" | custom-call | flops 10066329600 | bytes 23592960 | tf_op jit(solution)/shard_map/attend_forward/pallas_call | solution.py:290
  165.1 29.3 %feed_forward.3 = (bf16[2,2,502,768]{3,2,1,0:T(8,128)(2,1)}, f32[2,16,768]{2,1,0:T(8,128)}, bf16[2,512,768]{2,1,0:T(8,128)(2,1)}, f32[2,512,128]{2,1,0:T(8,128)}...) custom-call(s32[2]{0:T(128)} %refs_0_.11, ...), custom_call_target="tpu_custom_call", output_to_operand_aliasing={{0}: (9, {})} | custom-call | flops 10871635968 | bytes 23592960 | tf_op jit(solution)/shard_map/feed_forward/pallas_call | solution.py:290
  194.4 22.1 %feed_backward.2 = (bf16[2,512,768]{2,1,0:T(8,128)(2,1)}, bf16[2,512,3072]{2,1,0:T(8,128)(2,1)}, f32[2,512,768]{2,1,0:T(8,128)}, bf16[2,512,768]{2,1,0:T(8,128)(...) custom-call(s32[2]{0:T(128)} %refs_0_.11, bf16[2,2,502,768]{3,2,1,0:T(8,128)(2,1)} %copy.182, ...), custom_call_target="tpu_custom_call" | custom-call | flops 9663676416 | bytes 23592960 | tf_op jit(solution)/shard_map/feed_backward/pallas_call | solution.py:290
  216.5 28.7 %attend_backward.2 = (bf16[2,2,502,768]{3,2,1,0:T(8,128)(2,1)}, f32[2,16,768]{2,1,0:T(8,128)}, bf16[2,512,768]{2,1,0:T(8,128)(2,1)}, bf16[2,512,768]{2,1,0:T(8,1...) custom-call(s32[2]{0:T(128)} %refs_0_.11, f32[2,16,768]{2,1,0:T(8,128)} %pad_convert_fusion.refs_2_.refs_1_, ...), custom_call_target="tpu_custom_call" | custom-call | flops 17716740096 | bytes 31457280 | tf_op jit(solution)/shard_map/attend_backward/pallas_call | solution.py:290
  245.2 22.3 %feed_backward.3 = (bf16[2,512,768]{2,1,0:T(8,128)(2,1)}, bf16[2,512,3072]{2,1,0:T(8,128)(2,1)}, f32[2,512,768]{2,1,0:T(8,128)}, bf16[2,512,768]{2,1,0:T(8,128)(...) custom-call(s32[2]{0:T(128)} %refs_0_.11, bf16[2,2,502,768]{3,2,1,0:T(8,128)(2,1)} %copy.182, ...), custom_call_target="tpu_custom_call" | custom-call | flops 9663676416 | bytes 23592960 | tf_op jit(solution)/shard_map/feed_backward/pallas_call | solution.py:290
  267.6 14.6 %weight_product.1 = bf16[3072,768]{1,0:T(8,128)(2,1)} custom-call(bf16[2,512,3072]{2,1,0:T(8,128)(2,1)} %get-tuple-element.151.refs_0_, bf16[2,512,3072]{2,1,0:T(8,128)(2,1)} %get-tuple-element.152.refs_1_, bf16[2,512,768]{2,1,0:T(8,128)(2,1)} %get-tuple-element.153.refs_2_, bf16[2,512,768]{2,1,0:T(8,128)(2,1)} %get-tuple-element.154.refs_3_), custom_call_target="tpu_custom_call" | custom-call | flops 9663676416 | bytes 15728640 | tf_op jit(solution)/shard_map/weight_product/pallas_call | solution.py:397
  282.2 20.7 %product_up.1 = (bf16[4,2,2,5,24,768]{5,4,3,2,1,0:T(8,128)(2,1)}, bf16[4,2,2,5,24,768]{5,4,3,2,1,0:T(8,128)(2,1)}) custom-call(s32[4]{0:T(128)} %pad_add_fusion.me, bf16[2,512,768]{2,1,0:T(8,128)(2,1)} %get-tuple-element.155.refs_3_.refs_0_.refs_8_, bf16[2,512,768]{2,1,0:T(8,128)(2,1)} %get-tuple-element.129.refs_3_.refs_8_.refs_1_, ...), custom_call_target="tpu_custom_call" | custom-call | flops 12079595520 | bytes 27918336 | tf_op jit(solution)/shard_map/product_up/pallas_call | solution.py:702
  303.2 5.4 %collective-permute-done.11 = bf16[4,2,2,5,24,768]{5,4,3,2,1,0:T(8,128)(2,1)} collective-permute-done((bf16[4,2,2,5,24,768]{5,4,3,2,1,0:T(8,128)(2,1)}, bf16[4,2,2,5,24,768]{5,4,3,2,1,0:T(8,128)(2,1)}, u32[]{:S(2)}, u32[]{:S(2)}) %collective-permute-start.11) | collective-permute-done | bytes 2949152 | tf_op jit(solution)/shard_map/ppermute | solution.py:425
  308.6 1.5 fusion.23
  310.1 1.3 fusion.1
  311.4 1.5 collective-permute-start.13
  314.5 29.1 %attend_backward.3 = (bf16[2,2,502,768]{3,2,1,0:T(8,128)(2,1)}, f32[2,16,768]{2,1,0:T(8,128)}, bf16[2,512,768]{2,1,0:T(8,128)(2,1)}, bf16[2,512,768]{2,1,0:T(8,1...) custom-call(s32[2]{0:T(128)} %refs_0_.11, ...), custom_call_target="tpu_custom_call", output_to_operand_aliasing={{0}: (14, {})} | custom-call | flops 17716740096 | bytes 31457280 | tf_op jit(solution)/shard_map/attend_backward/pallas_call | solution.py:290
  343.7 1.6 bitcast_add_fusion
  346.2 1.6 bitcast_add_fusion.1
  347.8 19.2 %product_first.1 = (bf16[4,2,2,80,768]{4,3,2,1,0:T(8,128)(2,1)}, bf16[4,2,2,80,768]{4,3,2,1,0:T(8,128)(2,1)}) custom-call(s32[4]{0:T(128)} %pad_add_fusion.me, f32[2,8,768]{2,1,0:T(8,128)} %get-tuple-element.143.refs_0_, f32[2,8,768]{2,1,0:T(8,128)} %get-tuple-element.170.refs_1_, f32[2,8,768]{2,1,0:T(8,128)} %get-tuple-element.171.refs_2_, ...), custom_call_target="tpu_custom_call" | custom-call | flops 7247757312 | bytes 16121856 | tf_op jit(solution)/shard_map/product_first/pallas_call | solution.py:750
  367.2 1.5 collective-permute-start.22
  369.5 9.4 %collective-permute-done.22 = bf16[2,5,24,768]{3,2,1,0:T(8,128)(2,1)S(1)} collective-permute-done((bf16[2,5,24,768]{3,2,1,0:T(8,128)(2,1)S(1)}, bf16[2,5,24,768]{3,2,1,0:T(8,128)(2,1)S(1)}, u32[]{:S(2)}, u32[]{:S(2)}) %collective-permute-start.22) | collective-permute-done | bytes 368672 | tf_op jit(solution)/shard_map/ppermute | solution.py:425
  378.9 1.3 collective-permute-start.23
  380.2 1.9 collective-permute-done.24
  382.2 1.9 collective-permute-start.25
  384.1 1.9 collective-permute-start.26
  386.8 1.8 collective-permute-start.15
  388.6 4.0 copy.185
  392.6 4.7 %collective-permute-done.17 = bf16[2,2,80,768]{3,2,1,0:T(8,128)(2,1)S(1)} collective-permute-done((bf16[2,2,80,768]{3,2,1,0:T(8,128)(2,1)S(1)}, bf16[2,2,80,768]{3,2,1,0:T(8,128)(2,1)S(1)}, u32[]{:S(2)}, u32[]{:S(2)}) %collective-permute-start.17) | collective-permute-done | bytes 491552 | tf_op jit(solution)/shard_map/ppermute | solution.py:425
  398.6 2.6 collective-permute-start.16
  401.3 4.0 copy.184
  406.2 3.2 collective-permute-start.19
  409.4 2.4 collective-permute-start.21
  412.5 8.6 %reduce-scatter.2.cloned.1.call-done = bf16[96,768]{1,0:T(8,128)(2,1)} async-done(((bf16[3072,768]{1,0:T(8,128)(2,1)}), bf16[96,768]{1,0:T(8,128)(2,1)}) %reduce-scatter.2.cloned.1.call-update) | async-done | bytes 147472 | tf_op jit(solution)/shard_map/reduce_scatter | solution.py:869
  421.1 1.6 convert_element_type.237
  (126 shorter events, 22.0 us)
Async XLA Ops:
  7.2 3.1 copy-start.22
  7.2 3.1 copy-start.21
  7.2 3.1 copy-start.20
  7.2 3.1 copy-start.19
  7.2 3.1 copy-start.18
  7.2 3.1 copy-start.17
  7.3 3.1 copy-start.16
  7.3 3.1 copy-start.15
  7.3 3.3 copy-start.23
  7.3 102.4 %all-gather.3.cloned.1.call-start = ((), (), s32[]{:S(2)}) async-start(), calls=%async_computation.2 | async-start | bytes 9732096 | tf_op jit(solution)/shard_map/all_gather | solution.py:784
  10.3 410.8 %reduce-scatter.2.cloned.1.call-start = ((), (), s32[]{:S(2)}) async-start(), calls=%async_computation.1 | async-start | bytes 4866048 | tf_op jit(solution)/shard_map/reduce_scatter | solution.py:869
  13.2 40.2 %copy-start.2 = (bf16[2,2,502,768]{3,1,2,0:T(2,128)(2,1)S(1)}, bf16[2,2,502,768]{3,1,2,0:T(2,128)(2,1)}, u32[]{:S(2)}) copy-start(bf16[2,2,502,768]{3,1,2,0:T(2,128)(2,1)} %param.20) | copy-start | bytes 9252868
  13.2 7.9 %collective-permute-start = (bf16[104,768]{1,0:T(8,128)(2,1)}, bf16[104,768]{1,0:T(8,128)(2,1)S(1)}, u32[]{:S(2)}, u32[]{:S(2)}) collective-permute-start(bf16[104,768]{1,0:T(8,128)(2,1)} %pack_first.1), channel_id=1, source_target_pairs={{0,8},{1,9},{2,10},{3,11},{4,12},{5,13},{6,14},{7,15},{8,0},{9,1},... | collective-permute-start | bytes 479240 | tf_op jit(solution)/shard_map/ppermute | solution.py:425
  16.3 11.2 %collective-permute-start.4 = (bf16[104,768]{1,0:T(8,128)(2,1)}, bf16[104,768]{1,0:T(8,128)(2,1)S(1)}, u32[]{:S(2)}, u32[]{:S(2)}) collective-permute-start(bf16[104,768]{1,0:T(8,128)(2,1)} %pack_first.1), channel_id=1, source_target_pairs={{0,24},{1,25},{2,26},{3,27},{4,28},{5,29},{6,30},{7,31},{8,16},{9,... | collective-permute-start | bytes 479240 | tf_op jit(solution)/shard_map/ppermute | solution.py:425
  18.7 20.5 %collective-permute-start.3 = (bf16[104,768]{1,0:T(8,128)(2,1)}, bf16[104,768]{1,0:T(8,128)(2,1)S(1)}, u32[]{:S(2)}, u32[]{:S(2)}) collective-permute-start(bf16[104,768]{1,0:T(8,128)(2,1)} %pack_first.1), channel_id=1, source_target_pairs={{0,16},{1,17},{2,18},{3,19},{4,20},{5,21},{6,22},{7,23},{8,24},{9,... | collective-permute-start | bytes 479240 | tf_op jit(solution)/shard_map/ppermute | solution.py:425
  22.0 18.8 %collective-permute-start.1 = (bf16[2,104,768]{2,1,0:T(8,128)(2,1)S(1)}, bf16[2,104,768]{2,1,0:T(8,128)(2,1)S(1)}, u32[]{:S(2)}, u32[]{:S(2)}) collective-permute-start(bf16[2,104,768]{2,1,0:T(8,128)(2,1)S(1)} %pad_maximum_fusion.2), channel_id=1, source_target_pairs={{0,4},{1,5},{2,6},{3,7},{4,0},{5,1},{6,2},{7,3},{8,12},{9,13},{10,... | collective-permute-start | bytes 958472 | tf_op jit(solution)/shard_map/ppermute | solution.py:425
  39.3 12.6 %collective-permute-start.5 = (bf16[2,104,768]{2,1,0:T(8,128)(2,1)S(1)}, bf16[2,104,768]{2,1,0:T(8,128)(2,1)S(1)}, u32[]{:S(2)}, u32[]{:S(2)}) collective-permute-start(bf16[2,104,768]{2,1,0:T(8,128)(2,1)S(1)} %pad_maximum_fusion.3), channel_id=1, source_target_pairs={{0,1},{1,0},{2,3},{3,2},{4,5},{5,4},{6,7},{7,6},{8,9},{9,8},{10,11... | collective-permute-start | bytes 958472 | tf_op jit(solution)/shard_map/ppermute | solution.py:425
  41.9 26.5 %copy-start.5 = (bf16[4,104,768]{2,1,0:T(8,128)(2,1)}, bf16[4,104,768]{2,1,0:T(8,128)(2,1)S(1)}, u32[]{:S(2)}) copy-start(bf16[4,104,768]{2,1,0:T(8,128)(2,1)S(1)} %pad_maximum_fusion.refs_0_) | copy-start | bytes 1916932
  41.9 26.5 %collective-permute-start.2 = (bf16[4,104,768]{2,1,0:T(8,128)(2,1)S(1)}, bf16[4,104,768]{2,1,0:T(8,128)(2,1)S(1)}, u32[]{:S(2)}, u32[]{:S(2)}) collective-permute-start(bf16[4,104,768]{2,1,0:T(8,128)(2,1)S(1)} %pad_maximum_fusion.refs_0_), channel_id=1, source_target_pairs={{0,1},{1,0},{2,3},{3,2},{4,5},{5,4},{6,7},{7,6},{8,9},{9,8},{10,11... | collective-permute-start | bytes 1916936 | tf_op jit(solution)/shard_map/ppermute | solution.py:425
  51.9 17.0 %copy-start.6 = (bf16[4,104,768]{2,1,0:T(8,128)(2,1)}, bf16[4,104,768]{2,1,0:T(8,128)(2,1)S(1)}, u32[]{:S(2)}) copy-start(bf16[4,104,768]{2,1,0:T(8,128)(2,1)S(1)} %pad_maximum_fusion.1.refs_2_) | copy-start | bytes 1916932
  51.9 3.5 copy-start.3
  52.0 16.4 %collective-permute-start.6 = (bf16[4,104,768]{2,1,0:T(8,128)(2,1)S(1)}, bf16[4,104,768]{2,1,0:T(8,128)(2,1)S(1)}, u32[]{:S(2)}, u32[]{:S(2)}) collective-permute-start(bf16[4,104,768]{2,1,0:T(8,128)(2,1)S(1)} %pad_maximum_fusion.1.refs_2_), channel_id=1, source_target_pairs={{0,4},{1,5},{2,6},{3,7},{4,0},{5,1},{6,2},{7,3},{8,12},{9,13},{10,... | collective-permute-start | bytes 1916936 | tf_op jit(solution)/shard_map/ppermute | solution.py:425
  55.5 14.0 %copy-start.12 = (bf16[2,10,768]{2,0,1:T(2,128)(2,1)S(1)}, bf16[2,10,768]{2,0,1:T(2,128)(2,1)}, u32[]{:S(2)}) copy-start(bf16[2,10,768]{2,0,1:T(2,128)(2,1)} %param.39) | copy-start | bytes 92164
  68.3 5.0 %copy-start.9 = (bf16[4,104,768]{2,1,0:T(8,128)(2,1)}, bf16[4,104,768]{2,1,0:T(8,128)(2,1)S(1)}, u32[]{:S(2)}) copy-start(bf16[4,104,768]{2,1,0:T(8,128)(2,1)S(1)} %collective-permute-done.2.refs_1_) | copy-start | bytes 1916932
  68.4 5.0 %copy-start.10 = (bf16[4,104,768]{2,1,0:T(8,128)(2,1)}, bf16[4,104,768]{2,1,0:T(8,128)(2,1)S(1)}, u32[]{:S(2)}) copy-start(bf16[4,104,768]{2,1,0:T(8,128)(2,1)S(1)} %collective-permute-done.6.refs_3_) | copy-start | bytes 1916932
  68.4 2.4 collective-permute-start.7
  68.4 3.1 collective-permute-start.8
  68.9 3.5 collective-permute-start.9
  69.0 4.4 %collective-permute-start.10 = (bf16[4,104,768]{2,1,0:T(8,128)(2,1)S(1)}, bf16[4,104,768]{2,1,0:T(8,128)(2,1)}, u32[]{:S(2)}, u32[]{:S(2)}) collective-permute-start(bf16[4,104,768]{2,1,0:T(8,128)(2,1)S(1)} %collective-permute-done.6.refs_3_), channel_id=1, source_target_pairs={{0,2},{1,3},{2,0},{3,1},{4,6},{5,7},{6,4},{7,5},{8,10},{9,11},{10,... | collective-permute-start | bytes 1916936 | tf_op jit(solution)/shard_map/ppermute | solution.py:425
  302.9 5.7 %collective-permute-start.11 = (bf16[4,2,2,5,24,768]{5,4,3,2,1,0:T(8,128)(2,1)}, bf16[4,2,2,5,24,768]{5,4,3,2,1,0:T(8,128)(2,1)}, u32[]{:S(2)}, u32[]{:S(2)}) collective-permute-start(bf16[4,2,2,5,24,768]{5,4,3,2,1,0:T(8,128)(2,1)} %get-tuple-element.162), channel_id=1, source_target_pairs={{0,2},{1,3},{2,0},{3,1},{4,6},{5,7},{6,4},{7,5},{8,10},{9,11},{10,... | collective-permute-start | bytes 8847368 | tf_op jit(solution)/shard_map/ppermute | solution.py:425
  303.2 6.9 %copy-start.4 = (bf16[4,2,2,5,24,768]{5,4,3,2,1,0:T(8,128)(2,1)S(1)}, bf16[4,2,2,5,24,768]{5,4,3,2,1,0:T(8,128)(2,1)}, u32[]{:S(2)}) copy-start(bf16[4,2,2,5,24,768]{5,4,3,2,1,0:T(8,128)(2,1)} %get-tuple-element.161) | copy-start | bytes 8847364
  311.4 32.3 %collective-permute-start.13 = (bf16[2,2,5,24,768]{4,3,2,1,0:T(8,128)(2,1)S(1)}, bf16[2,2,5,24,768]{4,3,2,1,0:T(8,128)(2,1)S(1)}, u32[]{:S(2)}, u32[]{:S(2)}) collective-permute-start(bf16[2,2,5,24,768]{4,3,2,1,0:T(8,128)(2,1)S(1)} %fusion.1), channel_id=1, source_target_pairs={{0,4},{1,5},{2,6},{3,7},{4,0},{5,1},{6,2},{7,3},{8,12},{9,13},{10,... | collective-permute-start | bytes 2211848 | tf_op jit(solution)/shard_map/ppermute | solution.py:425
  314.0 31.3 %collective-permute-start.12 = (bf16[2,2,5,24,768]{4,3,2,0,1:T(8,128)(2,1)}, bf16[2,2,5,24,768]{4,3,2,0,1:T(8,128)(2,1)S(1)}, u32[]{:S(2)}, u32[]{:S(2)}) collective-permute-start(bf16[2,2,5,24,768]{4,3,2,0,1:T(8,128)(2,1)} %fusion), channel_id=1, source_target_pairs={{0,1},{1,0},{2,3},{3,2},{4,5},{5,4},{6,7},{7,6},{8,9},{9,8},{10,11... | collective-permute-start | bytes 2211848 | tf_op jit(solution)/shard_map/ppermute | solution.py:425
  347.8 20.8 %copy-start.13 = (f32[2,16,768]{2,1,0:T(8,128)S(1)}, f32[2,16,768]{2,1,0:T(8,128)}, u32[]{:S(2)}) copy-start(f32[2,16,768]{2,1,0:T(8,128)} %get-tuple-element.191) | copy-start | bytes 294916
  367.1 19.0 %collective-permute-start.14 = (bf16[4,2,2,80,768]{4,3,2,1,0:T(8,128)(2,1)}, bf16[4,2,2,80,768]{4,3,2,1,0:T(8,128)(2,1)S(1)}, u32[]{:S(2)}, u32[]{:S(2)}) collective-permute-start(bf16[4,2,2,80,768]{4,3,2,1,0:T(8,128)(2,1)} %get-tuple-element.185), channel_id=1, source_target_pairs={{0,2},{1,3},{2,0},{3,1},{4,6},{5,7},{6,4},{7,5},{8,10},{9,11},{10,... | collective-permute-start | bytes 5898248 | tf_op jit(solution)/shard_map/ppermute | solution.py:425
  367.2 11.7 %collective-permute-start.22 = (bf16[2,5,24,768]{3,2,1,0:T(8,128)(2,1)S(1)}, bf16[2,5,24,768]{3,2,1,0:T(8,128)(2,1)S(1)}, u32[]{:S(2)}, u32[]{:S(2)}) collective-permute-start(bf16[2,5,24,768]{3,2,1,0:T(8,128)(2,1)S(1)} %get-tuple-element.315), channel_id=1, source_target_pairs={{0,4},{1,5},{2,6},{3,7},{4,0},{5,1},{6,2},{7,3},{8,12},{9,13},{10,... | collective-permute-start | bytes 1105928 | tf_op jit(solution)/shard_map/ppermute | solution.py:425
  369.3 16.8 %copy-start.7 = (bf16[4,2,2,80,768]{4,3,2,1,0:T(8,128)(2,1)S(1)}, bf16[4,2,2,80,768]{4,3,2,1,0:T(8,128)(2,1)}, u32[]{:S(2)}) copy-start(bf16[4,2,2,80,768]{4,3,2,1,0:T(8,128)(2,1)} %get-tuple-element.184) | copy-start | bytes 5898244
  369.3 12.8 %collective-permute-start.24 = (bf16[2,5,24,768]{3,2,1,0:T(8,128)(2,1)S(1)}, bf16[2,5,24,768]{3,2,1,0:T(8,128)(2,1)S(1)}, u32[]{:S(2)}, u32[]{:S(2)}) collective-permute-start(bf16[2,5,24,768]{3,2,1,0:T(8,128)(2,1)S(1)} %get-tuple-element.316), channel_id=1, source_target_pairs={{0,1},{1,0},{2,3},{3,2},{4,5},{5,4},{6,7},{7,6},{8,9},{9,8},{10,11... | collective-permute-start | bytes 1105928 | tf_op jit(solution)/shard_map/ppermute | solution.py:425
  378.9 22.2 %collective-permute-start.23 = (bf16[5,24,768]{2,1,0:T(8,128)(2,1)S(1)}, bf16[5,24,768]{2,1,0:T(8,128)(2,1)S(1)}, u32[]{:S(2)}, u32[]{:S(2)}) collective-permute-start(bf16[5,24,768]{2,1,0:T(8,128)(2,1)S(1)} %fusion.20), channel_id=1, source_target_pairs={{0,8},{1,9},{2,10},{3,11},{4,12},{5,13},{6,14},{7,15},{8,0},{9,1},... | collective-permute-start | bytes 552968 | tf_op jit(solution)/shard_map/ppermute | solution.py:425
  382.2 19.0 %collective-permute-start.25 = (bf16[5,24,768]{2,1,0:T(8,128)(2,1)S(1)}, bf16[5,24,768]{2,1,0:T(8,128)(2,1)S(1)}, u32[]{:S(2)}, u32[]{:S(2)}) collective-permute-start(bf16[5,24,768]{2,1,0:T(8,128)(2,1)S(1)} %get-tuple-element.298), channel_id=1, source_target_pairs={{0,16},{1,17},{2,18},{3,19},{4,20},{5,21},{6,22},{7,23},{8,24},{9,... | collective-permute-start | bytes 552968 | tf_op jit(solution)/shard_map/ppermute | solution.py:425
  384.1 17.1 %collective-permute-start.26 = (bf16[5,24,768]{2,1,0:T(8,128)(2,1)S(1)}, bf16[5,24,768]{2,1,0:T(8,128)(2,1)S(1)}, u32[]{:S(2)}, u32[]{:S(2)}) collective-permute-start(bf16[5,24,768]{2,1,0:T(8,128)(2,1)S(1)} %get-tuple-element.299), channel_id=1, source_target_pairs={{0,24},{1,25},{2,26},{3,27},{4,28},{5,29},{6,30},{7,31},{8,16},{9,... | collective-permute-start | bytes 552968 | tf_op jit(solution)/shard_map/ppermute | solution.py:425
  386.2 11.1 %collective-permute-start.17 = (bf16[2,2,80,768]{3,2,1,0:T(8,128)(2,1)S(1)}, bf16[2,2,80,768]{3,2,1,0:T(8,128)(2,1)S(1)}, u32[]{:S(2)}, u32[]{:S(2)}) collective-permute-start(bf16[2,2,80,768]{3,2,1,0:T(8,128)(2,1)S(1)} %fusion.6), channel_id=1, source_target_pairs={{0,4},{1,5},{2,6},{3,7},{4,0},{5,1},{6,2},{7,3},{8,12},{9,13},{10,... | collective-permute-start | bytes 1474568 | tf_op jit(solution)/shard_map/ppermute | solution.py:425
  386.8 11.6 %collective-permute-start.15 = (bf16[2,2,80,768]{3,2,0,1:T(8,128)(2,1)S(1)}, bf16[2,2,80,768]{3,2,0,1:T(8,128)(2,1)S(1)}, u32[]{:S(2)}, u32[]{:S(2)}) collective-permute-start(bf16[2,2,80,768]{3,2,0,1:T(8,128)(2,1)S(1)} %fusion.5), channel_id=1, source_target_pairs={{0,1},{1,0},{2,3},{3,2},{4,5},{5,4},{6,7},{7,6},{8,9},{9,8},{10,11... | collective-permute-start | bytes 1474568 | tf_op jit(solution)/shard_map/ppermute | solution.py:425
  397.5 8.6 %collective-permute-start.18 = (bf16[2,80,768]{2,1,0:T(8,128)(2,1)S(1)}, bf16[2,80,768]{2,1,0:T(8,128)(2,1)S(1)}, u32[]{:S(2)}, u32[]{:S(2)}) collective-permute-start(bf16[2,80,768]{2,1,0:T(8,128)(2,1)S(1)} %fusion.16), channel_id=1, source_target_pairs={{0,1},{1,0},{2,3},{3,2},{4,5},{5,4},{6,7},{7,6},{8,9},{9,8},{10,11... | collective-permute-start | bytes 737288 | tf_op jit(solution)/shard_map/ppermute | solution.py:425
  398.6 7.6 %collective-permute-start.16 = (bf16[2,80,768]{2,1,0:T(8,128)(2,1)S(1)}, bf16[2,80,768]{2,1,0:T(8,128)(2,1)S(1)}, u32[]{:S(2)}, u32[]{:S(2)}) collective-permute-start(bf16[2,80,768]{2,1,0:T(8,128)(2,1)S(1)} %fusion.15), channel_id=1, source_target_pairs={{0,4},{1,5},{2,6},{3,7},{4,0},{5,1},{6,2},{7,3},{8,12},{9,13},{10,... | collective-permute-start | bytes 737288 | tf_op jit(solution)/shard_map/ppermute | solution.py:425
  406.2 16.5 %collective-permute-start.19 = (bf16[80,768]{1,0:T(8,128)(2,1)S(1)}, bf16[80,768]{1,0:T(8,128)(2,1)S(1)}, u32[]{:S(2)}, u32[]{:S(2)}) collective-permute-start(bf16[80,768]{1,0:T(8,128)(2,1)S(1)} %fusion.21), channel_id=1, source_target_pairs={{0,8},{1,9},{2,10},{3,11},{4,12},{5,13},{6,14},{7,15},{8,0},{9,1},... | collective-permute-start | bytes 368648 | tf_op jit(solution)/shard_map/ppermute | solution.py:425
  409.4 13.3 %collective-permute-start.20 = (bf16[80,768]{1,0:T(8,128)(2,1)S(1)}, bf16[80,768]{1,0:T(8,128)(2,1)S(1)}, u32[]{:S(2)}, u32[]{:S(2)}) collective-permute-start(bf16[80,768]{1,0:T(8,128)(2,1)S(1)} %get-tuple-element.194), channel_id=1, source_target_pairs={{0,16},{1,17},{2,18},{3,19},{4,20},{5,21},{6,22},{7,23},{8,24},{9,... | collective-permute-start | bytes 368648 | tf_op jit(solution)/shard_map/ppermute | solution.py:425
  409.4 13.3 %collective-permute-start.21 = (bf16[80,768]{1,0:T(8,128)(2,1)S(1)}, bf16[80,768]{1,0:T(8,128)(2,1)S(1)}, u32[]{:S(2)}, u32[]{:S(2)}) collective-permute-start(bf16[80,768]{1,0:T(8,128)(2,1)S(1)} %get-tuple-element.195), channel_id=1, source_target_pairs={{0,24},{1,25},{2,26},{3,27},{4,28},{5,29},{6,30},{7,31},{8,16},{9,... | collective-permute-start | bytes 368648 | tf_op jit(solution)/shard_map/ppermute | solution.py:425
  (5 other events, 11.9 us)
Sparse Core Ops, SparseCore 0:
  11.6 98.0 all-gather.2
  303.3 117.7 reduce-scatter.1
